TPU v7x, 32 devices: a whole 2x2x4 slice. The times are simulated.
32 devices in a mesh: dp: 8 (over y, x, core), expert: 4 (over z).
Axes of the slice: x: 2, y: 2, z: 4, core: 2. Of those that a mesh axis runs over, the one named last changes fastest.
Arguments:
- tokens: bfloat16 [12288, 2048], P(('dp', 'expert')), may hold values from -6 to 6
- cotangent: bfloat16 [12288, 2048], P(('dp', 'expert')), may hold values from -6 to 6
- attention_gain: bfloat16 [2048], P(('dp', 'expert')), may hold values from 0.5 to 1.5
- query_weight: bfloat16 [2048, 2048], P(('dp', 'expert')), may hold values from -0.125 to 0.125
- key_weight: bfloat16 [2048, 2048], P(('dp', 'expert')), may hold values from -0.125 to 0.125
- value_weight: bfloat16 [2048, 2048], P(('dp', 'expert')), may hold values from -0.125 to 0.125
- out_weight: bfloat16 [2048, 2048], P(('dp', 'expert')), may hold values from -3 to 3
- query_norm: bfloat16 [2048], P(('dp', 'expert')), may hold values from 0.099609375 to 1.8984375
- key_norm: bfloat16 [2048], P(('dp', 'expert')), may hold values from 0.099609375 to 1.8984375
- mixture_gain: bfloat16 [2048], P(('dp', 'expert')), may hold values from 0.5 to 1.5
- router_weight: bfloat16 [2048, 16], P(('dp', 'expert')), may hold values from -0.25 to 0.25
- gate_weight: bfloat16 [16, 2048, 1024], P('expert', 'dp'), may hold values from -0.125 to 0.125
- up_weight: bfloat16 [16, 2048, 1024], P('expert', 'dp'), may hold values from -0.125 to 0.125
- down_weight: bfloat16 [16, 1024, 2048], P('expert', 'dp'), may hold values from -1.5 to 1.5
- segments: int32 [8, 1536], P('dp'), may hold values from 0 to 4, as said below
- positions: int32 [8, 1536], P('dp'), may hold values from 0 to 1151, as said below
- priority: int32 [8, 1536], P('dp'), may hold values from 0 to 1535, each once within a row
- routes: int32 [8, 1536, 8], P('dp'), may hold values from 0 to 15, all different within a row; in each aligned block of 384 rows (0 to 383, 384 to 767, ..., all dimensions but the last counted through in order) at most 288 rows name the same one
Outputs:
- output: bfloat16 [12288, 2048], P(('dp', 'expert'))
- input_grad: float32 [12288, 2048], P(('dp', 'expert'))
- grad_attention_gain: float32 [2048], P(('dp', 'expert'))
- grad_query_weight: float32 [2048, 2048], P(('dp', 'expert'))
- grad_key_weight: float32 [2048, 2048], P(('dp', 'expert'))
- grad_value_weight: float32 [2048, 2048], P(('dp', 'expert'))
- grad_out_weight: float32 [2048, 2048], P(('dp', 'expert'))
- grad_query_norm: float32 [2048], P(('dp', 'expert'))
- grad_key_norm: float32 [2048], P(('dp', 'expert'))
- grad_mixture_gain: float32 [2048], P(('dp', 'expert'))
- grad_router_weight: float32 [2048, 16], P(('dp', 'expert'))
- grad_gate_weight: float32 [16, 2048, 1024], P('expert', 'dp')
- grad_up_weight: float32 [16, 2048, 1024], P('expert', 'dp')
- grad_down_weight: float32 [16, 1024, 2048], P('expert', 'dp')
Inputs may be any that keep to these rules, and one draw needn't show every extreme that they name: In each group the 1536 rows form blocks of 128 rows, each block of one segment; segment 0 (the prompt) has 1024 rows and each of the segments 1 to 4 has 128 rows. The prompt's rows hold positions 0 to 1023, each once and rising along the rows; the rows of each continuation hold 1024 to 1151, rising. `priority`: each group's row lists the group's 1536 tokens, each once. `routes`: each token names 8 different experts; among the rows of one device (aligned blocks of 384 rows) no expert is named more than 288 times, and in some such block one expert exactly 288 times.
All inputs are finite; a program needn't handle non-finite values.
Results may differ from a plain program's by a relative error of at most 0.022.
Values may be sent and summed in bfloat16 or wider, within the bound.
A program may use at most 384 MiB of HBM per device.

v0:
```python
import math

import jax
import jax.numpy as jnp
from jax import lax
from jax.sharding import PartitionSpec as P

HEADS = 16
HEAD_DIM = 128
TOPK = 8
EXPERTS = 16
GTOK = 1536
CAP = 768


EPS = 1e-05


def norm_apply(values, gain_vec):
    inverse = lax.rsqrt(jnp.mean(values * values, axis=-1, keepdims=True) + EPS)
    unit_rows = values * inverse
    return (unit_rows * gain_vec, unit_rows, inverse)


def norm_back(grad_rows, unit_rows, inverse, gain_vec):
    grad_unit = grad_rows * gain_vec
    grad_gain = jnp.sum(grad_rows * unit_rows, axis=0)
    inner_mean = jnp.mean(grad_unit * unit_rows, axis=-1, keepdims=True)
    return (inverse * (grad_unit - unit_rows * inner_mean), grad_gain)


def rope_tables(places):
    frequency = 10000.0 ** (-jnp.arange(0, HEAD_DIM // 2, dtype=jnp.float32) * 2.0 / HEAD_DIM)
    angles = places.astype(jnp.float32)[:, None] * frequency[None, :]
    return (jnp.cos(angles)[:, None, :], jnp.sin(angles)[:, None, :])


def rotate(values, cosine_table, sine_table):
    half_dim = values.shape[-1] // 2
    first_half = values[..., :half_dim]
    second_half = values[..., half_dim:]
    return jnp.concatenate(
        [
            first_half * cosine_table - second_half * sine_table,
            second_half * cosine_table + first_half * sine_table,
        ],
        axis=-1,
    )


def rotate_back(grads, cosine_table, sine_table):
    half_dim = grads.shape[-1] // 2
    first_half = grads[..., :half_dim]
    second_half = grads[..., half_dim:]
    return jnp.concatenate(
        [
            first_half * cosine_table + second_half * sine_table,
            second_half * cosine_table - first_half * sine_table,
        ],
        axis=-1,
    )


def visible(query_segs, query_places, key_segs, key_places):
    shared = (key_segs[None, :] == 0) | (key_segs[None, :] == query_segs[:, None])
    return shared & (key_places[None, :] <= query_places[:, None])


def cross_rows(left, right):
    return lax.dot_general(
        left, right, (((0,), (0,)), ((), ())), preferred_element_type=jnp.float32
    )


def by_transpose(left, right):
    return lax.dot_general(
        left, right, (((1,), (1,)), ((), ())), preferred_element_type=jnp.float32
    )


def slot_tables(group_routes, group_order, tok_dev):
    expert_ids = jnp.arange(EXPERTS, dtype=jnp.int32)
    route_hits = jnp.sum(
        (group_routes[:, :, None] == expert_ids[None, None, :]).astype(jnp.int32), axis=1
    )
    ranked = route_hits[group_order]
    before = jnp.cumsum(ranked, axis=0) - ranked
    inverse = jnp.zeros((GTOK,), jnp.int32).at[group_order].set(jnp.arange(GTOK, dtype=jnp.int32))
    global_slot = before[inverse]
    device_hits = route_hits.reshape(GTOK // tok_dev, tok_dev, EXPERTS)
    local_rank = (jnp.cumsum(device_hits, axis=1) - device_hits).reshape(GTOK, EXPERTS)
    return (route_hits, global_slot, local_rank)


def receive_table(
    route_hits, global_slot, local_rank, first_expert, experts_here, peer_count, tok_dev, most_rows
):
    mine_hits = lax.dynamic_slice_in_dim(route_hits, first_expert, experts_here, axis=1)
    mine_slot = lax.dynamic_slice_in_dim(global_slot, first_expert, experts_here, axis=1)
    mine_rank = lax.dynamic_slice_in_dim(local_rank, first_expert, experts_here, axis=1)
    source = jnp.arange(GTOK, dtype=jnp.int32) // tok_dev
    column = source[:, None] * most_rows + mine_rank
    stride = peer_count * most_rows
    valid_mask = (mine_hits > 0) & (mine_slot < CAP)
    slot_place = jnp.where(
        valid_mask,
        jnp.arange(experts_here, dtype=jnp.int32)[None, :] * stride + column,
        experts_here * stride,
    )
    slot_table = jnp.full((experts_here * stride + 1,), CAP, jnp.int32)
    slot_table = slot_table.at[slot_place.reshape(-1)].set(mine_slot.reshape(-1))
    return slot_table[: experts_here * stride].reshape(experts_here, stride)


def to_experts(rows, target, most_rows):
    model_width = rows.shape[-1]
    buffer = jnp.zeros((EXPERTS * most_rows + 1, model_width), jnp.bfloat16)
    buffer = buffer.at[target.reshape(-1)].set(rows.reshape(-1, model_width))
    sending = buffer[: EXPERTS * most_rows].reshape(EXPERTS, most_rows, model_width)
    return lax.all_to_all(sending, "expert", split_axis=0, concat_axis=1, tiled=True)


def from_experts(rows):
    return lax.all_to_all(rows, "expert", split_axis=1, concat_axis=0, tiled=True)


def compact(arrived, slot_table):

    def compact_one_expert(rows, places):
        return jnp.zeros((CAP + 1, rows.shape[-1]), rows.dtype).at[places].set(rows)[:CAP]

    return jax.vmap(compact_one_expert)(arrived, slot_table)


def spread(slot_rows, slot_table):

    def spread_one_expert(rows, places):
        return jnp.take(rows, places, axis=0, mode="fill", fill_value=0)

    return jax.vmap(spread_one_expert)(slot_rows, slot_table)


def fetch_expert(shards):
    return (
        lax.all_gather(shards[0], "dp", axis=0, tiled=True),
        lax.all_gather(shards[1], "dp", axis=0, tiled=True),
        lax.all_gather(shards[2], "dp", axis=0, tiled=True),
    )


def weights_for(shards):
    return fetch_expert(shards)


def body(
    tokens,
    cotangent,
    attention_gain,
    query_weight,
    key_weight,
    value_weight,
    out_weight,
    query_norm,
    key_norm,
    mixture_gain,
    router_weight,
    gate_weight,
    up_weight,
    down_weight,
    segments,
    positions,
    priority,
    routes,
):
    tok_dev = tokens.shape[0]
    model_width = tokens.shape[1]
    experts_here = gate_weight.shape[0]
    peer_count = lax.axis_size("expert")
    most_rows = (3 * tok_dev * TOPK + 2 * EXPERTS - 1) // (2 * EXPERTS)
    position = lax.axis_index("expert")
    first_row = position * tok_dev
    first_expert = position * experts_here
    score_scale = HEAD_DIM ** (-0.5)
    key_block = math.gcd(GTOK, 512)
    block_count = GTOK // key_block
    gathered = (
        lax.all_gather(attention_gain, ("dp", "expert"), axis=0, tiled=True),
        lax.all_gather(query_weight, ("dp", "expert"), axis=0, tiled=True),
        lax.all_gather(key_weight, ("dp", "expert"), axis=0, tiled=True),
        lax.all_gather(value_weight, ("dp", "expert"), axis=0, tiled=True),
        lax.all_gather(out_weight, ("dp", "expert"), axis=0, tiled=True),
        lax.all_gather(query_norm, ("dp", "expert"), axis=0, tiled=True),
        lax.all_gather(key_norm, ("dp", "expert"), axis=0, tiled=True),
        lax.all_gather(mixture_gain, ("dp", "expert"), axis=0, tiled=True),
        lax.all_gather(router_weight, ("dp", "expert"), axis=0, tiled=True),
    )
    attend_gain = gathered[0].astype(jnp.float32)
    query_full, key_full, value_full, out_full = (
        gathered[1],
        gathered[2],
        gathered[3],
        gathered[4],
    )
    query_gain = gathered[5].astype(jnp.float32)
    key_gain = gathered[6].astype(jnp.float32)
    mix_gain = gathered[7].astype(jnp.float32)
    router_full = gathered[8]
    expert_source = (gate_weight, up_weight, down_weight)
    group_segs = segments[0]
    group_places = positions[0]
    seg_rows = lax.dynamic_slice_in_dim(group_segs, first_row, tok_dev)
    place_rows = lax.dynamic_slice_in_dim(group_places, first_row, tok_dev)
    cosine_table, sine_table = rope_tables(place_rows)
    token_f = tokens.astype(jnp.float32)
    normed_in, unit_in, inverse_in = norm_apply(token_f, attend_gain)
    normed_b = normed_in.astype(jnp.bfloat16)
    query_pre = jnp.dot(normed_b, query_full, preferred_element_type=jnp.float32)
    key_pre = jnp.dot(normed_b, key_full, preferred_element_type=jnp.float32)
    value_pre = jnp.dot(normed_b, value_full, preferred_element_type=jnp.float32)
    query_n, query_unit, query_inverse = norm_apply(query_pre, query_gain)
    key_n, key_unit, key_inverse = norm_apply(key_pre, key_gain)
    query_b = rotate(query_n.reshape(tok_dev, HEADS, HEAD_DIM), cosine_table, sine_table).astype(
        jnp.bfloat16
    )
    key_b = (
        rotate(key_n.reshape(tok_dev, HEADS, HEAD_DIM), cosine_table, sine_table)
        .reshape(tok_dev, model_width)
        .astype(jnp.bfloat16)
    )
    value_b = value_pre.astype(jnp.bfloat16)
    key_all, value_all = (
        lax.all_gather(key_b, "expert", axis=0, tiled=True),
        lax.all_gather(value_b, "expert", axis=0, tiled=True),
    )
    key_blocks = key_all.reshape(block_count, key_block, HEADS, HEAD_DIM)
    value_blocks = value_all.reshape(block_count, key_block, HEADS, HEAD_DIM)
    seg_blocks = group_segs.reshape(block_count, key_block)
    place_blocks = group_places.reshape(block_count, key_block)
    block_items = (key_blocks, value_blocks, seg_blocks, place_blocks)

    def block_scores(key_blk, seg_blk, place_blk):
        raw = jnp.einsum("qhd,khd->hqk", query_b, key_blk, preferred_element_type=jnp.float32)
        mask_blk = visible(seg_rows, place_rows, seg_blk, place_blk)
        return jnp.where(mask_blk[None], raw * score_scale, -1e30)

    def lse_step(running, scan_items):
        run_max, run_total = running
        key_blk, value_blk, seg_blk, place_blk = scan_items
        scores = block_scores(key_blk, seg_blk, place_blk)
        new_max = jnp.maximum(run_max, jnp.max(scores, axis=-1))
        run_total = run_total * jnp.exp(run_max - new_max) + jnp.sum(
            jnp.exp(scores - new_max[..., None]), axis=-1
        )
        return ((new_max, run_total), None)

    start_max = jnp.full((HEADS, tok_dev), -1e30, jnp.float32)
    start_total = jnp.zeros((HEADS, tok_dev), jnp.float32)
    (final_max, final_total), unused = lax.scan(lse_step, (start_max, start_total), block_items)
    log_total = final_max + jnp.log(final_total)

    def out_step(running, scan_items):
        key_blk, value_blk, seg_blk, place_blk = scan_items
        scores = block_scores(key_blk, seg_blk, place_blk)
        probs_b = jnp.exp(scores - log_total[..., None]).astype(jnp.bfloat16)
        return (
            running
            + jnp.einsum("hqk,khd->qhd", probs_b, value_blk, preferred_element_type=jnp.float32),
            None,
        )

    mixed_f, unused = lax.scan(
        out_step, jnp.zeros((tok_dev, HEADS, HEAD_DIM), jnp.float32), block_items
    )
    mixed_b = mixed_f.reshape(tok_dev, model_width).astype(jnp.bfloat16)
    resid = token_f + jnp.dot(mixed_b, out_full, preferred_element_type=jnp.float32)
    mix_n, mix_unit, mix_inverse = norm_apply(resid, mix_gain)
    mix_b = mix_n.astype(jnp.bfloat16)
    logits = jnp.dot(mix_b, router_full, preferred_element_type=jnp.float32)
    router = jax.nn.softmax(logits, axis=-1)
    route_hits, global_slot, local_rank = slot_tables(routes[0], priority[0], tok_dev)
    my_routes = lax.dynamic_slice_in_dim(routes[0], first_row, tok_dev)
    my_slot = jnp.take_along_axis(
        lax.dynamic_slice_in_dim(global_slot, first_row, tok_dev), my_routes, axis=1
    )
    my_rank = jnp.take_along_axis(
        lax.dynamic_slice_in_dim(local_rank, first_row, tok_dev), my_routes, axis=1
    )
    kept_mask = my_slot < CAP
    kept_f = kept_mask.astype(jnp.float32)
    target = jnp.where(kept_mask, my_routes * most_rows + my_rank, EXPERTS * most_rows)
    route_weight = jnp.take_along_axis(router, my_routes, axis=1) * kept_f
    slot_table = receive_table(
        route_hits,
        global_slot,
        local_rank,
        first_expert,
        experts_here,
        peer_count,
        tok_dev,
        most_rows,
    )
    sent_rows = jnp.broadcast_to(mix_b[:, None, :], (tok_dev, TOPK, model_width))
    inputs_b = compact(to_experts(sent_rows, target, most_rows), slot_table)

    def expert_step(running, scan_items):
        shards, rows = scan_items
        full_weights = weights_for(shards)
        gate_pre = jnp.dot(rows, full_weights[0], preferred_element_type=jnp.float32)
        up_pre = jnp.dot(rows, full_weights[1], preferred_element_type=jnp.float32)
        hidden = (jax.nn.silu(gate_pre) * up_pre).astype(jnp.bfloat16)
        result = jnp.dot(hidden, full_weights[2], preferred_element_type=jnp.float32).astype(
            jnp.bfloat16
        )
        return (running, (result, gate_pre, up_pre))

    unused, (expert_out, gate_keep, up_keep) = lax.scan(expert_step, 0, (expert_source, inputs_b))
    returned = from_experts(spread(expert_out, slot_table)).reshape(
        EXPERTS * most_rows, model_width
    )
    picked = jnp.take(returned, target, axis=0, mode="fill", fill_value=0)
    moe_out = jnp.sum(route_weight[:, :, None] * picked, axis=1)
    output = (resid + moe_out).astype(jnp.bfloat16)
    grad_f = cotangent.astype(jnp.float32)
    route_grad = jnp.sum(grad_f[:, None, :] * picked, axis=-1) * kept_f
    grad_rows = (route_weight[:, :, None] * grad_f[:, None, :]).astype(jnp.bfloat16)
    grad_in_b = compact(to_experts(grad_rows, target, most_rows), slot_table)

    def expert_back(running, scan_items):
        shards, rows, grad_out_rows, gate_pre, up_pre = scan_items
        full_weights = weights_for(shards)
        silu_gate = jax.nn.silu(gate_pre)
        hidden = (silu_gate * up_pre).astype(jnp.bfloat16)
        grad_hidden = by_transpose(grad_out_rows, full_weights[2])
        grad_down = cross_rows(hidden, grad_out_rows)
        sigmoid_gate = jax.nn.sigmoid(gate_pre)
        grad_gate = (
            grad_hidden * up_pre * (sigmoid_gate * (1.0 + gate_pre * (1.0 - sigmoid_gate)))
        ).astype(jnp.bfloat16)
        grad_up = (grad_hidden * silu_gate).astype(jnp.bfloat16)
        grad_gate_w = cross_rows(rows, grad_gate)
        grad_up_w = cross_rows(rows, grad_up)
        grad_rows_in = (
            by_transpose(grad_gate, full_weights[0]) + by_transpose(grad_up, full_weights[1])
        ).astype(jnp.bfloat16)
        grad_set = (
            lax.psum_scatter(
                grad_gate_w.astype(jnp.bfloat16), "dp", scatter_dimension=0, tiled=True
            ).astype(jnp.float32),
            lax.psum_scatter(
                grad_up_w.astype(jnp.bfloat16), "dp", scatter_dimension=0, tiled=True
            ).astype(jnp.float32),
            lax.psum_scatter(
                grad_down.astype(jnp.bfloat16), "dp", scatter_dimension=0, tiled=True
            ).astype(jnp.float32),
        )
        return (running, (grad_rows_in, grad_set))

    unused, (grad_inputs, expert_grads) = lax.scan(
        expert_back, 0, (expert_source, inputs_b, grad_in_b, gate_keep, up_keep)
    )
    grad_back = from_experts(spread(grad_inputs, slot_table)).reshape(
        EXPERTS * most_rows, model_width
    )
    grad_routed = jnp.sum(
        jnp.take(grad_back, target, axis=0, mode="fill", fill_value=0), axis=1, dtype=jnp.float32
    )
    expert_ids = jnp.arange(EXPERTS, dtype=jnp.int32)
    grad_router_in = jnp.sum(
        (my_routes[:, :, None] == expert_ids[None, None, :]).astype(jnp.float32)
        * route_grad[:, :, None],
        axis=1,
    )
    grad_logits = (
        router * (grad_router_in - jnp.sum(router * grad_router_in, axis=-1, keepdims=True))
    ).astype(jnp.bfloat16)
    grad_router = cross_rows(mix_b, grad_logits)
    grad_mix = grad_routed + by_transpose(grad_logits, router_full)
    grad_resid_part, grad_mix_gain = norm_back(grad_mix, mix_unit, mix_inverse, mix_gain)
    grad_resid = grad_f + grad_resid_part
    grad_branch = grad_resid.astype(jnp.bfloat16)
    grad_out_w = cross_rows(mixed_b, grad_branch)
    grad_heads = (
        by_transpose(grad_branch, out_full).astype(jnp.bfloat16).reshape(tok_dev, HEADS, HEAD_DIM)
    )

    def delta_step(running, scan_items):
        key_blk, value_blk, seg_blk, place_blk = scan_items
        probs = jnp.exp(block_scores(key_blk, seg_blk, place_blk) - log_total[..., None])
        grad_probs = jnp.einsum(
            "qhd,khd->hqk", grad_heads, value_blk, preferred_element_type=jnp.float32
        )
        return (running + jnp.sum(probs * grad_probs, axis=-1), None)

    delta, unused = lax.scan(delta_step, jnp.zeros((HEADS, tok_dev), jnp.float32), block_items)

    def grad_step(running, scan_items):
        key_blk, value_blk, seg_blk, place_blk = scan_items
        probs = jnp.exp(block_scores(key_blk, seg_blk, place_blk) - log_total[..., None])
        grad_probs = jnp.einsum(
            "qhd,khd->hqk", grad_heads, value_blk, preferred_element_type=jnp.float32
        )
        grad_raw = (probs * (grad_probs - delta[..., None]) * score_scale).astype(jnp.bfloat16)
        running = running + jnp.einsum(
            "hqk,khd->qhd", grad_raw, key_blk, preferred_element_type=jnp.float32
        )
        grad_key_blk = jnp.einsum(
            "hqk,qhd->khd", grad_raw, query_b, preferred_element_type=jnp.float32
        )
        grad_value_blk = jnp.einsum(
            "hqk,qhd->khd",
            probs.astype(jnp.bfloat16),
            grad_heads,
            preferred_element_type=jnp.float32,
        )
        return (running, (grad_key_blk, grad_value_blk))

    grad_query_rot, (grad_key_blocks, grad_value_blocks) = lax.scan(
        grad_step, jnp.zeros((tok_dev, HEADS, HEAD_DIM), jnp.float32), block_items
    )
    grad_key_rows, grad_value_rows = (
        lax.psum_scatter(
            grad_key_blocks.reshape(GTOK, model_width).astype(jnp.bfloat16),
            "expert",
            scatter_dimension=0,
            tiled=True,
        ).astype(jnp.float32),
        lax.psum_scatter(
            grad_value_blocks.reshape(GTOK, model_width).astype(jnp.bfloat16),
            "expert",
            scatter_dimension=0,
            tiled=True,
        ).astype(jnp.float32),
    )
    grad_value_b = grad_value_rows.astype(jnp.bfloat16)
    grad_key_n = rotate_back(
        grad_key_rows.reshape(tok_dev, HEADS, HEAD_DIM), cosine_table, sine_table
    ).reshape(tok_dev, model_width)
    grad_key_pre, grad_key_gain = norm_back(grad_key_n, key_unit, key_inverse, key_gain)
    grad_key_b = grad_key_pre.astype(jnp.bfloat16)
    grad_query_n = rotate_back(grad_query_rot, cosine_table, sine_table).reshape(
        tok_dev, model_width
    )
    grad_query_pre, grad_query_gain = norm_back(grad_query_n, query_unit, query_inverse, query_gain)
    grad_query_b = grad_query_pre.astype(jnp.bfloat16)
    grad_query_w = cross_rows(normed_b, grad_query_b)
    grad_key_w = cross_rows(normed_b, grad_key_b)
    grad_value_w = cross_rows(normed_b, grad_value_b)
    grad_normed = (
        by_transpose(grad_query_b, query_full)
        + by_transpose(grad_key_b, key_full)
        + by_transpose(grad_value_b, value_full)
    )
    grad_in_part, grad_attend_gain = norm_back(grad_normed, unit_in, inverse_in, attend_gain)
    input_grad = grad_resid + grad_in_part
    dense_out = (
        lax.psum_scatter(grad_attend_gain, ("dp", "expert"), scatter_dimension=0, tiled=True),
        lax.psum_scatter(grad_query_w, ("dp", "expert"), scatter_dimension=0, tiled=True),
        lax.psum_scatter(grad_key_w, ("dp", "expert"), scatter_dimension=0, tiled=True),
        lax.psum_scatter(grad_value_w, ("dp", "expert"), scatter_dimension=0, tiled=True),
        lax.psum_scatter(grad_out_w, ("dp", "expert"), scatter_dimension=0, tiled=True),
        lax.psum_scatter(grad_query_gain, ("dp", "expert"), scatter_dimension=0, tiled=True),
        lax.psum_scatter(grad_key_gain, ("dp", "expert"), scatter_dimension=0, tiled=True),
        lax.psum_scatter(grad_mix_gain, ("dp", "expert"), scatter_dimension=0, tiled=True),
        lax.psum_scatter(grad_router, ("dp", "expert"), scatter_dimension=0, tiled=True),
    )
    return (
        output,
        input_grad,
        dense_out[0],
        dense_out[1],
        dense_out[2],
        dense_out[3],
        dense_out[4],
        dense_out[5],
        dense_out[6],
        dense_out[7],
        dense_out[8],
        expert_grads[0],
        expert_grads[1],
        expert_grads[2],
    )


def solution(mesh):
    placed = (
        P(("dp", "expert"), None),
        P(("dp", "expert"), None),
        P(("dp", "expert")),
        P(("dp", "expert"), None),
        P(("dp", "expert"), None),
        P(("dp", "expert"), None),
        P(("dp", "expert"), None),
        P(("dp", "expert")),
        P(("dp", "expert")),
        P(("dp", "expert")),
        P(("dp", "expert"), None),
        P("expert", "dp", None),
        P("expert", "dp", None),
        P("expert", "dp", None),
        P("dp", None),
        P("dp", None),
        P("dp", None),
        P("dp", None, None),
    )
    return jax.shard_map(
        body,
        mesh=mesh,
        in_specs=placed,
        out_specs=(
            P(("dp", "expert"), None),
            P(("dp", "expert"), None),
            P(("dp", "expert")),
            P(("dp", "expert"), None),
            P(("dp", "expert"), None),
            P(("dp", "expert"), None),
            P(("dp", "expert"), None),
            P(("dp", "expert")),
            P(("dp", "expert")),
            P(("dp", "expert")),
            P(("dp", "expert"), None),
            P("expert", "dp", None),
            P("expert", "dp", None),
            P("expert", "dp", None),
        ),
        check_vma=False,
    )
```

profile of v0, /device:TPU:10, one launch (start us, length us, event | category | flops | bytes accessed | tf_op | source)
XLA Modules:
  0.0 6604.5 jit_solution(7764193840472414413)
XLA Ops:
  12.9 42.0 all-reduce.9
  59.2 30.6 all-gather.36.cloned.1.call-done
  103.7 65.0 all-gather.40.cloned.1.call-done
  188.8 58.8 all-gather.32.cloned.1.call-done
  257.0 71.2 %all-gather.6 = bf16[32,64,16]{1,2,0:T(8,128)(2,1)S(1)} all-gather(bf16[1,64,16]{1,2,0:T(8,128)(2,1)S(1)} %bitcast.545), channel_id=1, replica_groups=mesh['dp'=8,'expert'=4] {'dp','expert'}, dimensions={0}, use_global_device_ids=true | all-gather | bytes 67584 | tf_op jit(solution)/shard_map/all_gather | solution.py:195
  407.1 71.9 %all-gather.34.cloned.1.call-done = bf16[1536,2048]{1,0:T(8,128)(2,1)} async-done(((bf16[384,2048]{1,0:T(8,128)(2,1)}), bf16[1536,2048]{1,0:T(8,128)(2,1)}) %all-gather.34.cloned.1.call-update) | async-done | bytes 6291472 | tf_op jit(solution)/shard_map/all_gather | solution.py:233
  486.8 50.8 while.82
  538.3 52.8 while.83
  630.8 28.2 scatter_custom_fusion.2
  705.2 33.3 scatter_custom_fusion.3
  755.4 335.7 %all-to-all-done = bf16[16,288,2048]{2,1,0:T(8,128)(2,1)} async-done(((bf16[16,288,2048]{2,1,0:T(8,128)(2,1)}), bf16[16,288,2048]{2,1,0:T(8,128)(2,1)}, u32[]{:S(2)}, u32[]{:S(2)}) %all-to-all-start) | async-done | bytes 18874400 | tf_op jit(solution)/shard_map/all_to_all | solution.py:120
  1147.9 34.4 scatter_custom_fusion.4
  1229.8 276.2 %all-to-all-done.2 = bf16[16,288,2048]{2,1,0:T(8,128)(2,1)} async-done(((bf16[16,288,2048]{2,1,0:T(8,128)(2,1)}), bf16[16,288,2048]{2,1,0:T(8,128)(2,1)}, u32[]{:S(2)}, u32[]{:S(2)}) %all-to-all-start.2) | async-done | bytes 18874400 | tf_op jit(solution)/shard_map/all_to_all | solution.py:120
  1523.0 34.3 scatter_custom_fusion.5
  1610.9 513.2 %while.80 = (s32[]{:T(128)}, bf16[4,768,2048]{2,1,0:T(8,128)(2,1)}, f32[4,768,1024]{2,1,0:T(8,128)}, f32[4,768,1024]{2,1,0:T(8,128)}, bf16[4,768,2048]{2,1,0:T(8...) while((s32[]{:T(128)}, bf16[4,768,2048]{2,1,0:T(8,128)(2,1)}, ...), condition=%wide.region_22.24_spmd, body=%wide.region_21.23_spmd.sunk | while | flops 9669967872 | bytes 86509808 | solution.py:316
  1615.6 37.5 all-gather.46.cloned.1.call-done
  1662.4 30.2 all-gather.48.cloned.1.call-done
  1701.7 30.2 all-gather.44.cloned.1.call-done
  1745.8 35.1 all-gather.46.cloned.1.call-done
  1790.3 30.1 all-gather.48.cloned.1.call-done
  1829.6 29.9 all-gather.44.cloned.1.call-done
  1873.5 35.4 all-gather.46.cloned.1.call-done
  1918.4 29.8 all-gather.48.cloned.1.call-done
  1957.6 29.8 all-gather.44.cloned.1.call-done
  2001.3 35.1 all-gather.46.cloned.1.call-done
  2045.7 30.0 all-gather.48.cloned.1.call-done
  2084.9 30.0 all-gather.44.cloned.1.call-done
  2130.3 1141.6 %while.81 = (s32[]{:T(128)}, bf16[4,768,2048]{2,1,0:T(8,128)(2,1)}, f32[4,256,1024]{2,1,0:T(8,128)}, f32[4,256,1024]{2,1,0:T(8,128)}, f32[4,128,2048]{2,1,0:T(8,...) while((s32[]{:T(128)}, bf16[4,768,2048]{2,1,0:T(8,128)(2,1)}, ...), condition=%wide.region_30.34_spmd, body=%wide.region_26.33_spmd.sunk | while | flops 19352518656 | bytes 174590384 | solution.py:358
  2227.9 37.1 all-gather.52.cloned.1.call-done
  2273.8 30.5 all-gather.54.cloned.1.call-done
  2314.0 45.0 reduce-scatter.27.cloned.1.call-done
  2361.1 52.8 reduce-scatter.29.cloned.1.call-done
  2513.3 37.0 all-gather.52.cloned.1.call-done
  2559.0 30.5 all-gather.54.cloned.1.call-done
  2599.1 45.1 reduce-scatter.27.cloned.1.call-done
  2646.3 52.8 reduce-scatter.29.cloned.1.call-done
  2768.5 28.0 reduce-scatter.31.cloned.1.call-done
  2798.6 37.0 all-gather.52.cloned.1.call-done
  2844.3 30.5 all-gather.54.cloned.1.call-done
  2884.4 45.1 reduce-scatter.27.cloned.1.call-done
  2931.6 52.8 reduce-scatter.29.cloned.1.call-done
  3053.4 28.1 reduce-scatter.31.cloned.1.call-done
  3083.6 37.0 all-gather.52.cloned.1.call-done
  3129.4 30.5 all-gather.54.cloned.1.call-done
  3169.6 45.0 reduce-scatter.27.cloned.1.call-done
  3216.7 53.0 reduce-scatter.29.cloned.1.call-done
  3271.9 150.6 %gather_fusion.7 = bf16[4608,2048]{1,0:T(8,128)(2,1)} fusion(bf16[4,768,2048]{2,1,0:T(8,128)(2,1)} %get-tuple-element.363, s32[4608]{0:T(1024)S(1)} %copy-done), kind=kCustom, calls=%fused_computation.4.clone | custom fusion | bytes 37785600 | tf_op jit(solution)/shard_map/vmap(jit(_take))/gather | solution.py:138
  3422.5 151.4 %gather_fusion.5 = bf16[4608,2048]{1,0:T(8,128)(2,1)} fusion(bf16[4,768,2048]{2,1,0:T(8,128)(2,1)} %get-tuple-element.360, s32[4608]{0:T(1024)S(1)} %copy-done), kind=kCustom, calls=%fused_computation.1.clone | custom fusion | bytes 37785600 | tf_op jit(solution)/shard_map/vmap(jit(_take))/gather | solution.py:138
  3573.9 48.5 copy_select_fusion
  3622.4 473.2 %all_to_all.66 = bf16[4,1152,2048]{2,0,1:T(4,128)(2,1)} all-to-all(bf16[4,1152,2048]{2,0,1:T(4,128)(2,1)} %get-tuple-element.1062), channel_id=1, replica_groups=mesh['dp'=8,'expert'=4] {'expert'}, dimensions={1} | all-to-all | bytes 37748736 | tf_op jit(solution)/shard_map/all_to_all | solution.py:124
  4135.8 375.1 %all-to-all-done.1 = bf16[4,1152,2048]{2,0,1:T(4,128)(2,1)} async-done(((bf16[4,1152,2048]{2,0,1:T(4,128)(2,1)}), bf16[4,1152,2048]{2,0,1:T(4,128)(2,1)}, u32[]{:S(2)}, u32[]{:S(2)}) %all-to-all-start.1) | async-done | bytes 18874400 | tf_op jit(solution)/shard_map/all_to_all | solution.py:124
  4531.6 32.6 gather_fusion.8
  4564.2 32.6 gather_fusion.6
  4597.0 30.4 fusion.123
  4638.7 29.4 while.84
  4668.1 96.6 %while.85 = (s32[]{:T(128)}, f32[384,16,128]{0,2,1:T(8,128)}, bf16[3,512,16,128]{3,1,2,0:T(8,128)(2,1)}, bf16[3,512,16,128]{3,1,2,0:T(8,128)(2,1)}, bf16[3,512,1...) while((s32[]{:T(128)}, f32[384,16,128]{0,2,1:T(8,128)}, ...), condition=%wide.region_40.44_spmd.clone, body=%wide.region_39.43_spmd.clone.sunk | while | flops 4063494656 | bytes 210397968 | solution.py:417
  4804.6 86.3 %reduce-scatter.13.cloned.1.call-done = bf16[384,2048]{1,0:T(8,128)(2,1)} async-done(((bf16[1536,2048]{1,0:T(8,128)(2,1)}), bf16[384,2048]{1,0:T(8,128)(2,1)}) %reduce-scatter.13.cloned.1.call-update) | async-done | bytes 1572880 | tf_op jit(solution)/shard_map/reduce_scatter | solution.py:421
  4940.4 64.0 reduce-scatter.15.cloned.1.call-done
  5014.1 116.1 %reduce-scatter.25.cloned.1.call-done = f32[64,16]{1,0:T(8,128)} async-done(((f32[2048,16]{1,0:T(8,128)}), f32[64,16]{1,0:T(8,128)}) %reduce-scatter.25.cloned.1.call-update) | async-done | bytes 4112
  5153.4 54.5 all-reduce.8
  5215.6 287.1 %reduce-scatter.23.cloned.1.call-done = f32[64,2048]{1,0:T(8,128)} async-done(((f32[2048,2048]{1,0:T(8,128)}), f32[64,2048]{1,0:T(8,128)}) %reduce-scatter.23.cloned.1.call-update) | async-done | bytes 524304 | tf_op jit(solution)/shard_map/reduce_scatter | solution.py:460
  5502.7 364.7 %reduce-scatter.19.cloned.1.call-done = f32[64,2048]{1,0:T(8,128)} async-done(((f32[2048,2048]{1,0:T(8,128)}), f32[64,2048]{1,0:T(8,128)}) %reduce-scatter.19.cloned.1.call-update) | async-done | bytes 524304 | tf_op jit(solution)/shard_map/reduce_scatter | solution.py:458
  5867.4 365.0 %reduce-scatter.17.cloned.1.call-done = f32[64,2048]{1,0:T(8,128)} async-done(((f32[2048,2048]{1,0:T(8,128)}), f32[64,2048]{1,0:T(8,128)}) %reduce-scatter.17.cloned.1.call-update) | async-done | bytes 524304 | tf_op jit(solution)/shard_map/reduce_scatter | solution.py:457
  6232.4 365.0 %reduce-scatter.21.cloned.1.call-done = f32[64,2048]{1,0:T(8,128)} async-done(((f32[2048,2048]{1,0:T(8,128)}), f32[64,2048]{1,0:T(8,128)}) %reduce-scatter.21.cloned.1.call-update) | async-done | bytes 524304 | tf_op jit(solution)/shard_map/reduce_scatter | solution.py:459
  (670 shorter events, 1406.8 us)
Async XLA Ops:
  7.2 82.6 %all-gather.36.cloned.1.call-start = ((), (), s32[]{:S(2)}) async-start(), calls=%async_computation.16 | async-start | bytes 8650752 | tf_op jit(solution)/shard_map/all_gather | solution.py:189
  7.9 160.8 %all-gather.40.cloned.1.call-start = ((), (), s32[]{:S(2)}) async-start(), calls=%async_computation.18 | async-start | bytes 8650752 | tf_op jit(solution)/shard_map/all_gather | solution.py:188
  8.7 239.0 %all-gather.32.cloned.1.call-start = ((), (), s32[]{:S(2)}) async-start(), calls=%async_computation.14 | async-start | bytes 8650752 | tf_op jit(solution)/shard_map/all_gather | solution.py:190
  9.4 388.4 %all-gather.38.cloned.1.call-start = ((), (), s32[]{:S(2)}) async-start(), calls=%async_computation.17 | async-start | bytes 7864320 | tf_op jit(solution)/shard_map/all_gather | solution.py:232
  54.9 192.8 %copy-start.44 = (f32[2048]{0:T(1024)}, f32[2048]{0:T(1024)S(1)}, u32[]{:S(2)}) copy-start(f32[2048]{0:T(1024)S(1)} %convert_element_type.137) | copy-start | bytes 24580
  54.9 119.9 %copy-start.68 = (f32[2048]{0:T(1024)}, f32[2048]{0:T(1024)S(1)}, u32[]{:S(2)}) copy-start(f32[2048]{0:T(1024)S(1)} %convert_element_type.143) | copy-start | bytes 24580
  58.7 188.9 %copy-start.63 = (f32[384]{0:T(512)}, f32[384]{0:T(512)S(1)}, u32[]{:S(2)}) copy-start(f32[384]{0:T(512)S(1)} %add_rsqrt_fusion.3) | copy-start | bytes 4612
  59.1 122.8 %copy-start.46 = (f32[384,64]{0,1:T(8,128)}, f32[384,64]{0,1:T(8,128)S(1)}, u32[]{:S(2)}) copy-start(f32[384,64]{0,1:T(8,128)S(1)} %get-tuple-element.1064) | copy-start | bytes 294916
  59.2 122.8 %copy-start.48 = (f32[384,64]{0,1:T(8,128)}, f32[384,64]{0,1:T(8,128)S(1)}, u32[]{:S(2)}) copy-start(f32[384,64]{0,1:T(8,128)S(1)} %get-tuple-element.1065) | copy-start | bytes 294916
  188.7 140.3 %copy-start.76 = (s32[1,1536,8]{1,2,0:T(8,128)S(1)}, s32[1,1536,8]{1,2,0:T(8,128)}, u32[]{:S(2)}) copy-start(s32[1,1536,8]{1,2,0:T(8,128)} %param.53) | copy-start | bytes 147460
  188.7 290.3 %all-gather.34.cloned.1.call-start = ((), (), s32[]{:S(2)}) async-start(), calls=%async_computation.15 | async-start | bytes 7864320 | tf_op jit(solution)/shard_map/all_gather | solution.py:233
  255.7 74.6 %copy-start.90 = (s32[1,1536]{1,0:T(1,128)S(1)}, s32[1,1536]{1,0:T(1,128)}, u32[]{:S(2)}) copy-start(s32[1,1536]{1,0:T(1,128)} %param.52) | copy-start | bytes 18436
  255.7 339.3 %all-gather.42.cloned.1.call-start = ((), (), s32[]{:S(2)}) async-start(), calls=%async_computation.19 | async-start | bytes 8650752 | tf_op jit(solution)/shard_map/all_gather | solution.py:191
  675.9 415.2 %all-to-all-start = ((bf16[16,288,2048]{2,1,0:T(8,128)(2,1)}), bf16[16,288,2048]{2,1,0:T(8,128)(2,1)}, u32[]{:S(2)}, u32[]{:S(2)}) async-start(bf16[16,288,2048]{2,1,0:T(8,128)(2,1)} %bitcast.500), calls=%async_computation.3 | async-start | bytes 37748736 | tf_op jit(solution)/shard_map/all_to_all | solution.py:120
  1091.1 414.9 %all-to-all-start.2 = ((bf16[16,288,2048]{2,1,0:T(8,128)(2,1)}), bf16[16,288,2048]{2,1,0:T(8,128)(2,1)}, u32[]{:S(2)}, u32[]{:S(2)}) async-start(bf16[16,288,2048]{2,1,0:T(8,128)(2,1)} %bitcast.498), calls=%async_computation.5 | async-start | bytes 37748736 | tf_op jit(solution)/shard_map/all_to_all | solution.py:120
  1610.9 42.3 all-gather.46.cloned.1.call-start
  1612.8 79.8 %all-gather.48.cloned.1.call-start = ((), (), s32[]{:S(2)}) async-start(), calls=%async_computation.29 | async-start | bytes 4718592 | tf_op jit(solution)/shard_map/while/body/eval_jaxpr/all_gather | solution.py:145
  1614.7 117.2 %all-gather.44.cloned.1.call-start = ((), (), s32[]{:S(2)}) async-start(), calls=%async_computation.27 | async-start | bytes 4718592 | tf_op jit(solution)/shard_map/while/body/eval_jaxpr/all_gather | solution.py:147
  1741.1 39.9 all-gather.46.cloned.1.call-start
  1743.0 77.4 %all-gather.48.cloned.1.call-start = ((), (), s32[]{:S(2)}) async-start(), calls=%async_computation.29 | async-start | bytes 4718592 | tf_op jit(solution)/shard_map/while/body/eval_jaxpr/all_gather | solution.py:145
  1744.9 114.6 %all-gather.44.cloned.1.call-start = ((), (), s32[]{:S(2)}) async-start(), calls=%async_computation.27 | async-start | bytes 4718592 | tf_op jit(solution)/shard_map/while/body/eval_jaxpr/all_gather | solution.py:147
  1868.7 40.2 all-gather.46.cloned.1.call-start
  1870.6 77.5 %all-gather.48.cloned.1.call-start = ((), (), s32[]{:S(2)}) async-start(), calls=%async_computation.29 | async-start | bytes 4718592 | tf_op jit(solution)/shard_map/while/body/eval_jaxpr/all_gather | solution.py:145
  1872.6 114.8 %all-gather.44.cloned.1.call-start = ((), (), s32[]{:S(2)}) async-start(), calls=%async_computation.27 | async-start | bytes 4718592 | tf_op jit(solution)/shard_map/while/body/eval_jaxpr/all_gather | solution.py:147
  1996.5 39.9 all-gather.46.cloned.1.call-start
  1998.4 77.2 %all-gather.48.cloned.1.call-start = ((), (), s32[]{:S(2)}) async-start(), calls=%async_computation.29 | async-start | bytes 4718592 | tf_op jit(solution)/shard_map/while/body/eval_jaxpr/all_gather | solution.py:145
  2000.4 114.5 %all-gather.44.cloned.1.call-start = ((), (), s32[]{:S(2)}) async-start(), calls=%async_computation.27 | async-start | bytes 4718592 | tf_op jit(solution)/shard_map/while/body/eval_jaxpr/all_gather | solution.py:147
  2130.3 1141.6 %copy-start = (s32[4608]{0:T(1024)S(1)}, s32[4608]{0:T(1024)}, u32[]{:S(2)}) copy-start(s32[4608]{0:T(1024)} %reshape.934) | copy-start | bytes 55300
  2130.7 40.2 all-gather.50.cloned.1.call-start
  2131.6 94.2 %reduce-scatter.31.cloned.1.call-start = ((), (), s32[]{:S(2)}) async-start(), calls=%async_computation.35 | async-start | bytes 4718592 | tf_op jit(solution)/shard_map/while/body/eval_jaxpr/reduce_scatter | solution.py:352
  2141.0 124.0 %all-gather.52.cloned.1.call-start = ((), (), s32[]{:S(2)}) async-start(), calls=%async_computation.31 | async-start | bytes 4718592 | tf_op jit(solution)/shard_map/while/body/eval_jaxpr/all_gather | solution.py:146
  2143.0 161.2 %all-gather.54.cloned.1.call-start = ((), (), s32[]{:S(2)}) async-start(), calls=%async_computation.32 | async-start | bytes 4718592 | tf_op jit(solution)/shard_map/while/body/eval_jaxpr/all_gather | solution.py:145
  2145.0 214.0 %reduce-scatter.27.cloned.1.call-start = ((), (), s32[]{:S(2)}) async-start(), calls=%async_computation.33 | async-start | bytes 4718592 | tf_op jit(solution)/shard_map/while/body/eval_jaxpr/reduce_scatter | solution.py:346
  2189.8 224.1 %reduce-scatter.29.cloned.1.call-start = ((), (), s32[]{:S(2)}) async-start(), calls=%async_computation.34 | async-start | bytes 4718592 | tf_op jit(solution)/shard_map/while/body/eval_jaxpr/reduce_scatter | solution.py:349
  2416.0 40.2 all-gather.50.cloned.1.call-start
  2416.9 94.3 %reduce-scatter.31.cloned.1.call-start = ((), (), s32[]{:S(2)}) async-start(), calls=%async_computation.35 | async-start | bytes 4718592 | tf_op jit(solution)/shard_map/while/body/eval_jaxpr/reduce_scatter | solution.py:352
  2426.3 123.9 %all-gather.52.cloned.1.call-start = ((), (), s32[]{:S(2)}) async-start(), calls=%async_computation.31 | async-start | bytes 4718592 | tf_op jit(solution)/shard_map/while/body/eval_jaxpr/all_gather | solution.py:146
  2428.3 161.2 %all-gather.54.cloned.1.call-start = ((), (), s32[]{:S(2)}) async-start(), calls=%async_computation.32 | async-start | bytes 4718592 | tf_op jit(solution)/shard_map/while/body/eval_jaxpr/all_gather | solution.py:145
  2430.3 213.9 %reduce-scatter.27.cloned.1.call-start = ((), (), s32[]{:S(2)}) async-start(), calls=%async_computation.33 | async-start | bytes 4718592 | tf_op jit(solution)/shard_map/while/body/eval_jaxpr/reduce_scatter | solution.py:346
  2475.2 223.9 %reduce-scatter.29.cloned.1.call-start = ((), (), s32[]{:S(2)}) async-start(), calls=%async_computation.34 | async-start | bytes 4718592 | tf_op jit(solution)/shard_map/while/body/eval_jaxpr/reduce_scatter | solution.py:349
  2701.2 40.2 all-gather.50.cloned.1.call-start
  2702.1 94.4 %reduce-scatter.31.cloned.1.call-start = ((), (), s32[]{:S(2)}) async-start(), calls=%async_computation.35 | async-start | bytes 4718592 | tf_op jit(solution)/shard_map/while/body/eval_jaxpr/reduce_scatter | solution.py:352
  2711.7 123.9 %all-gather.52.cloned.1.call-start = ((), (), s32[]{:S(2)}) async-start(), calls=%async_computation.31 | async-start | bytes 4718592 | tf_op jit(solution)/shard_map/while/body/eval_jaxpr/all_gather | solution.py:146
  2713.7 161.2 %all-gather.54.cloned.1.call-start = ((), (), s32[]{:S(2)}) async-start(), calls=%async_computation.32 | async-start | bytes 4718592 | tf_op jit(solution)/shard_map/while/body/eval_jaxpr/all_gather | solution.py:145
  2715.6 213.9 %reduce-scatter.27.cloned.1.call-start = ((), (), s32[]{:S(2)}) async-start(), calls=%async_computation.33 | async-start | bytes 4718592 | tf_op jit(solution)/shard_map/while/body/eval_jaxpr/reduce_scatter | solution.py:346
  2760.5 223.9 %reduce-scatter.29.cloned.1.call-start = ((), (), s32[]{:S(2)}) async-start(), calls=%async_computation.34 | async-start | bytes 4718592 | tf_op jit(solution)/shard_map/while/body/eval_jaxpr/reduce_scatter | solution.py:349
  2986.6 39.9 all-gather.50.cloned.1.call-start
  2987.4 94.1 %reduce-scatter.31.cloned.1.call-start = ((), (), s32[]{:S(2)}) async-start(), calls=%async_computation.35 | async-start | bytes 4718592 | tf_op jit(solution)/shard_map/while/body/eval_jaxpr/reduce_scatter | solution.py:352
  2996.9 123.8 %all-gather.52.cloned.1.call-start = ((), (), s32[]{:S(2)}) async-start(), calls=%async_computation.31 | async-start | bytes 4718592 | tf_op jit(solution)/shard_map/while/body/eval_jaxpr/all_gather | solution.py:146
  2998.9 161.0 %all-gather.54.cloned.1.call-start = ((), (), s32[]{:S(2)}) async-start(), calls=%async_computation.32 | async-start | bytes 4718592 | tf_op jit(solution)/shard_map/while/body/eval_jaxpr/all_gather | solution.py:145
  3000.8 213.7 %reduce-scatter.27.cloned.1.call-start = ((), (), s32[]{:S(2)}) async-start(), calls=%async_computation.33 | async-start | bytes 4718592 | tf_op jit(solution)/shard_map/while/body/eval_jaxpr/reduce_scatter | solution.py:346
  3045.4 224.2 %reduce-scatter.29.cloned.1.call-start = ((), (), s32[]{:S(2)}) async-start(), calls=%async_computation.34 | async-start | bytes 4718592 | tf_op jit(solution)/shard_map/while/body/eval_jaxpr/reduce_scatter | solution.py:349
  3422.5 151.4 %copy-start.56 = (pred[4,1152]{0,1:T(8,128)(4,1)S(1)}, pred[4,1152]{0,1:T(8,128)(4,1)}, u32[]{:S(2)}) copy-start(pred[4,1152]{0,1:T(8,128)(4,1)} %copy.352) | copy-start | bytes 13828
  4095.6 415.2 %all-to-all-start.1 = ((bf16[4,1152,2048]{2,0,1:T(4,128)(2,1)}), bf16[4,1152,2048]{2,0,1:T(4,128)(2,1)}, u32[]{:S(2)}, u32[]{:S(2)}) async-start(bf16[4,1152,2048]{2,0,1:T(4,128)(2,1)} %get-tuple-element.1063), calls=%async_computation.4 | async-start | bytes 37748736 | tf_op jit(solution)/shard_map/all_to_all | solution.py:124
  4105.2 785.6 %reduce-scatter.13.cloned.1.call-start = ((), (), s32[]{:S(2)}) async-start(), calls=%async_computation.20 | async-start | bytes 7864320 | tf_op jit(solution)/shard_map/reduce_scatter | solution.py:421
  4777.5 226.9 %reduce-scatter.15.cloned.1.call-start = ((), (), s32[]{:S(2)}) async-start(), calls=%async_computation.21 | async-start | bytes 7864320 | tf_op jit(solution)/shard_map/reduce_scatter | solution.py:427
  4790.6 339.5 %reduce-scatter.25.cloned.1.call-start = ((), (), s32[]{:S(2)}) async-start(), calls=%async_computation.26 | async-start | bytes 1081344
  4794.7 708.0 %reduce-scatter.23.cloned.1.call-start = ((), (), s32[]{:S(2)}) async-start(), calls=%async_computation.25 | async-start | bytes 17301504 | tf_op jit(solution)/shard_map/reduce_scatter | solution.py:460
  4804.3 89.6 %copy-start.7 = (f32[384,16,128]{0,2,1:T(8,128)S(1)}, f32[384,16,128]{0,2,1:T(8,128)}, u32[]{:S(2)}) copy-start(f32[384,16,128]{0,2,1:T(8,128)} %get-tuple-element.365) | copy-start | bytes 9437188
  4804.3 89.6 %copy-start.47 = (f32[384,64]{0,1:T(8,128)S(1)}, f32[384,64]{0,1:T(8,128)}, u32[]{:S(2)}) copy-start(f32[384,64]{0,1:T(8,128)} %copy-done.46) | copy-start | bytes 294916
  4804.3 89.6 %copy-start.49 = (f32[384,64]{0,1:T(8,128)S(1)}, f32[384,64]{0,1:T(8,128)}, u32[]{:S(2)}) copy-start(f32[384,64]{0,1:T(8,128)} %copy-done.48) | copy-start | bytes 294916
  4804.3 1063.0 %reduce-scatter.19.cloned.1.call-start = ((), (), s32[]{:S(2)}) async-start(), calls=%async_computation.23 | async-start | bytes 17301504 | tf_op jit(solution)/shard_map/reduce_scatter | solution.py:458
  4917.7 1314.6 %reduce-scatter.17.cloned.1.call-start = ((), (), s32[]{:S(2)}) async-start(), calls=%async_computation.22 | async-start | bytes 17301504 | tf_op jit(solution)/shard_map/reduce_scatter | solution.py:457
  4940.2 1657.2 %reduce-scatter.21.cloned.1.call-start = ((), (), s32[]{:S(2)}) async-start(), calls=%async_computation.24 | async-start | bytes 17301504 | tf_op jit(solution)/shard_map/reduce_scatter | solution.py:459
  (96 other events, 1255.8 us)
Sparse Core Ops, SparseCore 0:
  10.9 78.7 all-gather.35
  92.7 75.9 all-gather.39
  171.6 75.9 all-gather.31
  249.6 113.8 all-gather.37
  365.5 113.4 all-gather.33
  481.8 78.3 all-gather.41
  1614.3 38.7 all-gather.45
  1655.8 36.7 all-gather.47
  1695.2 36.7 all-gather.43
  1744.2 36.6 all-gather.45
  1783.6 36.7 all-gather.47
  1822.8 36.7 all-gather.43
  1872.2 36.7 all-gather.45
  1911.4 36.7 all-gather.47
  1950.6 36.7 all-gather.43
  1999.7 36.7 all-gather.45
  2038.9 36.7 all-gather.47
  2078.1 36.7 all-gather.43
  2134.2 36.7 all-gather.49
  2174.5 51.2 reduce-scatter.30
  2228.3 36.7 all-gather.51
  2267.5 36.7 all-gather.53
  2307.6 51.2 reduce-scatter.26
  2362.5 51.3 reduce-scatter.28
  2419.5 36.7 all-gather.49
  2459.9 51.2 reduce-scatter.30
  2513.5 36.7 all-gather.51
  2552.7 36.7 all-gather.53
  2592.8 51.2 reduce-scatter.26
  2647.7 51.3 reduce-scatter.28
  2704.7 36.7 all-gather.49
  2745.2 51.2 reduce-scatter.30
  2798.8 36.7 all-gather.51
  2838.1 36.7 all-gather.53
  2878.2 51.2 reduce-scatter.26
  2933.1 51.3 reduce-scatter.28
  2989.7 36.7 all-gather.49
  3030.2 51.2 reduce-scatter.30
  3083.8 36.7 all-gather.51
  3123.1 36.7 all-gather.53
  3163.2 51.2 reduce-scatter.26
  3218.3 51.3 reduce-scatter.28
  4777.6 113.1 reduce-scatter.12
  4893.1 111.2 reduce-scatter.14
  5006.5 123.5 reduce-scatter.24
  5133.0 369.6 reduce-scatter.22
  5505.5 361.8 reduce-scatter.18
  5870.2 362.1 reduce-scatter.16
  6235.2 362.1 reduce-scatter.20
where the time goes:
time: 6620 us; the launch traced here: 6600 us
  waiting for transfers between devices  4120 us (62%)
  local copies, waits for them, and re-layouts  978 us (15%)
  blocking collectives  641 us (10%)
  matrix products  579 us (9%)
  other arithmetic  231 us (3%)
    all_to_all x2, waiting for transfers between devices, to_experts(): lax.all_to_all(sending, 'expert', split_axis=0, concat_axis=1, tiled=True)  612 us
    all_to_all x1, blocking collectives, from_experts(): lax.all_to_all(rows, 'expert', split_axis=1, concat_axis=0, tiled=True)  473 us
    all_to_all x1, waiting for transfers between devices, from_experts(): lax.all_to_all(rows, 'expert', split_axis=1, concat_axis=0, tiled=True)  375 us
    reduce_scatter x1, waiting for transfers between devices, body(): lax.psum_scatter(grad_query_w, ('dp', 'expert'), scatter_dimension=0, til...  365 us
    reduce_scatter x1, waiting for transfers between devices, body(): lax.psum_scatter(grad_value_w, ('dp', 'expert'), scatter_dimension=0, til...  365 us
    reduce_scatter x1, waiting for transfers between devices, body(): lax.psum_scatter(grad_key_w, ('dp', 'expert'), scatter_dimension=0, tiled...  365 us
    gather x3, local copies, waits for them, and re-layouts, spread_one_expert(): return jnp.take(rows, places, axis=0, mode='fill', fill_value=0)  303 us
    all_gather x8, waiting for transfers between devices, fetch_expert(): lax.all_gather(shards[1], 'dp', axis=0, tiled=True)  291 us
  transfers between devices with their start and end apart: 52, of which 50 were waited for; matrix products, arithmetic and copies ran while one was open for 14% of the time, Pallas kernels for 0%

commit v1 on v0

v1 whole, which is shorter than its diff:
```python
import functools

import jax
import jax.numpy as jnp
from jax import lax
from jax.experimental import pallas as pl
from jax.experimental.pallas import tpu as pltpu
from jax.sharding import PartitionSpec as P

HEADS = 16
HEAD_DIM = 128
TOPK = 8
EXPERTS = 16
GTOK = 1536
CAP = 768
PROMPT = 1024
CLEN = 128
BLOCKS = GTOK // CLEN
TILE = 256
EPS = 1e-05
BOTH = ("dp", "expert")
F32 = jnp.float32
BF16 = jnp.bfloat16
SCALE = HEAD_DIM ** (-0.5)
NEG = -1e30
SMALL = 128
MESH = pl.DeviceIdType.MESH


def norm_back(grad_rows, unit_rows, inverse, gain_vec):
    grad_unit = grad_rows * gain_vec
    inner_mean = jnp.mean(grad_unit * unit_rows, axis=-1, keepdims=True)
    return inverse * (grad_unit - unit_rows * inner_mean)


def cross_rows(left, right):
    return lax.dot_general(left, right, (((0,), (0,)), ((), ())), preferred_element_type=F32)


def by_transpose(left, right):
    return lax.dot_general(left, right, (((1,), (1,)), ((), ())), preferred_element_type=F32)


def plain(left, right):
    return lax.dot_general(left, right, (((1,), (0,)), ((), ())), preferred_element_type=F32)


def causal(rows):
    return lax.broadcasted_iota(jnp.int32, (rows, rows), 1) <= lax.broadcasted_iota(
        jnp.int32, (rows, rows), 0
    )


def tiles():
    out = []
    for i in range(PROMPT // TILE):
        keys = [(0, i * TILE, False)] if i else []
        out.append((i * TILE, TILE, keys + [(i * TILE, TILE, True)]))
    for c in range(PROMPT // CLEN, BLOCKS):
        out.append((c * CLEN, CLEN, [(0, PROMPT, False), (c * CLEN, CLEN, True)]))
    return out


def rope(values, cos_rows, sin_rows):
    return values * cos_rows + pltpu.roll(values, HEAD_DIM // 2, 1) * sin_rows


def attend_kernel(
    order, q_pre, k_pre, v_pre, inv_q, inv_k, gain_q, gain_k, cos, sin, q_rot, k_rot, v_out, mixed, lse
):
    for i in range(BLOCKS):
        here = pl.ds(i * CLEN, CLEN)
        there = pl.ds(pl.multiple_of(order[i] * CLEN, CLEN), CLEN)
        cos_rows, sin_rows = cos[there, :], sin[there, :]
        q_n = q_pre[there, :] * inv_q[there, :] * gain_q[...]
        k_n = k_pre[there, :] * inv_k[there, :] * gain_k[...]
        q_rot[here, :] = rope(q_n, cos_rows, sin_rows).astype(BF16)
        k_rot[here, :] = rope(k_n, cos_rows, sin_rows).astype(BF16)
        v_out[here, :] = v_pre[there, :].astype(BF16)
    for start, rows, keys in tiles():
        q = q_rot[pl.ds(start, rows), :]
        parts = []
        for k_start, k_rows, masked in keys:
            s = by_transpose(q, k_rot[pl.ds(k_start, k_rows), :]) * SCALE
            parts.append(jnp.where(causal(rows), s, NEG) if masked else s)
        top = functools.reduce(jnp.maximum, [jnp.max(s, axis=1, keepdims=True) for s in parts])
        exps = [jnp.exp(s - top) for s in parts]
        total = functools.reduce(lambda a, b: a + b, [jnp.sum(e, axis=1, keepdims=True) for e in exps])
        over = 1.0 / total
        result = None
        for e, (k_start, k_rows, _) in zip(exps, keys):
            term = plain((e * over).astype(BF16), v_out[pl.ds(k_start, k_rows), :])
            result = term if result is None else result + term
        lse[pl.ds(start, rows), :] = jnp.broadcast_to(top + jnp.log(total), (rows, HEAD_DIM))
        for j in range(rows // CLEN):
            block = start // CLEN + j
            there = pl.ds(pl.multiple_of(order[block] * CLEN, CLEN), CLEN)
            mixed[there, :] = result[j * CLEN : (j + 1) * CLEN].astype(BF16)


def attend(order, qkv, inv_q, inv_k, gain_q, gain_k, cos, sin):
    heads = qkv.shape[1] // (3 * HEAD_DIM)
    head = lambda off: pl.BlockSpec((GTOK, HEAD_DIM), lambda h, o: (0, h + off))
    whole = lambda w: pl.BlockSpec((GTOK, w), lambda h, o: (0, 0))
    gain = pl.BlockSpec((1, HEAD_DIM), lambda h, o: (0, h))
    wide = jax.ShapeDtypeStruct((GTOK, heads * HEAD_DIM), BF16)
    return pl.pallas_call(
        attend_kernel,
        grid_spec=pltpu.PrefetchScalarGridSpec(
            num_scalar_prefetch=1,
            grid=(heads,),
            in_specs=[head(0), head(heads), head(2 * heads), whole(1), whole(1), gain, gain]
            + [whole(HEAD_DIM)] * 2,
            out_specs=[head(0)] * 5,
        ),
        out_shape=[wide] * 4 + [jax.ShapeDtypeStruct((GTOK, heads * HEAD_DIM), F32)],
        compiler_params=pltpu.CompilerParams(vmem_limit_bytes=48 * 2**20),
    )(order, qkv, qkv, qkv, inv_q, inv_k, gain_q, gain_k, cos, sin)


def attend_back_kernel(
    order, q_rot, k_rot, v_in, lse, grad_mixed, cos, sin, dq_out, dk_out, dv_out, grads, dq, dk, dv
):
    for i in range(BLOCKS):
        there = pl.ds(pl.multiple_of(order[i] * CLEN, CLEN), CLEN)
        grads[pl.ds(i * CLEN, CLEN), :] = grad_mixed[there, :]
    dk[...] = jnp.zeros_like(dk)
    dv[...] = jnp.zeros_like(dv)
    for start, rows, keys in tiles():
        here = pl.ds(start, rows)
        q, g, level = q_rot[here, :], grads[here, :], lse[here, 0:1]
        probs, grad_probs, delta = [], [], 0.0
        for k_start, k_rows, masked in keys:
            s = by_transpose(q, k_rot[pl.ds(k_start, k_rows), :]) * SCALE
            s = jnp.where(causal(rows), s, NEG) if masked else s
            p = jnp.exp(s - level)
            gp = by_transpose(g, v_in[pl.ds(k_start, k_rows), :])
            delta = delta + jnp.sum(p * gp, axis=1, keepdims=True)
            probs.append(p)
            grad_probs.append(gp)
        total = None
        for p, gp, (k_start, k_rows, _) in zip(probs, grad_probs, keys):
            there = pl.ds(k_start, k_rows)
            raw = (p * (gp - delta) * SCALE).astype(BF16)
            term = plain(raw, k_rot[there, :])
            total = term if total is None else total + term
            dk[there, :] += cross_rows(raw, q)
            dv[there, :] += cross_rows(p.astype(BF16), g)
        dq[here, :] = total
    for i in range(BLOCKS):
        here = pl.ds(i * CLEN, CLEN)
        there = pl.ds(pl.multiple_of(order[i] * CLEN, CLEN), CLEN)
        cos_rows, sin_rows = cos[there, :], sin[there, :]
        dq_out[there, :] = rope(dq[here, :], cos_rows, -sin_rows)
        dk_out[there, :] = rope(dk[here, :], cos_rows, -sin_rows)
        dv_out[there, :] = dv[here, :].astype(BF16)


def attend_back(order, q_rot, k_rot, v_in, lse, grad_mixed, cos, sin):
    heads = q_rot.shape[1] // HEAD_DIM
    head = pl.BlockSpec((GTOK, HEAD_DIM), lambda h, o: (0, h))
    whole = pl.BlockSpec((GTOK, HEAD_DIM), lambda h, o: (0, 0))
    wide = lambda t: jax.ShapeDtypeStruct((GTOK, heads * HEAD_DIM), t)
    return pl.pallas_call(
        attend_back_kernel,
        grid_spec=pltpu.PrefetchScalarGridSpec(
            num_scalar_prefetch=1,
            grid=(heads,),
            in_specs=[head] * 5 + [whole] * 2,
            out_specs=[head] * 3,
            scratch_shapes=[
                pltpu.VMEM((GTOK, HEAD_DIM), BF16),
                pltpu.VMEM((GTOK, HEAD_DIM), F32),
                pltpu.VMEM((GTOK, HEAD_DIM), F32),
                pltpu.VMEM((GTOK, HEAD_DIM), F32),
            ],
        ),
        out_shape=[wide(F32), wide(F32), wide(BF16)],
        compiler_params=pltpu.CompilerParams(vmem_limit_bytes=48 * 2**20),
    )(order, q_rot, k_rot, v_in, lse, grad_mixed, cos, sin)


ANY=pl.BlockSpec(memory_space=pl.ANY); VM=pl.BlockSpec(memory_space=pltpu.VMEM)

def peer(i): return {"expert": i}

def greet_line(n):
    p=lax.axis_index("expert")
    bar=pltpu.get_barrier_semaphore()
    @pl.when(p>0)
    def _(): pl.semaphore_signal(bar,inc=1,device_id=peer(p-1))
    @pl.when(p<n-1)
    def _(): pl.semaphore_signal(bar,inc=1,device_id=peer(p+1))
    pl.semaphore_wait(bar,(p>0).astype(jnp.int32)+(p<n-1).astype(jnp.int32))
    return p

def greet_all(n):
    p=lax.axis_index("expert")
    bar=pltpu.get_barrier_semaphore()
    for s in range(1,n): pl.semaphore_signal(bar,inc=1,device_id=peer(lax.rem(p+s,n)))
    pl.semaphore_wait(bar,n-1)
    return p

def params(cid,mb=60): return pltpu.CompilerParams(collective_id=cid,has_side_effects=True,vmem_limit_bytes=mb*2**20)

def ag_kernel(n,rows,x,out,to_right,to_left,recv,local):
    p=greet_line(n)
    at=lambda j: out.at[pl.ds(pl.multiple_of(j*rows,rows),rows)]
    own=pltpu.make_async_copy(x,at(p),local); own.start()
    def copy(src,j,sems,q):
        return pltpu.make_async_remote_copy(src_ref=src,dst_ref=at(j),send_sem=sems.at[j],recv_sem=recv.at[j],device_id=peer(q),device_id_type=MESH)
    right=lambda src,j: copy(src,j,to_right,p+1)
    left=lambda src,j: copy(src,j,to_left,p-1)
    @pl.when(p<n-1)
    def _(): right(x,p).start()
    @pl.when(p>0)
    def _(): left(x,p).start()
    for s in range(1,n):
        j=p-s
        @pl.when(j>=0)
        def _():
            right(at(j),j).wait_recv()
            @pl.when(p<n-1)
            def _(): right(at(j),j).start()
        k=p+s
        @pl.when(k<n)
        def _():
            left(at(k),k).wait_recv()
            @pl.when(p>0)
            def _(): left(at(k),k).start()
    own.wait()
    for j in range(n):
        @pl.when((j<=p)&(p<n-1))
        def _(): right(x,j).wait_send()
        @pl.when((j>=p)&(p>0))
        def _(): left(x,j).wait_send()

def ag_z(x,n,cid):
    rows=x.shape[0]
    return pl.pallas_call(functools.partial(ag_kernel,n,rows),out_shape=jax.ShapeDtypeStruct((n*rows,)+x.shape[1:],x.dtype),
        in_specs=[ANY],out_specs=ANY,scratch_shapes=[pltpu.SemaphoreType.DMA((n,))]*3+[pltpu.SemaphoreType.DMA],
        compiler_params=params(cid))(x)

def rs_kernel(n,rows,C,depth,part,out,from_left,from_right,to_right,to_left,recv_r,recv_l):
    p=greet_line(n)
    size=rows//C
    def at(j,c): return part.at[pl.ds(pl.multiple_of(j*rows+c*size,size),size)]
    def right(j,c): return pltpu.make_async_remote_copy(src_ref=at(j,c),dst_ref=from_left.at[j*C+c],send_sem=to_right.at[j*C+c],recv_sem=recv_r.at[j*C+c],device_id=peer(p+1),device_id_type=MESH)
    def left(j,c): return pltpu.make_async_remote_copy(src_ref=at(j,c),dst_ref=from_right.at[j*C+c],send_sem=to_left.at[j*C+c],recv_sem=recv_l.at[j*C+c],device_id=peer(p-1),device_id_type=MESH)
    def add(j,c,buf):
        at(j,c)[...]=(at(j,c)[...].astype(F32)+buf[j*C+c].astype(F32)).astype(BF16)
    order=[(s,c) for s in range(n-1) for c in range(C)]
    for m,(s,c) in enumerate(order):
        j=n-1-s
        @pl.when(j>p)
        def _():
            @pl.when(p>0)
            def _():
                right(j,c).wait_recv(); add(j,c,from_left)
            if m>=depth:
                s0,c0=order[m-depth]
                right(n-1-s0,c0).wait_send()
            right(j,c).start()
        k=s
        @pl.when(k<p)
        def _():
            @pl.when(p<n-1)
            def _():
                left(k,c).wait_recv(); add(k,c,from_right)
            if m>=depth:
                s0,c0=order[m-depth]
                left(s0,c0).wait_send()
            left(k,c).start()
    for c in range(C):
        @pl.when(p>0)
        def _():
            right(p,c).wait_recv(); add(p,c,from_left)
        @pl.when(p<n-1)
        def _():
            left(p,c).wait_recv(); add(p,c,from_right)
        out[pl.ds(c*size,size)]=at(p,c)[...]
    for m,(s,c) in enumerate(order):
        j=n-1-s
        last_r=(n-1-p)*C
        @pl.when((j>p)&(m>=last_r-depth))
        def _(): right(j,c).wait_send()
        last_l=p*C
        @pl.when((s<p)&(m>=last_l-depth))
        def _(): left(s,c).wait_send()

def rs_z(part,n,cid,C=4,depth=2):
    rows=part.shape[0]//n; D=part.shape[1]
    return pl.pallas_call(functools.partial(rs_kernel,n,rows,C,depth),out_shape=jax.ShapeDtypeStruct((rows,D),BF16),
        in_specs=[VM],out_specs=VM,scratch_shapes=[pltpu.VMEM((n*C,rows//C,D),BF16)]*2+[pltpu.SemaphoreType.DMA((n*C,))]*4,
        compiler_params=params(cid))(part)

def a2a_kernel(n,rows,cols,x,out,send,recv,local):
    p=greet_all(n)
    src=lambda j: x.at[pl.ds(pl.multiple_of(j*rows,rows),rows)]
    dst=lambda c: out.at[:,pl.ds(pl.multiple_of(c*cols,cols),cols)]
    own=pltpu.make_async_copy(src(p),dst(p),local); own.start()
    def send_to(s):
        j=lax.rem(p+s,n)
        return pltpu.make_async_remote_copy(src_ref=src(j),dst_ref=dst(p),send_sem=send.at[s],recv_sem=recv.at[s],device_id=peer(j),device_id_type=MESH)
    for s in range(1,n): send_to(s).start()
    for s in range(1,n):
        c=lax.rem(p-s+n,n)
        pltpu.make_async_remote_copy(src_ref=src(p),dst_ref=dst(c),send_sem=send.at[s],recv_sem=recv.at[s],device_id=peer(c),device_id_type=MESH).wait_recv()
    for s in range(1,n): send_to(s).wait_send()
    own.wait()

def a2a_z(x,n,cid):
    rows=x.shape[0]//n; cols=x.shape[1]
    return pl.pallas_call(functools.partial(a2a_kernel,n,rows,cols),out_shape=jax.ShapeDtypeStruct((rows,n*cols),x.dtype),
        in_specs=[ANY],out_specs=ANY,scratch_shapes=[pltpu.SemaphoreType.DMA((n,))]*2+[pltpu.SemaphoreType.DMA],
        compiler_params=params(cid))(x)

def exchange_kernel(n, rows, x, out, send, recv, local):
    p = greet_all(n)
    at = lambda ref, j: ref.at[pl.ds(pl.multiple_of(j * rows, rows), rows)]
    own = pltpu.make_async_copy(at(x, p), at(out, p), local)
    own.start()

    def to(s):
        j = lax.rem(p + s, n)
        return pltpu.make_async_remote_copy(
            src_ref=at(x, j), dst_ref=at(out, p), send_sem=send.at[s], recv_sem=recv.at[s], device_id=peer(j),
            device_id_type=MESH,
        )

    for s in range(1, n):
        to(s).start()
    for s in range(1, n):
        to(s).wait_recv()
    for s in range(1, n):
        to(s).wait_send()
    own.wait()


def exchange_z(x, n, cid):
    return pl.pallas_call(
        functools.partial(exchange_kernel, n, x.shape[0] // n),
        out_shape=jax.ShapeDtypeStruct(x.shape, x.dtype),
        in_specs=[ANY],
        out_specs=ANY,
        scratch_shapes=[pltpu.SemaphoreType.DMA((n,))] * 2 + [pltpu.SemaphoreType.DMA],
        compiler_params=params(cid),
    )(x)


def sum_kernel(n,x,out,got,send,recv):
    p=greet_all(n)
    def send_to(s):
        return pltpu.make_async_remote_copy(src_ref=x,dst_ref=got.at[s],send_sem=send.at[s],recv_sem=recv.at[s],device_id=peer(lax.rem(p+s,n)),device_id_type=MESH)
    for s in range(1,n): send_to(s).start()
    tot=x[...]
    for s in range(1,n):
        send_to(s).wait_recv(); tot=tot+got[s]
    out[...]=tot
    for s in range(1,n): send_to(s).wait_send()

def sum_z(x,n,cid):
    return pl.pallas_call(functools.partial(sum_kernel,n),out_shape=jax.ShapeDtypeStruct(x.shape,x.dtype),in_specs=[VM],out_specs=VM,
        scratch_shapes=[pltpu.VMEM((n,)+x.shape,x.dtype)]+[pltpu.SemaphoreType.DMA((n,))]*2,compiler_params=params(cid))(x)


def row_moves(ways, dp):
    return [(d * ways + z, z * dp + d) for d in range(dp) for z in range(ways)]


def hops(up, down, count, ways):
    for _ in range(count):
        up = up + [lax.ppermute(up[-1], "expert", [(i, i + 1) for i in range(ways - 1)])]
        down = down + [lax.ppermute(down[-1], "expert", [(i + 1, i) for i in range(ways - 1)])]
    return up, down


def later(sent, other):
    up, down = sent
    last_up, last_down, other = lax.optimization_barrier((up[-1], down[-1], other))
    return up[:-1] + [last_up], down[:-1] + [last_down], other


def line_up(up, down, ways):
    line = jnp.concatenate(up[:0:-1] + down, axis=0)
    rows = down[0].shape[0]
    start = (ways - 1 - lax.axis_index("expert")) * rows
    return lax.dynamic_slice_in_dim(line, start, ways * rows, axis=0)


def block_order(segs, places):
    seg = segs.reshape(BLOCKS, CLEN)[:, 0]
    place = places.reshape(BLOCKS, CLEN)[:, 0]
    stand = jnp.where(seg == 0, place // CLEN, PROMPT // CLEN - 1 + seg)
    blocks = jnp.arange(BLOCKS, dtype=jnp.int32)
    return jnp.sum(jnp.where(stand[None, :] == blocks[:, None], blocks[None, :], 0), axis=1)


def slots(routes, priority):
    experts = jnp.arange(EXPERTS, dtype=jnp.int32)
    hits = jnp.any(routes[:, :, None] == experts[None, None, :], axis=1)
    index = jnp.arange(GTOK, dtype=jnp.int32)
    rank = jnp.sum(jnp.where(priority[:, None] == index[None, :], index[:, None], 0), axis=0)
    earlier = (rank[None, :] < rank[:, None]).astype(BF16)
    return hits, plain(earlier, hits.astype(BF16)).astype(jnp.int32)


def body(
    tokens,
    cotangent,
    attention_gain,
    query_weight,
    key_weight,
    value_weight,
    out_weight,
    query_norm,
    key_norm,
    mixture_gain,
    router_weight,
    gate_weight,
    up_weight,
    down_weight,
    segments,
    positions,
    priority,
    routes,
):
    tok_dev, width = tokens.shape
    experts_here = gate_weight.shape[0]
    ways = lax.axis_size("expert")
    z = lax.axis_index("expert")
    cols = width // ways
    first_row = z * tok_dev

    small = jnp.concatenate(
        [attention_gain[:, None], query_norm[:, None], key_norm[:, None], mixture_gain[:, None], router_weight],
        axis=1,
    )
    small = jnp.pad(small, ((0, 0), (0, SMALL - small.shape[1])))
    shard = jnp.stack([query_weight, key_weight, value_weight], axis=1)
    shard = shard.reshape(-1, 3, ways, cols).transpose(2, 0, 1, 3).reshape(ways, -1, 3 * cols)
    rest = jnp.concatenate([out_weight, small], axis=1)
    shard = jnp.concatenate([shard, jnp.broadcast_to(rest[None], (ways,) + rest.shape)], axis=2)
    shard = exchange_z(shard.reshape(-1, shard.shape[-1]), ways, 1)
    dense = lax.all_gather(shard, "dp", axis=0, tiled=True)
    qkv_weight = dense[:, : 3 * cols]
    out_full = dense[:, 3 * cols : 3 * cols + width]
    small = dense[:, 3 * cols + width :]
    attend_gain = small[:, 0].astype(F32)
    mix_gain = small[:, 3].astype(F32)
    router_full = small[:, 4 : 4 + EXPERTS]
    my_gains = lax.dynamic_slice_in_dim(small[:, 1:3], z * cols, cols, axis=0).astype(F32)
    gain_q, gain_k = my_gains[:, 0][None], my_gains[:, 1][None]
    out_mine = lax.dynamic_slice_in_dim(out_full, z * cols, cols, axis=0)
    tokens_all = ag_z(tokens, ways, 2)
    gate_full = lax.all_gather(gate_weight, "dp", axis=1, tiled=True)
    up_full = lax.all_gather(up_weight, "dp", axis=1, tiled=True)
    down_full = lax.all_gather(down_weight, "dp", axis=1, tiled=True)
    steps = [ways // 2, (3 * ways) // 4]
    early, tokens_all = lax.optimization_barrier((cotangent, tokens_all))
    sent = hops([early], [early], steps[0] - 1, ways)

    segs, places = segments[0], positions[0]
    order = block_order(segs, places)
    frequency = 10000.0 ** (-jnp.arange(0, HEAD_DIM // 2, dtype=F32) * 2.0 / HEAD_DIM)
    angles = places.astype(F32)[:, None] * frequency[None, :]
    cos, sin = jnp.cos(angles), jnp.sin(angles)
    cos = jnp.concatenate([cos, cos], axis=1)
    sin = jnp.concatenate([-sin, sin], axis=1)
    hits, slot = slots(routes[0], priority[0])
    my_hits = lax.dynamic_slice_in_dim(hits, z * experts_here, experts_here, axis=1)
    my_slot = lax.dynamic_slice_in_dim(slot, z * experts_here, experts_here, axis=1)
    my_slot = jnp.where(my_hits & (my_slot < CAP), my_slot, -1)
    chosen = my_slot.T[:, None, :] == jnp.arange(CAP, dtype=jnp.int32)[None, :, None]
    pick = chosen.astype(BF16)

    token_f = tokens_all.astype(F32)
    inverse_in = lax.rsqrt(jnp.mean(token_f * token_f, axis=-1, keepdims=True) + EPS)
    normed = (token_f * inverse_in * attend_gain).astype(BF16)
    qkv = plain(normed, qkv_weight)
    squares = jnp.sum(jnp.square(qkv[:, : 2 * cols]).reshape(GTOK, 2, cols), axis=-1)
    squares = sum_z(jnp.pad(squares.T, ((0, 6), (0, 0))), ways, 3)
    inv_q = lax.rsqrt(squares[0] / width + EPS)[:, None]
    inv_k = lax.rsqrt(squares[1] / width + EPS)[:, None]
    q_rot, k_rot, v_b, mixed_heads, lse = attend(order, qkv, inv_q, inv_k, gain_q, gain_k, cos, sin)
    mixed = a2a_z(mixed_heads, ways, 4)
    own_f = tokens.astype(F32)
    resid = own_f + plain(mixed, out_full)
    mix_inverse = lax.rsqrt(jnp.mean(resid * resid, axis=-1, keepdims=True) + EPS)
    mix_unit = resid * mix_inverse
    mix = (mix_unit * mix_gain).astype(BF16)
    mix_all = ag_z(mix, ways, 5)
    up, down, mix_all = later(sent, mix_all)
    sent = hops(up, down, steps[1] - steps[0], ways)

    router_all = jax.nn.softmax(plain(mix_all, router_full), axis=-1)
    my_weight = lax.dynamic_slice_in_dim(router_all, z * experts_here, experts_here, axis=1)
    slot_weight = jnp.sum(jnp.where(chosen, my_weight.T[:, None, :], 0.0), axis=-1)
    inputs = jnp.einsum("est,td->esd", pick, mix_all, preferred_element_type=F32).astype(BF16)
    up, down, inputs = later(sent, inputs)
    grad_all = line_up(*hops(up, down, ways - steps[1], ways), ways)
    gate_pre = jnp.einsum("esd,edf->esf", inputs, gate_full, preferred_element_type=F32)
    up_pre = jnp.einsum("esd,edf->esf", inputs, up_full, preferred_element_type=F32)
    sig = jax.nn.sigmoid(gate_pre)
    silu = gate_pre * sig
    hidden = (silu * up_pre).astype(BF16)
    grad_slots = jnp.einsum("est,td->esd", pick, grad_all, preferred_element_type=F32)
    grad_eo = (grad_slots * slot_weight[:, :, None]).astype(BF16)
    grad_down = jnp.einsum("esf,esd->efd", hidden, grad_eo, preferred_element_type=F32).astype(BF16)
    grad_eo, grad_down = lax.optimization_barrier((grad_eo, grad_down))
    out_down = lax.psum_scatter(grad_down, "dp", scatter_dimension=1, tiled=True).astype(F32)
    grad_hidden = jnp.einsum("esd,efd->esf", grad_eo, down_full, preferred_element_type=F32)
    grad_gate = (grad_hidden * up_pre * (sig * (1.0 + gate_pre * (1.0 - sig)))).astype(BF16)
    grad_up = (grad_hidden * silu).astype(BF16)
    grad_gate_w = jnp.einsum("esd,esf->edf", inputs, grad_gate, preferred_element_type=F32).astype(BF16)
    grad_gate, grad_up, grad_gate_w = lax.optimization_barrier((grad_gate, grad_up, grad_gate_w))
    out_gate = lax.psum_scatter(grad_gate_w, "dp", scatter_dimension=1, tiled=True).astype(F32)
    grad_up_w = jnp.einsum("esd,esf->edf", inputs, grad_up, preferred_element_type=F32).astype(BF16)
    grad_gate, grad_up, hidden, grad_up_w = lax.optimization_barrier((grad_gate, grad_up, hidden, grad_up_w))
    out_up = lax.psum_scatter(grad_up_w, "dp", scatter_dimension=1, tiled=True).astype(F32)

    expert_out = jnp.einsum("esf,efd->esd", hidden, down_full, preferred_element_type=F32).astype(BF16)
    slot_dots = jnp.sum(grad_slots * expert_out.astype(F32), axis=-1)
    my_route_grad = jnp.sum(jnp.where(chosen, slot_dots[:, :, None], 0.0), axis=1)
    route_grad = lax.all_to_all(my_route_grad, "expert", split_axis=1, concat_axis=0, tiled=True).T
    grad_in = (
        jnp.einsum("esf,edf->esd", grad_gate, gate_full, preferred_element_type=F32)
        + jnp.einsum("esf,edf->esd", grad_up, up_full, preferred_element_type=F32)
    ).astype(BF16)
    part = cross_rows(
        pick.reshape(experts_here * CAP, GTOK), grad_in.reshape(experts_here * CAP, width)
    ).astype(BF16)
    grad_routed = rs_z(part, ways, 6).astype(F32)
    spread = jnp.where(chosen, my_weight.T[:, None, :], 0.0).astype(BF16).reshape(experts_here * CAP, GTOK)
    part = cross_rows(spread, expert_out.reshape(experts_here * CAP, width)).astype(BF16)
    moe = lax.psum_scatter(part, "expert", scatter_dimension=0, tiled=True)
    output = (resid + moe.astype(F32)).astype(BF16)

    router = lax.dynamic_slice_in_dim(router_all, first_row, tok_dev, axis=0)
    grad_logits = (router * (route_grad - jnp.sum(router * route_grad, axis=-1, keepdims=True))).astype(BF16)
    grad_router_w = cross_rows(mix, grad_logits)
    grad_mix = grad_routed + by_transpose(grad_logits, router_full)
    grad_mix_gain = jnp.sum(grad_mix * mix_unit, axis=0)
    grad_resid = cotangent.astype(F32) + norm_back(grad_mix, mix_unit, mix_inverse, mix_gain)
    grad_branch = grad_resid.astype(BF16)
    branch_all = ag_z(grad_branch, ways, 7)
    grad_heads = by_transpose(branch_all, out_mine).astype(BF16)
    grad_out_w = cross_rows(mixed_heads, branch_all).astype(BF16)
    out_out = lax.psum_scatter(grad_out_w, "dp", scatter_dimension=0, tiled=True)
    out_out = lax.ppermute(out_out, BOTH, row_moves(ways, lax.axis_size("dp"))).astype(F32)

    dq, dk, dv = attend_back(order, q_rot, k_rot, v_b, lse, grad_heads, cos, sin)
    q_unit = qkv[:, :cols] * inv_q
    k_unit = qkv[:, cols : 2 * cols] * inv_k
    inner = jnp.stack(
        [jnp.sum(dq * gain_q * q_unit, axis=-1), jnp.sum(dk * gain_k * k_unit, axis=-1)], axis=0
    )
    inner = sum_z(jnp.pad(inner, ((0, 6), (0, 0))), ways, 8) / width
    grad_q_gain = jnp.sum(dq * q_unit, axis=0)
    grad_k_gain = jnp.sum(dk * k_unit, axis=0)
    grad_q = (inv_q * (dq * gain_q - q_unit * inner[0][:, None])).astype(BF16)
    grad_k = (inv_k * (dk * gain_k - k_unit * inner[1][:, None])).astype(BF16)
    grad_qkv = jnp.concatenate([grad_q, grad_k, dv], axis=1)
    grad_normed_part = by_transpose(grad_qkv, qkv_weight)
    grad_attend_gain = jnp.sum(grad_normed_part * (token_f * inverse_in), axis=0)
    grad_normed = rs_z(grad_normed_part.astype(BF16), ways, 9).astype(F32)
    own_inverse = lax.dynamic_slice_in_dim(inverse_in, first_row, tok_dev, axis=0)
    input_grad = grad_resid + norm_back(grad_normed, own_f * own_inverse, own_inverse, attend_gain)

    place = lambda part: lax.dynamic_update_slice(jnp.zeros((width,), F32), part, (z * cols,))
    extra = jnp.concatenate(
        [
            jnp.stack([grad_attend_gain, place(grad_q_gain), place(grad_k_gain), grad_mix_gain], axis=1),
            grad_router_w,
            jnp.zeros((width, SMALL - 4 - EXPERTS), F32),
        ],
        axis=1,
    )
    grad_qkv_w = jnp.concatenate([cross_rows(normed, grad_qkv), extra], axis=1).astype(BF16)
    grad_qkv_w = lax.psum_scatter(grad_qkv_w, "dp", scatter_dimension=0, tiled=True)
    grad_qkv_w = exchange_z(grad_qkv_w, ways, 10).reshape(ways, -1, 3 * cols + SMALL)
    grad_w = [
        grad_qkv_w[:, :, i * cols : (i + 1) * cols].transpose(1, 0, 2).reshape(-1, width).astype(F32)
        for i in range(3)
    ]
    packed = jnp.sum(grad_qkv_w[:, :, 3 * cols :].astype(F32), axis=0)
    return (
        output,
        input_grad,
        packed[:, 0],
        grad_w[0],
        grad_w[1],
        grad_w[2],
        out_out,
        packed[:, 1],
        packed[:, 2],
        packed[:, 3],
        packed[:, 4 : 4 + EXPERTS],
        out_gate,
        out_up,
        out_down,
    )


def solution(mesh):
    rows = P(BOTH, None)
    vec = P(BOTH)
    expert = P("expert", "dp", None)
    group = P("dp", None)
    return jax.shard_map(
        body,
        mesh=mesh,
        in_specs=(rows, rows, vec, rows, rows, rows, rows, vec, vec, vec, rows, expert, expert, expert)
        + (group, group, group, P("dp", None, None)),
        out_specs=(rows, rows, vec, rows, rows, rows, rows, vec, vec, vec, rows, expert, expert, expert),
        check_vma=False,
    )
```

time: 6620 us -> 1690 us (0.26)
  waiting for transfers between devices: 4120 us -> 320 us
  local copies, waits for them, and re-layouts: 978 us -> 63.1 us
  Pallas kernels: 0 us -> 785 us
  blocking collectives: 641 us -> 0 us
  matrix products: 579 us -> 397 us
  other arithmetic: 231 us -> 67.6 us
    reduce_scatter x18 -> x6, waiting for transfers between devices: 2040 us -> 314 us  [the longest x1 116 us: body(): lax.psum_scatter(grad_up_w, 'dp', scatter_dimension=1, tiled=True)]
    all_to_all x3 -> x1, waiting for transfers between devices: 987 us -> 0.01 us  [body(): lax.all_to_all(my_route_grad, 'expert', split_axis=1, concat_axis=0, tile...]
    all_gather x30 -> x4, waiting for transfers between devices: 983 us -> 0.04 us  [the longest x1 0.02 us: body(): gate_full = lax.all_gather(gate_weight, 'dp', axis=1, tiled=True)]
    pallas_call x0 -> x12, Pallas kernels: none -> 785 us  [the longest x2 307 us: rs_z(): pl.pallas_call(functools.partial(rs_kernel, n, rows, C, depth), out_shape...]
    all_to_all x1 -> x0, blocking collectives: 473 us -> none  [from_experts(): lax.all_to_all(rows, 'expert', split_axis=1, concat_axis=0, tiled=True)]
    gather x16 -> x0, local copies, waits for them, and re-layouts: 441 us -> none  [the longest x3 303 us: spread_one_expert(): return jnp.take(rows, places, axis=0, mode='fill', fill_value=0)]
    unnamed x217 -> x93, local copies, waits for them, and re-layouts: 169 us -> 14.3 us
    dot_general x17 -> x3, matrix products: 145 us -> 29.6 us  [by_transpose(): lax.dot_general(left, right, (((1,), (1,)), ((), ())), preferred_element_...]
  transfers between devices with their start and end apart: 52 -> 18, of which waited for: 50 -> 4; matrix products, arithmetic and copies ran while one was open for 14% -> 23% of each run, Pallas kernels for 0% -> 37%
where the time goes in v1:
time: 1690 us; the launch traced here: 1680 us
  Pallas kernels  785 us (46%)
  matrix products  397 us (23%)
  waiting for transfers between devices  320 us (19%)
  other arithmetic  67.6 us (4%)
  local copies, waits for them, and re-layouts  63.1 us (4%)
  starting transfers between devices  32.1 us (2%)
    pallas_call x2, Pallas kernels, rs_z(): pl.pallas_call(functools.partial(rs_kernel, n, rows, C, depth), out_shape...  307 us
    pallas_call x3, Pallas kernels, ag_z(): pl.pallas_call(functools.partial(ag_kernel, n, rows), out_shape=jax.Shape...  298 us
    reduce_scatter x1, waiting for transfers between devices, body(): lax.psum_scatter(grad_up_w, 'dp', scatter_dimension=1, tiled=True)  116 us
    reduce_scatter x1, waiting for transfers between devices, body(): lax.psum_scatter(grad_down, 'dp', scatter_dimension=1, tiled=True)  115 us
    reduce_scatter x1, waiting for transfers between devices, body(): lax.psum_scatter(grad_gate_w, 'dp', scatter_dimension=1, tiled=True)  82.9 us
    pallas_call x2, Pallas kernels, exchange_z(): pl.pallas_call(functools.partial(exchange_kernel, n, x.shape[0] // n), ou...  75.8 us
    dot_general x5, matrix products, cross_rows(): lax.dot_general(left, right, (((0,), (0,)), ((), ())), preferred_element_...  73.6 us
    pallas_call x1, Pallas kernels, a2a_z(): pl.pallas_call(functools.partial(a2a_kernel, n, rows, cols), out_shape=ja...  33.8 us
  transfers between devices with their start and end apart: 18, of which 4 were waited for; matrix products, arithmetic and copies ran while one was open for 23% of the time, Pallas kernels for 37%

profile of v1, /device:TPU:10, one launch (start us, length us, event | category | flops | bytes accessed | tf_op | source)
XLA Modules:
  0.0 1680.2 jit_solution(8297504760016617917)
XLA Ops:
  13.6 1.8 pad_maximum_fusion.4
  17.1 44.6 %shard_map.282 = bf16[256,3712]{1,0:T(8,128)(2,1)} custom-call(bf16[256,3712]{1,0:T(8,128)(2,1)} %pad_maximum_fusion.3.x), custom_call_target="tpu_custom_call" | custom-call | tf_op jit(solution)/shard_map/pallas_call | solution.py:341
  63.9 104.8 %shard_map.281 = bf16[1536,2048]{1,0:T(8,128)(2,1)} custom-call(bf16[384,2048]{1,0:T(8,128)(2,1)} %x.7), custom_call_target="tpu_custom_call" | custom-call | tf_op jit(solution)/shard_map/pallas_call | solution.py:240
  168.6 3.0 collective-permute-start
  171.6 4.6 collective-permute-start.1
  176.8 4.1 fusion.7
  183.5 2.8 fusion.45
  186.9 1.8 convert_reduce_fusion
  188.7 18.2 %fusion.24 = f32[1536,1536]{0,1:T(8,128)} fusion(bf16[2048,3712]{1,0:T(8,128)(2,1)} %all-gather.5.cloned.1.call-done, bf16[1536,2048]{1,0:T(8,128)(2,1)} %shard_map.281, f32[2048]{0:T(1024)S(1)} %get-tuple-element.121, f32[1536]{0:T(1024)S(1)} %add_rsqrt_fusion), kind=kOutput, calls=%fused_computation.48 | convolution fusion | flops 9676259328 | bytes 22034432 | tf_op jit(solution)/shard_map/dot_general | solution.py:45
  206.9 9.8 copy.174.q_pre.k_pre.v_pre
  216.7 3.5 bitcast_reduce_fusion
  220.8 8.1 shard_map.283
  232.6 26.1 %shard_map.284 = (bf16[1536,512]{1,0:T(8,128)(2,1)S(1)}, bf16[1536,512]{1,0:T(8,128)(2,1)}, bf16[1536,512]{1,0:T(8,128)(2,1)}, bf16[1536,512]{1,0:T(8,128)(2,1)}, f32[1536,512]{1,0:T(8,128)}) custom-call(s32[12]{0:T(128)S(1)} %select_reduce_fusion.3.order, f32[1536,1536]{1,0:T(8,128)} %copy.174.q_pre.k_pre.v_pre, f32[1536,1536]{1,0:T(8,128)} %copy.174.q_pre.k_pre.v_pre, ...), custom_call_target="tpu_custom_call" | custom-call | tf_op jit(solution)/shard_map/pallas_call | solution.py:107
  259.9 33.8 %shard_map.285 = bf16[384,2048]{1,0:T(8,128)(2,1)} custom-call(bf16[1536,512]{1,0:T(8,128)(2,1)} %get-tuple-element.40.x), custom_call_target="tpu_custom_call" | custom-call | tf_op jit(solution)/shard_map/pallas_call | solution.py:314
  293.7 8.0 multiply_reduce_fusion.7
  305.0 104.4 %shard_map.286 = bf16[1536,2048]{1,0:T(8,128)(2,1)} custom-call(bf16[384,2048]{1,0:T(8,128)(2,1)} %multiply_convert_fusion.6.x), custom_call_target="tpu_custom_call" | custom-call | tf_op jit(solution)/shard_map/pallas_call | solution.py:240
  409.5 3.3 collective-permute-start.2
  412.7 4.1 collective-permute-start.3
  416.9 24.7 %fusion.18 = bf16[4,768,2048]{2,1,0:T(8,128)(2,1)} fusion(s32[4,1536]{1,0:T(4,128)S(1)} %select_bitcast_fusion, bf16[1536,2048]{1,0:T(8,128)(2,1)} %shard_map.286), kind=kOutput, calls=%fused_computation.40 | convolution fusion | flops 19338362880 | bytes 18898944 | tf_op jit(solution)/shard_map/est,td->esd/dot_general | solution.py:499
  441.6 2.9 fusion.62
  444.4 8.3 slice.117
  452.8 2.4 select_reduce_fusion
  455.3 2.2 collective-permute-start.4
  457.5 4.8 collective-permute-start.5
  462.3 23.0 %fusion.63 = f32[4,768,1024]{2,1,0:T(8,128)} fusion(bf16[4,768,2048]{2,1,0:T(8,128)(2,1)} %fusion.18, bf16[4,2048,1024]{2,1,0:T(8,128)(2,1)} %all-gather.7.cloned.1.call-done), kind=kOutput, calls=%fused_computation.163 | convolution fusion | flops 12884901888 | bytes 41943040 | tf_op jit(solution)/shard_map/esd,edf->esf/dot_general | solution.py:502
  485.3 26.5 %multiply_convert_fusion.3 = (bf16[4,768,1024]{2,1,0:T(8,128)(2,1)}, f32[4,768,1024]{2,1,0:T(8,128)}) fusion(f32[4,768,1024]{2,1,0:T(8,128)} %fusion.63, bf16[4,768,2048]{2,1,0:T(8,128)(2,1)} %fusion.18, bf16[4,2048,1024]{2,1,0:T(8,128)(2,1)} %all-gather.9.cloned.1.call-done), kind=kOutput, calls=%fused_computation.24 | convolution fusion | flops 12903776256 | bytes 60817408 | tf_op jit(solution)/shard_map/esd,edf->esf/dot_general | solution.py:503
  521.4 25.8 %multiply_convert_fusion = (bf16[4,768,2048]{2,1,0:T(8,128)(2,1)}, f32[4,768,2048]{2,1,0:T(8,128)}) fusion(f32[4,768]{1,0:T(4,128)S(1)} %select_reduce_fusion, bf16[2688,2048]{1,0:T(8,128)(2,1)S(1)} %constant_dynamic-update-slice_fusion, s32[]{:T(128)S(6)} %select_n.63, s32[4,1536]{1,0:T(4,128)S(1)} %select_bitcast_fusion), kind=kOutput, calls=%fused_computation.2 | convolution fusion | flops 19344654336 | bytes 44077060 | tf_op jit(solution)/shard_map/est,td->esd/dot_general | solution.py:507
  547.2 22.2 %convolution_convert_fusion.2 = bf16[4,1024,2048]{2,1,0:T(8,128)(2,1)} fusion(bf16[4,768,1024]{2,1,0:T(8,128)(2,1)} %get-tuple-element.51, bf16[4,768,2048]{2,1,0:T(8,128)(2,1)} %get-tuple-element.48), kind=kOutput, calls=%fused_computation.16 | convolution fusion | flops 12893290496 | bytes 35651584 | tf_op jit(solution)/shard_map/esf,esd->efd/dot_general | solution.py:509
  569.5 29.6 %multiply_convert_fusion.1 = (bf16[4,768,1024]{2,1,0:T(8,128)(2,1)}, bf16[4,768,1024]{2,1,0:T(8,128)(2,1)}) fusion(f32[4,768,1024]{2,1,0:T(8,128)} %fusion.63, f32[4,768,1024]{2,1,0:T(8,128)} %get-tuple-element.163, bf16[4,768,2048]{2,1,0:T(8,128)(2,1)} %get-tuple-element.48, bf16[4,1024,2048]{2,1,0:T(8,128)(2,1)} %all-gather.11.cloned.1.call-done), kind=kOutput, calls=%fused_computation.22 | convolution fusion | flops 12925796352 | bytes 67108864 | tf_op jit(solution)/shard_map/esd,efd->esf/dot_general | solution.py:512
  599.1 19.5 %convolution_convert_fusion.1 = bf16[4,2048,1024]{2,1,0:T(8,128)(2,1)} fusion(bf16[4,768,2048]{2,1,0:T(8,128)(2,1)} %fusion.18, bf16[4,768,1024]{2,1,0:T(8,128)(2,1)} %get-tuple-element.52), kind=kOutput, calls=%fused_computation.15 | convolution fusion | flops 12893290496 | bytes 35651584 | tf_op jit(solution)/shard_map/esd,esf->edf/dot_general | solution.py:515
  618.6 19.5 %convolution_convert_fusion = bf16[4,2048,1024]{2,1,0:T(8,128)(2,1)} fusion(bf16[4,768,2048]{2,1,0:T(8,128)(2,1)} %fusion.18, bf16[4,768,1024]{2,1,0:T(8,128)(2,1)} %get-tuple-element.53), kind=kOutput, calls=%fused_computation.14 | convolution fusion | flops 12893290496 | bytes 35651584 | tf_op jit(solution)/shard_map/esd,esf->edf/dot_general | solution.py:518
  638.1 25.7 %multiply_reduce_fusion = (f32[4,768]{1,0:T(4,128)S(1)}, bf16[4,768,2048]{2,1,0:T(8,128)(2,1)}) fusion(f32[4,768,2048]{2,1,0:T(8,128)} %get-tuple-element.161, bf16[4,768,1024]{2,1,0:T(8,128)(2,1)} %get-tuple-element.51, bf16[4,1024,2048]{2,1,0:T(8,128)(2,1)} %all-gather.11.cloned.1.call-done), kind=kOutput, calls=%fused_computation | convolution fusion | flops 12910064640 | bytes 60829696 | tf_op jit(solution)/shard_map/esf,efd->esd/dot_general | solution.py:522
  663.8 3.7 select_reduce_fusion.1
  667.5 4.6 all-to-all-start
  672.1 21.9 %fusion.64 = f32[4,768,2048]{2,1,0:T(8,128)} fusion(bf16[4,768,1024]{2,1,0:T(8,128)(2,1)} %get-tuple-element.52, bf16[4,2048,1024]{2,1,0:T(8,128)(2,1)} %all-gather.7.cloned.1.call-done), kind=kOutput, calls=%fused_computation.164 | convolution fusion | flops 12884901888 | bytes 48234496 | tf_op jit(solution)/shard_map/esf,edf->esd/dot_general | solution.py:527
  694.0 24.3 %add_convert_fusion.8 = bf16[4,768,2048]{2,1,0:T(8,128)(2,1)} fusion(f32[4,768,2048]{2,1,0:T(8,128)} %fusion.64, bf16[4,768,1024]{2,1,0:T(8,128)(2,1)} %get-tuple-element.53, bf16[4,2048,1024]{2,1,0:T(8,128)(2,1)} %all-gather.9.cloned.1.call-done), kind=kOutput, calls=%fused_computation.1.clone.clone.clone.clone.2 | convolution fusion | flops 12897484800 | bytes 60817408 | tf_op jit(solution)/shard_map/esf,edf->esd/dot_general | solution.py:528
  718.4 24.4 %bitcast_convert_fusion.part = bf16[1536,2048]{1,0:T(8,128)(2,1)} fusion(s32[4,1536]{1,0:T(4,128)S(1)} %copy-done.24, bf16[4,768,2048]{2,1,0:T(8,128)(2,1)} %add_convert_fusion.8), kind=kOutput, calls=%fused_computation.20 | convolution fusion | flops 19335217152 | bytes 18898944 | tf_op jit(solution)/shard_map/dot_general | solution.py:37
  742.7 113.8 %shard_map.287 = bf16[384,2048]{1,0:T(8,128)(2,1)} custom-call(bf16[1536,2048]{1,0:T(8,128)(2,1)} %bitcast_convert_fusion.part), custom_call_target="tpu_custom_call" | custom-call | tf_op jit(solution)/shard_map/pallas_call | solution.py:293
  856.7 4.2 multiply_reduce_fusion.1
  860.9 1.7 copy-done.12
  862.6 3.6 fusion.61.x
  866.2 89.2 %shard_map.288 = bf16[1536,2048]{1,0:T(8,128)(2,1)} custom-call(bf16[384,2048]{1,0:T(8,128)(2,1)} %fusion.61.x), custom_call_target="tpu_custom_call" | custom-call | tf_op jit(solution)/shard_map/pallas_call | solution.py:240
  955.4 7.4 convolution_convert_fusion.5
  962.9 8.2 convolution_convert_fusion.6.grad_mixed
  971.1 27.4 %shard_map.289 = (f32[1536,512]{1,0:T(8,128)}, f32[1536,512]{1,0:T(8,128)}, bf16[1536,512]{1,0:T(8,128)(2,1)S(1)}) custom-call(s32[12]{0:T(128)S(1)} %select_reduce_fusion.3.order, bf16[1536,512]{1,0:T(8,128)(2,1)S(1)} %copy-done.1, bf16[1536,512]{1,0:T(8,128)(2,1)} %get-tuple-element.55.k_rot, bf16[1536,512]{1,0:T(8,128)(2,1)} %get-tuple-element.56.v_in, ...), custom_call_target="tpu_custom_call" | custom-call | tf_op jit(solution)/shard_map/pallas_call | solution.py:164
  998.5 6.1 multiply_reduce_fusion.2
  1005.3 9.1 shard_map.290
  1015.5 5.5 multiply_convert_fusion.5
  1021.0 17.2 %fusion.6 = (bf16[2048]{0:T(1024)(128)(2,1)S(1)}, bf16[1536,2048]{1,0:T(8,128)(2,1)}) fusion(bf16[1536,2048]{1,0:T(8,128)(2,1)} %shard_map.281, f32[1536]{0:T(1024)S(1)} %copy-done.38, bf16[2048,3712]{1,0:T(8,128)(2,1)} %all-gather.5.cloned.1.call-done, bf16[1536,512]{1,0:T(8,128)(2,1)S(1)} %copy-done.7, bf16[1536,512]{1,0:T(8,128)(2,1)S(1)} %get-tuple-element.145, ...), kind=kOutput, calls=%fused_computation.18 | convolution fusion | flops 9693558784 | bytes 23603200 | tf_op jit(solution)/shard_map/dot_general | solution.py:41
  1043.2 15.4 convolution_convert_fusion.3
  1058.8 12.0 concatenate.40
  1071.5 26.1 %bitcast_convert_fusion.1 = bf16[1536,2048]{1,0:T(8,128)(2,1)} fusion(bf16[4,768,2048]{2,1,0:T(8,128)(2,1)} %get-tuple-element.165, f32[4,1536]{1,0:T(4,128)S(1)} %copy-done.28, s32[4,1536]{1,0:T(4,128)S(1)} %copy-done.24), kind=kOutput, calls=%fused_computation.21 | convolution fusion | flops 19339935744 | bytes 18923520 | tf_op jit(solution)/shard_map/dot_general | solution.py:37
  1099.8 192.8 %shard_map.291 = bf16[384,2048]{1,0:T(8,128)(2,1)} custom-call(bf16[1536,2048]{1,0:T(8,128)(2,1)} %get-tuple-element.143.part), custom_call_target="tpu_custom_call" | custom-call | tf_op jit(solution)/shard_map/pallas_call | solution.py:293
  1292.6 4.9 collective-permute-start.6
  1297.5 2.6 fusion.32
  1300.1 2.3 collective-permute-done.6
  1303.3 31.2 %shard_map.292 = bf16[256,1664]{1,0:T(8,128)(2,1)} custom-call(bf16[256,1664]{1,0:T(8,128)(2,1)} %reduce-scatter.9.cloned.1.call-done.x), custom_call_target="tpu_custom_call" | custom-call | tf_op jit(solution)/shard_map/pallas_call | solution.py:341
  1340.8 6.4 fusion.35
  1347.2 82.9 %reduce-scatter.13.cloned.1.call-done = bf16[4,256,1024]{2,1,0:T(8,128)(2,1)} async-done(((bf16[4,2048,1024]{2,1,0:T(8,128)(2,1)}), bf16[4,256,1024]{2,1,0:T(8,128)(2,1)}) %reduce-scatter.13.cloned.1.call-update) | async-done | bytes 2097168 | tf_op jit(solution)/shard_map/reduce_scatter | solution.py:517
  1430.1 4.1 convert_element_type.226
  1434.2 115.5 %reduce-scatter.15.cloned.1.call-done = bf16[4,256,1024]{2,1,0:T(8,128)(2,1)} async-done(((bf16[4,2048,1024]{2,1,0:T(8,128)(2,1)}), bf16[4,256,1024]{2,1,0:T(8,128)(2,1)}) %reduce-scatter.15.cloned.1.call-update) | async-done | bytes 2097168 | tf_op jit(solution)/shard_map/reduce_scatter | solution.py:520
  1549.7 4.1 convert_element_type.227
  1553.7 115.3 %reduce-scatter.17.cloned.1.call-done = bf16[4,128,2048]{2,1,0:T(8,128)(2,1)} async-done(((bf16[4,1024,2048]{2,1,0:T(8,128)(2,1)}), bf16[4,128,2048]{2,1,0:T(8,128)(2,1)}) %reduce-scatter.17.cloned.1.call-update) | async-done | bytes 2097168 | tf_op jit(solution)/shard_map/reduce_scatter | solution.py:511
  1669.0 4.1 convert_element_type.228
  (192 shorter events, 48.9 us)
Async XLA Ops:
  7.2 8.4 copy-start.22
  7.2 179.7 %all-gather.5.cloned.1.call-start = ((), (), s32[]{:S(2)}) async-start(), calls=%async_computation.7 | async-start | bytes 17104896 | tf_op jit(solution)/shard_map/all_gather | solution.py:445
  61.7 400.5 %all-gather.7.cloned.1.call-start = ((), (), s32[]{:S(2)}) async-start(), calls=%async_computation.8 | async-start | bytes 18874368 | tf_op jit(solution)/shard_map/all_gather | solution.py:456
  62.5 113.7 %copy-start.39 = (s32[1,1536]{1,0:T(1,128)S(1)}, s32[1,1536]{1,0:T(1,128)}, u32[]{:S(2)}) copy-start(s32[1,1536]{1,0:T(1,128)} %param.32) | copy-start | bytes 18436
  62.5 113.8 %copy-start.36 = (s32[1,1536]{1,0:T(1,128)S(1)}, s32[1,1536]{1,0:T(1,128)}, u32[]{:S(2)}) copy-start(s32[1,1536]{1,0:T(1,128)} %param.33) | copy-start | bytes 18436
  62.5 113.9 %copy-start.40 = (s32[1,1536]{1,0:T(1,128)S(1)}, s32[1,1536]{1,0:T(1,128)}, u32[]{:S(2)}) copy-start(s32[1,1536]{1,0:T(1,128)} %param.34) | copy-start | bytes 18436
  62.5 114.1 %copy-start.35 = (s32[1,1536,8]{1,2,0:T(8,128)S(1)}, s32[1,1536,8]{1,2,0:T(8,128)}, u32[]{:S(2)}) copy-start(s32[1,1536,8]{1,2,0:T(8,128)} %param.35) | copy-start | bytes 147460
  62.5 422.7 %all-gather.9.cloned.1.call-start = ((), (), s32[]{:S(2)}) async-start(), calls=%async_computation.9 | async-start | bytes 18874368 | tf_op jit(solution)/shard_map/all_gather | solution.py:457
  63.3 506.2 %all-gather.11.cloned.1.call-start = ((), (), s32[]{:S(2)}) async-start(), calls=%async_computation.10 | async-start | bytes 18874368 | tf_op jit(solution)/shard_map/all_gather | solution.py:458
  168.6 240.8 %collective-permute-start = (bf16[384,2048]{1,0:T(8,128)(2,1)}, bf16[384,2048]{1,0:T(8,128)(2,1)}, u32[]{:S(2)}, u32[]{:S(2)}) collective-permute-start(bf16[384,2048]{1,0:T(8,128)(2,1)} %param.19), channel_id=1, source_target_pairs={{0,1},{1,2},{2,3},{4,5},{5,6},{6,7},{8,9},{9,10},{10,11},{12,13},{... | collective-permute-start | bytes 4718600 | tf_op jit(solution)/shard_map/ppermute | solution.py:373
  171.6 237.9 %collective-permute-start.1 = (bf16[384,2048]{1,0:T(8,128)(2,1)}, bf16[384,2048]{1,0:T(8,128)(2,1)}, u32[]{:S(2)}, u32[]{:S(2)}) collective-permute-start(bf16[384,2048]{1,0:T(8,128)(2,1)} %param.19), channel_id=1, source_target_pairs={{1,0},{2,1},{3,2},{5,4},{6,5},{7,6},{9,8},{10,9},{11,10},{13,12},{... | collective-permute-start | bytes 4718600 | tf_op jit(solution)/shard_map/ppermute | solution.py:374
  180.9 26.0 %copy-start.37 = (f32[1536]{0:T(1024)}, f32[1536]{0:T(1024)S(1)}, u32[]{:S(2)}) copy-start(f32[1536]{0:T(1024)S(1)} %add_rsqrt_fusion) | copy-start | bytes 18436
  183.5 337.9 %copy-start.23 = (s32[4,1536]{1,0:T(4,128)}, s32[4,1536]{1,0:T(4,128)S(1)}, u32[]{:S(2)}) copy-start(s32[4,1536]{1,0:T(4,128)S(1)} %select_bitcast_fusion) | copy-start | bytes 73732
  188.7 18.3 %copy-start.29 = (f32[2048]{0:T(1024)}, f32[2048]{0:T(1024)S(1)}, u32[]{:S(2)}) copy-start(f32[2048]{0:T(1024)S(1)} %get-tuple-element.121) | copy-start | bytes 24580
  188.7 113.1 %copy-start.25 = (f32[2048]{0:T(1024)}, f32[2048]{0:T(1024)S(1)}, u32[]{:S(2)}) copy-start(f32[2048]{0:T(1024)S(1)} %get-tuple-element.120) | copy-start | bytes 24580
  232.6 26.1 %copy-start.2 = (f32[512]{0:T(512)}, f32[512]{0:T(512)S(1)}, u32[]{:S(2)}) copy-start(f32[512]{0:T(512)S(1)} %get-tuple-element.130) | copy-start | bytes 6148
  232.6 26.1 %copy-start.4 = (f32[512]{0:T(512)}, f32[512]{0:T(512)S(1)}, u32[]{:S(2)}) copy-start(f32[512]{0:T(512)S(1)} %get-tuple-element.131) | copy-start | bytes 6148
  258.7 1.1 copy-start
  301.8 1.7 copy-start.8
  301.8 107.6 %copy-start.33 = (f32[384]{0:T(512)}, f32[384]{0:T(512)S(1)}, u32[]{:S(2)}) copy-start(f32[384]{0:T(512)S(1)} %add_rsqrt_fusion.3) | copy-start | bytes 4612
  409.4 32.1 %copy-start.11 = (bf16[1536,2048]{1,0:T(8,128)(2,1)S(1)}, bf16[1536,2048]{1,0:T(8,128)(2,1)}, u32[]{:S(2)}) copy-start(bf16[1536,2048]{1,0:T(8,128)(2,1)} %shard_map.286) | copy-start | bytes 18874372
  409.5 45.8 %collective-permute-start.2 = (bf16[384,2048]{1,0:T(8,128)(2,1)}, bf16[384,2048]{1,0:T(8,128)(2,1)}, u32[]{:S(2)}, u32[]{:S(2)}) collective-permute-start(bf16[384,2048]{1,0:T(8,128)(2,1)} %collective-permute-done), channel_id=1, source_target_pairs={{0,1},{1,2},{2,3},{4,5},{5,6},{6,7},{8,9},{9,10},{10,11},{12,13},{... | collective-permute-start | bytes 4718600 | tf_op jit(solution)/shard_map/ppermute | solution.py:373
  412.7 42.5 %collective-permute-start.3 = (bf16[384,2048]{1,0:T(8,128)(2,1)}, bf16[384,2048]{1,0:T(8,128)(2,1)S(1)}, u32[]{:S(2)}, u32[]{:S(2)}) collective-permute-start(bf16[384,2048]{1,0:T(8,128)(2,1)} %collective-permute-done.1), channel_id=1, source_target_pairs={{1,0},{2,1},{3,2},{5,4},{6,5},{7,6},{9,8},{10,9},{11,10},{13,12},{... | collective-permute-start | bytes 4718600 | tf_op jit(solution)/shard_map/ppermute | solution.py:374
  452.8 2.5 copy-start.20
  452.8 4.7 copy-start.27
  455.3 56.5 %collective-permute-start.4 = (bf16[384,2048]{1,0:T(8,128)(2,1)}, bf16[384,2048]{1,0:T(8,128)(2,1)}, u32[]{:S(2)}, u32[]{:S(2)}) collective-permute-start(bf16[384,2048]{1,0:T(8,128)(2,1)} %collective-permute-done.2), channel_id=1, source_target_pairs={{0,1},{1,2},{2,3},{4,5},{5,6},{6,7},{8,9},{9,10},{10,11},{12,13},{... | collective-permute-start | bytes 4718600 | tf_op jit(solution)/shard_map/ppermute | solution.py:373
  457.5 62.3 %collective-permute-start.5 = (bf16[384,2048]{1,0:T(8,128)(2,1)S(1)}, bf16[384,2048]{1,0:T(8,128)(2,1)}, u32[]{:S(2)}, u32[]{:S(2)}) collective-permute-start(bf16[384,2048]{1,0:T(8,128)(2,1)S(1)} %collective-permute-done.3), channel_id=1, source_target_pairs={{1,0},{2,1},{3,2},{5,4},{6,5},{7,6},{9,8},{10,9},{11,10},{13,12},{... | collective-permute-start | bytes 4718600 | tf_op jit(solution)/shard_map/ppermute | solution.py:374
  638.1 25.7 %copy-start.24 = (s32[4,1536]{1,0:T(4,128)S(1)}, s32[4,1536]{1,0:T(4,128)}, u32[]{:S(2)}) copy-start(s32[4,1536]{1,0:T(4,128)} %copy-done.23) | copy-start | bytes 73732
  667.5 189.1 %all-to-all-start = ((f32[4,4,384]{2,0,1:T(4,128)}), f32[4,4,384]{2,0,1:T(4,128)S(1)}, u32[]{:S(2)}, u32[]{:S(2)}) async-start(f32[4,4,384]{2,0,1:T(4,128)} %bitcast.20), calls=%async_computation.1 | async-start | bytes 49152 | tf_op jit(solution)/shard_map/all_to_all | solution.py:525
  672.1 620.5 %reduce-scatter.11.cloned.1.call-start = ((), (), s32[]{:S(2)}) async-start(), calls=%async_computation.13 | async-start | bytes 2359296 | tf_op jit(solution)/shard_map/reduce_scatter | solution.py:549
  742.7 113.9 %copy-start.21 = (f32[1536,16]{0,1:T(8,128)S(1)}, f32[1536,16]{0,1:T(8,128)}, u32[]{:S(2)}) copy-start(f32[1536,16]{0,1:T(8,128)} %copy-done.20) | copy-start | bytes 294916
  742.7 113.9 %copy-start.26 = (f32[2048]{0:T(1024)S(1)}, f32[2048]{0:T(1024)}, u32[]{:S(2)}) copy-start(f32[2048]{0:T(1024)} %copy-done.25) | copy-start | bytes 24580
  742.7 113.9 %copy-start.34 = (f32[384]{0:T(512)S(1)}, f32[384]{0:T(512)}, u32[]{:S(2)}) copy-start(f32[384]{0:T(512)} %copy-done.33) | copy-start | bytes 4612
  856.6 6.0 copy-start.9
  860.9 1.7 copy-start.12
  866.2 89.2 %copy-start.19 = (bf16[1536,512]{1,0:T(8,128)(2,1)S(1)}, bf16[1536,512]{1,0:T(8,128)(2,1)}, u32[]{:S(2)}) copy-start(bf16[1536,512]{1,0:T(8,128)(2,1)} %get-tuple-element.40.x) | copy-start | bytes 4718596
  962.9 8.2 copy-start.1
  971.1 27.4 %copy-start.3 = (f32[512]{0:T(512)S(1)}, f32[512]{0:T(512)}, u32[]{:S(2)}) copy-start(f32[512]{0:T(512)} %copy-done.2) | copy-start | bytes 6148
  971.1 27.4 %copy-start.5 = (f32[512]{0:T(512)S(1)}, f32[512]{0:T(512)}, u32[]{:S(2)}) copy-start(f32[512]{0:T(512)} %copy-done.4) | copy-start | bytes 6148
  971.1 27.4 %copy-start.31 = (f32[1536]{0:T(1024)S(1)}, f32[1536]{0:T(1024)}, u32[]{:S(2)}) copy-start(f32[1536]{0:T(1024)} %get-tuple-element.134) | copy-start | bytes 18436
  971.1 27.4 %copy-start.32 = (f32[1536]{0:T(1024)S(1)}, f32[1536]{0:T(1024)}, u32[]{:S(2)}) copy-start(f32[1536]{0:T(1024)} %get-tuple-element.135) | copy-start | bytes 18436
  998.5 6.1 copy-start.6
  1015.2 288.0 %reduce-scatter.9.cloned.1.call-start = ((), (), s32[]{:S(2)}) async-start(), calls=%async_computation.12 | async-start | bytes 7667712 | tf_op jit(solution)/shard_map/reduce_scatter | solution.py:580
  1015.5 5.5 copy-start.7
  1015.5 5.5 copy-start.38
  1021.0 17.3 %copy-start.17 = (bf16[1536,512]{1,0:T(8,128)(2,1)}, bf16[1536,512]{1,0:T(8,128)(2,1)S(1)}, u32[]{:S(2)}) copy-start(bf16[1536,512]{1,0:T(8,128)(2,1)S(1)} %get-tuple-element.144) | copy-start | bytes 4718596
  1021.0 17.3 %copy-start.18 = (bf16[1536,512]{1,0:T(8,128)(2,1)}, bf16[1536,512]{1,0:T(8,128)(2,1)S(1)}, u32[]{:S(2)}) copy-start(bf16[1536,512]{1,0:T(8,128)(2,1)S(1)} %get-tuple-element.145) | copy-start | bytes 4718596
  1021.0 19.9 %copy-start.13 = (bf16[384,2048]{1,0:T(8,128)(2,1)S(1)}, bf16[384,2048]{1,0:T(8,128)(2,1)}, u32[]{:S(2)}) copy-start(bf16[384,2048]{1,0:T(8,128)(2,1)} %multiply_convert_fusion.6.x) | copy-start | bytes 4718596
  1021.0 22.2 %copy-start.30 = (f32[2048]{0:T(1024)S(1)}, f32[2048]{0:T(1024)}, u32[]{:S(2)}) copy-start(f32[2048]{0:T(1024)} %copy-done.29) | copy-start | bytes 24580
  1041.6 1.0 copy-start.16
  1043.2 15.5 copy-start.14
  1043.2 15.5 copy-start.15
  1070.8 0.7 copy-start.28
  1070.8 270.0 %reduce-scatter.7.cloned.1.call-start = ((), (), s32[]{:S(2)}) async-start(), calls=%async_computation.11 | async-start | bytes 7864320 | tf_op jit(solution)/shard_map/reduce_scatter | solution.py:536
  1097.6 332.5 %reduce-scatter.13.cloned.1.call-start = ((), (), s32[]{:S(2)}) async-start(), calls=%async_computation.14 | async-start | bytes 18874368 | tf_op jit(solution)/shard_map/reduce_scatter | solution.py:517
  1098.4 451.3 %reduce-scatter.15.cloned.1.call-start = ((), (), s32[]{:S(2)}) async-start(), calls=%async_computation.15 | async-start | bytes 18874368 | tf_op jit(solution)/shard_map/reduce_scatter | solution.py:520
  1099.1 569.9 %reduce-scatter.17.cloned.1.call-start = ((), (), s32[]{:S(2)}) async-start(), calls=%async_computation.16 | async-start | bytes 18874368 | tf_op jit(solution)/shard_map/reduce_scatter | solution.py:511
  1292.5 48.3 %copy-start.10 = (f32[384,2048]{1,0:T(8,128)S(1)}, f32[384,2048]{1,0:T(8,128)}, u32[]{:S(2)}) copy-start(f32[384,2048]{1,0:T(8,128)} %copy-done.8) | copy-start | bytes 9437188
  1292.6 9.9 collective-permute-start.6
Sparse Core Ops, SparseCore 0:
  61.9 84.1 all-gather.4
  148.0 89.8 all-gather.6
  239.8 89.8 all-gather.8
  331.5 89.8 all-gather.10
  1015.4 41.7 reduce-scatter.10
  1070.9 64.7 reduce-scatter.8
  1138.0 157.0 reduce-scatter.6
  1298.8 131.2 reduce-scatter.12
  1433.7 115.9 reduce-scatter.14
  1553.1 115.9 reduce-scatter.16

commit v2 on v1

--- a/solution.py
+++ b/solution.py
@@ -439,13 +439,15 @@
     small = jnp.pad(small, ((0, 0), (0, SMALL - small.shape[1])))
     shard = jnp.stack([query_weight, key_weight, value_weight], axis=1)
     shard = shard.reshape(-1, 3, ways, cols).transpose(2, 0, 1, 3).reshape(ways, -1, 3 * cols)
-    rest = jnp.concatenate([out_weight, small], axis=1)
-    shard = jnp.concatenate([shard, jnp.broadcast_to(rest[None], (ways,) + rest.shape)], axis=2)
+    shard = jnp.concatenate([shard, jnp.broadcast_to(small[None], (ways,) + small.shape)], axis=2)
     shard = exchange_z(shard.reshape(-1, shard.shape[-1]), ways, 1)
     dense = lax.all_gather(shard, "dp", axis=0, tiled=True)
     qkv_weight = dense[:, : 3 * cols]
-    out_full = dense[:, 3 * cols : 3 * cols + width]
-    small = dense[:, 3 * cols + width :]
+    small = dense[:, 3 * cols :]
+    shard, out_weight, gate_weight, up_weight, down_weight = lax.optimization_barrier(
+        (shard, out_weight, gate_weight, up_weight, down_weight)
+    )
+    out_full = lax.all_gather(out_weight, BOTH, axis=0, tiled=True)
     attend_gain = small[:, 0].astype(F32)
     mix_gain = small[:, 3].astype(F32)
     router_full = small[:, 4 : 4 + EXPERTS]
@@ -530,11 +532,11 @@
     part = cross_rows(
         pick.reshape(experts_here * CAP, GTOK), grad_in.reshape(experts_here * CAP, width)
     ).astype(BF16)
+    part, out_down = lax.optimization_barrier((part, out_down))
     grad_routed = rs_z(part, ways, 6).astype(F32)
     spread = jnp.where(chosen, my_weight.T[:, None, :], 0.0).astype(BF16).reshape(experts_here * CAP, GTOK)
     part = cross_rows(spread, expert_out.reshape(experts_here * CAP, width)).astype(BF16)
     moe = lax.psum_scatter(part, "expert", scatter_dimension=0, tiled=True)
-    output = (resid + moe.astype(F32)).astype(BF16)
 
     router = lax.dynamic_slice_in_dim(router_all, first_row, tok_dev, axis=0)
     grad_logits = (router * (route_grad - jnp.sum(router * route_grad, axis=-1, keepdims=True))).astype(BF16)
@@ -543,12 +545,14 @@
     grad_mix_gain = jnp.sum(grad_mix * mix_unit, axis=0)
     grad_resid = cotangent.astype(F32) + norm_back(grad_mix, mix_unit, mix_inverse, mix_gain)
     grad_branch = grad_resid.astype(BF16)
+    grad_branch, out_gate = lax.optimization_barrier((grad_branch, out_gate))
     branch_all = ag_z(grad_branch, ways, 7)
     grad_heads = by_transpose(branch_all, out_mine).astype(BF16)
     grad_out_w = cross_rows(mixed_heads, branch_all).astype(BF16)
     out_out = lax.psum_scatter(grad_out_w, "dp", scatter_dimension=0, tiled=True)
     out_out = lax.ppermute(out_out, BOTH, row_moves(ways, lax.axis_size("dp"))).astype(F32)
 
+    grad_heads, out_up = lax.optimization_barrier((grad_heads, out_up))
     dq, dk, dv = attend_back(order, q_rot, k_rot, v_b, lse, grad_heads, cos, sin)
     q_unit = qkv[:, :cols] * inv_q
     k_unit = qkv[:, cols : 2 * cols] * inv_k
@@ -563,7 +567,9 @@
     grad_qkv = jnp.concatenate([grad_q, grad_k, dv], axis=1)
     grad_normed_part = by_transpose(grad_qkv, qkv_weight)
     grad_attend_gain = jnp.sum(grad_normed_part * (token_f * inverse_in), axis=0)
-    grad_normed = rs_z(grad_normed_part.astype(BF16), ways, 9).astype(F32)
+    part, moe = lax.optimization_barrier((grad_normed_part.astype(BF16), moe))
+    output = (resid + moe.astype(F32)).astype(BF16)
+    grad_normed = rs_z(part, ways, 9).astype(F32)
     own_inverse = lax.dynamic_slice_in_dim(inverse_in, first_row, tok_dev, axis=0)
     input_grad = grad_resid + norm_back(grad_normed, own_f * own_inverse, own_inverse, attend_gain)
 

time: 1690 us -> 1430 us (0.85)
  waiting for transfers between devices: 320 us -> 38.2 us
  Pallas kernels: 785 us -> 825 us
    pallas_call x3, Pallas kernels: 298 us -> 438 us  [ag_z(): pl.pallas_call(functools.partial(ag_kernel, n, rows), out_shape=jax.Shape...]
    reduce_scatter x1, waiting for transfers between devices: 116 us -> 0.02 us  [body(): lax.psum_scatter(grad_up_w, 'dp', scatter_dimension=1, tiled=True)]
    reduce_scatter x1, waiting for transfers between devices: 115 us -> 0.01 us  [body(): lax.psum_scatter(grad_down, 'dp', scatter_dimension=1, tiled=True)]
    reduce_scatter x1, waiting for transfers between devices: 82.9 us -> 0.02 us  [body(): lax.psum_scatter(grad_gate_w, 'dp', scatter_dimension=1, tiled=True)]
    pallas_call x2, Pallas kernels: 307 us -> 230 us  [rs_z(): pl.pallas_call(functools.partial(rs_kernel, n, rows, C, depth), out_shape...]
    ppermute x3, waiting for transfers between devices: 0.01 us -> 28.5 us  [hops(): lax.ppermute(up[-1], 'expert', [(i, i + 1) for i in range(ways - 1)])]
    pallas_call x2, Pallas kernels: 75.8 us -> 49.6 us  [exchange_z(): pl.pallas_call(functools.partial(exchange_kernel, n, x.shape[0] // n), ou...]
  transfers between devices with their start and end apart: 18 -> 19, of which waited for: 4 -> 4; matrix products, arithmetic and copies ran while one was open for 23% -> 35% of each run, Pallas kernels for 37% -> 54%
where the time goes in v2:
time: 1430 us
  Pallas kernels  825 us (58%)
  matrix products  401 us (28%)
  other arithmetic  66.8 us (5%)
  local copies, waits for them, and re-layouts  50 us (3%)
  waiting for transfers between devices  38.2 us (3%)
  starting transfers between devices  29.3 us (2%)
  between operations  15.2 us (1%)
    pallas_call x3, Pallas kernels, ag_z(): pl.pallas_call(functools.partial(ag_kernel, n, rows), out_shape=jax.Shape...  438 us
    pallas_call x2, Pallas kernels, rs_z(): pl.pallas_call(functools.partial(rs_kernel, n, rows, C, depth), out_shape...  230 us
    dot_general x5, matrix products, cross_rows(): lax.dot_general(left, right, (((0,), (0,)), ((), ())), preferred_element_...  74.3 us
    pallas_call x2, Pallas kernels, exchange_z(): pl.pallas_call(functools.partial(exchange_kernel, n, x.shape[0] // n), ou...  49.6 us
    pallas_call x1, Pallas kernels, a2a_z(): pl.pallas_call(functools.partial(a2a_kernel, n, rows, cols), out_shape=ja...  36 us
    dot_general x1, matrix products, body(): jnp.einsum('esd,efd->esf', grad_eo, down_full, preferred_element_type=F32)  33.5 us
    dot_general x4, matrix products, plain(): lax.dot_general(left, right, (((1,), (0,)), ((), ())), preferred_element_...  29.9 us
  transfers between devices with their start and end apart: 19, of which 4 were waited for; matrix products, arithmetic and copies ran while one was open for 35% of the time, Pallas kernels for 54%

profile of v2, /device:TPU:10, one launch (start us, length us, event | category | flops | bytes accessed | tf_op | source)
XLA Modules:
  0.0 1425.3 jit_solution(16115245719011160268)
XLA Ops:
  13.5 1.8 pad_maximum_fusion.3
  16.5 22.1 %shard_map.282 = bf16[256,1664]{1,0:T(8,128)(2,1)} custom-call(bf16[256,1664]{1,0:T(8,128)(2,1)} %pad_maximum_fusion.4.x), custom_call_target="tpu_custom_call" | custom-call | tf_op jit(solution)/shard_map/pallas_call | solution.py:341
  41.5 144.2 %shard_map.281 = bf16[1536,2048]{1,0:T(8,128)(2,1)} custom-call(bf16[384,2048]{1,0:T(8,128)(2,1)} %x.7), custom_call_target="tpu_custom_call" | custom-call | tf_op jit(solution)/shard_map/pallas_call | solution.py:240
  185.7 3.0 collective-permute-start
  188.6 4.2 collective-permute-start.1
  193.4 4.6 fusion.7
  200.8 2.8 fusion.43
  204.1 1.8 convert_reduce_fusion
  205.9 16.6 %fusion.24 = f32[1536,1536]{0,1:T(8,128)} fusion(bf16[2048,1664]{1,0:T(8,128)(2,1)} %all-gather.6.cloned.1.call-done, bf16[1536,2048]{1,0:T(8,128)(2,1)} %shard_map.281, f32[2048]{0:T(1024)S(1)} %get-tuple-element.151, f32[1536]{0:T(1024)S(1)} %add_rsqrt_fusion), kind=kOutput, calls=%fused_computation.48 | convolution fusion | flops 9676259328 | bytes 22034432 | tf_op jit(solution)/shard_map/dot_general | solution.py:45
  222.4 10.1 copy.174.q_pre.k_pre.v_pre
  232.5 3.5 bitcast_reduce_fusion
  236.6 8.3 shard_map.283
  248.6 26.3 %shard_map.284 = (bf16[1536,512]{1,0:T(8,128)(2,1)S(1)}, bf16[1536,512]{1,0:T(8,128)(2,1)}, bf16[1536,512]{1,0:T(8,128)(2,1)}, bf16[1536,512]{1,0:T(8,128)(2,1)}, f32[1536,512]{1,0:T(8,128)}) custom-call(s32[12]{0:T(128)S(1)} %select_reduce_fusion.3.order, f32[1536,1536]{1,0:T(8,128)} %copy.174.q_pre.k_pre.v_pre, f32[1536,1536]{1,0:T(8,128)} %copy.174.q_pre.k_pre.v_pre, ...), custom_call_target="tpu_custom_call" | custom-call | tf_op jit(solution)/shard_map/pallas_call | solution.py:107
  276.2 36.0 %shard_map.285 = bf16[384,2048]{1,0:T(8,128)(2,1)} custom-call(bf16[1536,512]{1,0:T(8,128)(2,1)} %get-tuple-element.52.x), custom_call_target="tpu_custom_call" | custom-call | tf_op jit(solution)/shard_map/pallas_call | solution.py:314
  312.2 8.9 multiply_reduce_fusion.7
  321.2 1.6 copy-done.8
  324.3 104.1 %shard_map.286 = bf16[1536,2048]{1,0:T(8,128)(2,1)} custom-call(bf16[384,2048]{1,0:T(8,128)(2,1)} %multiply_convert_fusion.6.x), custom_call_target="tpu_custom_call" | custom-call | tf_op jit(solution)/shard_map/pallas_call | solution.py:240
  428.5 3.3 collective-permute-start.2
  431.7 3.2 collective-permute-start.3
  434.9 24.7 %fusion.18 = bf16[4,768,2048]{2,1,0:T(8,128)(2,1)} fusion(s32[4,1536]{1,0:T(4,128)S(1)} %select_bitcast_fusion, bf16[1536,2048]{1,0:T(8,128)(2,1)} %shard_map.286), kind=kOutput, calls=%fused_computation.40 | convolution fusion | flops 19338362880 | bytes 18898944 | tf_op jit(solution)/shard_map/est,td->esd/dot_general | solution.py:501
  459.6 5.7 collective-permute-done.2
  465.3 3.0 collective-permute-done.3
  468.3 3.6 collective-permute-start.4
  471.9 2.9 fusion.59
  475.5 2.4 select_reduce_fusion
  477.9 2.5 collective-permute-start.5
  480.4 22.8 %collective-permute-done.4 = bf16[384,2048]{1,0:T(8,128)(2,1)S(1)} collective-permute-done((bf16[384,2048]{1,0:T(8,128)(2,1)S(1)}, bf16[384,2048]{1,0:T(8,128)(2,1)S(1)}, u32[]{:S(2)}, u32[]{:S(2)}) %collective-permute-start.4) | collective-permute-done | bytes 1572896 | tf_op jit(solution)/shard_map/ppermute | solution.py:373
  508.3 4.0 collective-permute-done.5
  512.5 24.6 %multiply_convert_fusion = (bf16[4,768,2048]{2,1,0:T(8,128)(2,1)}, f32[4,768,2048]{2,1,0:T(8,128)}) fusion(f32[4,768]{1,0:T(4,128)S(1)} %select_reduce_fusion, bf16[2688,2048]{1,0:T(8,128)(2,1)S(1)} %constant_dynamic-update-slice_fusion, s32[]{:T(128)S(6)} %select_n.62, s32[4,1536]{1,0:T(4,128)S(1)} %select_bitcast_fusion), kind=kOutput, calls=%fused_computation.2 | convolution fusion | flops 19344654336 | bytes 44077060 | tf_op jit(solution)/shard_map/est,td->esd/dot_general | solution.py:509
  537.1 22.5 %fusion.60 = f32[4,768,1024]{2,1,0:T(8,128)} fusion(bf16[4,768,2048]{2,1,0:T(8,128)(2,1)} %fusion.18, bf16[4,2048,1024]{2,1,0:T(8,128)(2,1)} %all-gather.10.cloned.1.call-done), kind=kOutput, calls=%fused_computation.159 | convolution fusion | flops 12884901888 | bytes 41943040 | tf_op jit(solution)/shard_map/esd,edf->esf/dot_general | solution.py:504
  559.6 26.8 %multiply_convert_fusion.3 = (bf16[4,768,1024]{2,1,0:T(8,128)(2,1)}, f32[4,768,1024]{2,1,0:T(8,128)}) fusion(f32[4,768,1024]{2,1,0:T(8,128)} %fusion.60, bf16[4,768,2048]{2,1,0:T(8,128)(2,1)} %fusion.18, bf16[4,2048,1024]{2,1,0:T(8,128)(2,1)} %all-gather.12.cloned.1.call-done), kind=kOutput, calls=%fused_computation.24 | convolution fusion | flops 12903776256 | bytes 60817408 | tf_op jit(solution)/shard_map/esd,edf->esf/dot_general | solution.py:505
  586.4 22.3 %convolution_convert_fusion.2 = bf16[4,1024,2048]{2,1,0:T(8,128)(2,1)} fusion(bf16[4,768,1024]{2,1,0:T(8,128)(2,1)} %get-tuple-element.75, bf16[4,768,2048]{2,1,0:T(8,128)(2,1)} %get-tuple-element.67), kind=kOutput, calls=%fused_computation.16 | convolution fusion | flops 12893290496 | bytes 35651584 | tf_op jit(solution)/shard_map/esf,esd->efd/dot_general | solution.py:511
  608.8 33.5 %multiply_convert_fusion.1 = (bf16[4,768,1024]{2,1,0:T(8,128)(2,1)}, bf16[4,768,1024]{2,1,0:T(8,128)(2,1)}) fusion(f32[4,768,1024]{2,1,0:T(8,128)} %fusion.60, f32[4,768,1024]{2,1,0:T(8,128)} %get-tuple-element.187, bf16[4,768,2048]{2,1,0:T(8,128)(2,1)} %get-tuple-element.67, bf16[4,1024,2048]{2,1,0:T(8,128)(2,1)} %all-gather.14.cloned.1.call-done), kind=kOutput, calls=%fused_computation.22 | convolution fusion | flops 12925796352 | bytes 67108864 | tf_op jit(solution)/shard_map/esd,efd->esf/dot_general | solution.py:514
  642.3 20.4 %convolution_convert_fusion.1 = bf16[4,2048,1024]{2,1,0:T(8,128)(2,1)} fusion(bf16[4,768,2048]{2,1,0:T(8,128)(2,1)} %fusion.18, bf16[4,768,1024]{2,1,0:T(8,128)(2,1)} %get-tuple-element.71), kind=kOutput, calls=%fused_computation.15 | convolution fusion | flops 12893290496 | bytes 35651584 | tf_op jit(solution)/shard_map/esd,esf->edf/dot_general | solution.py:517
  662.7 20.0 %convolution_convert_fusion = bf16[4,2048,1024]{2,1,0:T(8,128)(2,1)} fusion(bf16[4,768,2048]{2,1,0:T(8,128)(2,1)} %fusion.18, bf16[4,768,1024]{2,1,0:T(8,128)(2,1)} %get-tuple-element.72), kind=kOutput, calls=%fused_computation.14 | convolution fusion | flops 12893290496 | bytes 35651584 | tf_op jit(solution)/shard_map/esd,esf->edf/dot_general | solution.py:520
  682.8 26.0 %multiply_reduce_fusion = (f32[4,768]{1,0:T(4,128)S(1)}, bf16[4,768,2048]{2,1,0:T(8,128)(2,1)}) fusion(f32[4,768,2048]{2,1,0:T(8,128)} %get-tuple-element.185, bf16[4,768,1024]{2,1,0:T(8,128)(2,1)} %get-tuple-element.75, bf16[4,1024,2048]{2,1,0:T(8,128)(2,1)} %all-gather.14.cloned.1.call-done), kind=kOutput, calls=%fused_computation | convolution fusion | flops 12910064640 | bytes 60829696 | tf_op jit(solution)/shard_map/esf,efd->esd/dot_general | solution.py:524
  708.9 3.7 select_reduce_fusion.1
  712.5 4.5 all-to-all-start
  717.1 26.3 %bitcast_convert_fusion = bf16[1536,2048]{1,0:T(8,128)(2,1)} fusion(bf16[4,768,2048]{2,1,0:T(8,128)(2,1)} %get-tuple-element.189, f32[4,1536]{1,0:T(4,128)S(1)} %copy-done.26, s32[4,1536]{1,0:T(4,128)S(1)} %copy-done.22), kind=kOutput, calls=%fused_computation.20 | convolution fusion | flops 19339935744 | bytes 18923520 | tf_op jit(solution)/shard_map/dot_general | solution.py:37
  743.5 24.0 %fusion.61 = f32[4,768,2048]{2,1,0:T(8,128)} fusion(bf16[4,768,1024]{2,1,0:T(8,128)(2,1)} %get-tuple-element.71, bf16[4,2048,1024]{2,1,0:T(8,128)(2,1)} %all-gather.10.cloned.1.call-done), kind=kOutput, calls=%fused_computation.160 | convolution fusion | flops 12884901888 | bytes 48234496 | tf_op jit(solution)/shard_map/esf,edf->esd/dot_general | solution.py:529
  767.5 25.0 %add_convert_fusion.8 = bf16[4,768,2048]{2,1,0:T(8,128)(2,1)} fusion(f32[4,768,2048]{2,1,0:T(8,128)} %fusion.61, bf16[4,768,1024]{2,1,0:T(8,128)(2,1)} %get-tuple-element.72, bf16[4,2048,1024]{2,1,0:T(8,128)(2,1)} %all-gather.12.cloned.1.call-done), kind=kOutput, calls=%fused_computation.1.clone.clone.clone.clone.2 | convolution fusion | flops 12897484800 | bytes 60817408 | tf_op jit(solution)/shard_map/esf,edf->esd/dot_general | solution.py:530
  792.4 24.5 %bitcast_convert_fusion.1.part = bf16[1536,2048]{1,0:T(8,128)(2,1)} fusion(s32[4,1536]{1,0:T(4,128)S(1)} %copy-done.22, bf16[4,768,2048]{2,1,0:T(8,128)(2,1)} %add_convert_fusion.8), kind=kOutput, calls=%fused_computation.21 | convolution fusion | flops 19335217152 | bytes 18898944 | tf_op jit(solution)/shard_map/dot_general | solution.py:37
  818.4 4.1 convert_element_type.200
  822.5 115.2 %shard_map.287 = bf16[384,2048]{1,0:T(8,128)(2,1)} custom-call(bf16[1536,2048]{1,0:T(8,128)(2,1)} %bitcast_convert_fusion.1.part), custom_call_target="tpu_custom_call" | custom-call | tf_op jit(solution)/shard_map/pallas_call | solution.py:293
  937.8 4.2 convert_element_type.206
  942.0 2.6 multiply_reduce_fusion.1
  944.7 1.6 copy-done.12
  946.3 3.6 fusion.58.x
  949.9 189.7 %shard_map.288 = bf16[1536,2048]{1,0:T(8,128)(2,1)} custom-call(bf16[384,2048]{1,0:T(8,128)(2,1)} %fusion.58.x), custom_call_target="tpu_custom_call" | custom-call | tf_op jit(solution)/shard_map/pallas_call | solution.py:240
  1139.6 4.2 convert_element_type.208
  1143.9 8.2 convolution_convert_fusion.6.grad_mixed
  1152.0 27.6 %shard_map.289 = (f32[1536,512]{1,0:T(8,128)}, f32[1536,512]{1,0:T(8,128)}, bf16[1536,512]{1,0:T(8,128)(2,1)S(1)}) custom-call(s32[12]{0:T(128)S(1)} %select_reduce_fusion.3.order, bf16[1536,512]{1,0:T(8,128)(2,1)S(1)} %copy-done.1, bf16[1536,512]{1,0:T(8,128)(2,1)} %get-tuple-element.55.k_rot, bf16[1536,512]{1,0:T(8,128)(2,1)} %get-tuple-element.56.v_in, ...), custom_call_target="tpu_custom_call" | custom-call | tf_op jit(solution)/shard_map/pallas_call | solution.py:164
  1179.8 4.3 multiply_reduce_fusion.2
  1184.7 9.1 shard_map.290
  1194.7 7.4 convolution_convert_fusion.5
  1202.1 6.6 multiply_convert_fusion.5
  1208.8 16.4 %fusion.6 = (bf16[2048]{0:T(1024)(128)(2,1)S(1)}, bf16[1536,2048]{1,0:T(8,128)(2,1)}) fusion(bf16[1536,2048]{1,0:T(8,128)(2,1)} %shard_map.281, f32[1536]{0:T(1024)S(1)} %copy-done.36, bf16[2048,1664]{1,0:T(8,128)(2,1)} %all-gather.6.cloned.1.call-done, bf16[1536,512]{1,0:T(8,128)(2,1)S(1)} %copy-done.7, bf16[1536,512]{1,0:T(8,128)(2,1)} %get-tuple-element.169, ...), kind=kOutput, calls=%fused_computation.18 | convolution fusion | flops 9693558784 | bytes 23603200 | tf_op jit(solution)/shard_map/dot_general | solution.py:41
  1228.0 15.7 %convolution_convert_fusion.3 = bf16[2048,1536]{1,0:T(8,128)(2,1)} fusion(bf16[1536,512]{1,0:T(8,128)(2,1)S(1)} %copy-done.7, bf16[1536,512]{1,0:T(8,128)(2,1)} %get-tuple-element.169, bf16[1536,512]{1,0:T(8,128)(2,1)} %copy-done.17, bf16[1536,2048]{1,0:T(8,128)(2,1)} %shard_map.281, f32[2048]{0:T(1024)S(1)} %copy-done.28, f32[1536]{0:T(1024)S(1)} %copy-done.36), kind=kOutput, calls=%fused_computation.38 | convolution fusion | flops 9693560832 | bytes 17315840 | tf_op jit(solution)/shard_map/dot_general | solution.py:37
  1243.8 12.1 concatenate.36
  1256.0 114.6 %shard_map.291 = bf16[384,2048]{1,0:T(8,128)(2,1)} custom-call(bf16[1536,2048]{1,0:T(8,128)(2,1)} %get-tuple-element.84.part), custom_call_target="tpu_custom_call" | custom-call | tf_op jit(solution)/shard_map/pallas_call | solution.py:293
  1370.6 2.6 fusion.32
  1373.3 4.6 collective-permute-start.6
  1377.9 6.1 fusion.35
  1384.9 27.4 %shard_map.292 = bf16[256,1664]{1,0:T(8,128)(2,1)} custom-call(bf16[256,1664]{1,0:T(8,128)(2,1)} %reduce-scatter.15.cloned.1.call-done.x), custom_call_target="tpu_custom_call" | custom-call | tf_op jit(solution)/shard_map/pallas_call | solution.py:341
  (197 shorter events, 40.0 us)
Async XLA Ops:
  7.2 196.9 %all-gather.6.cloned.1.call-start = ((), (), s32[]{:S(2)}) async-start(), calls=%async_computation.7 | async-start | bytes 7667712 | tf_op jit(solution)/shard_map/all_gather | solution.py:444
  38.7 273.5 %all-gather.8.cloned.1.call-start = ((), (), s32[]{:S(2)}) async-start(), calls=%async_computation.8 | async-start | bytes 8650752 | tf_op jit(solution)/shard_map/all_gather | solution.py:450
  39.5 497.6 %all-gather.10.cloned.1.call-start = ((), (), s32[]{:S(2)}) async-start(), calls=%async_computation.9 | async-start | bytes 18874368 | tf_op jit(solution)/shard_map/all_gather | solution.py:458
  40.2 152.6 %copy-start.37 = (s32[1,1536]{1,0:T(1,128)S(1)}, s32[1,1536]{1,0:T(1,128)}, u32[]{:S(2)}) copy-start(s32[1,1536]{1,0:T(1,128)} %param.32) | copy-start | bytes 18436
  40.2 152.7 %copy-start.34 = (s32[1,1536]{1,0:T(1,128)S(1)}, s32[1,1536]{1,0:T(1,128)}, u32[]{:S(2)}) copy-start(s32[1,1536]{1,0:T(1,128)} %param.33) | copy-start | bytes 18436
  40.2 152.9 %copy-start.38 = (s32[1,1536]{1,0:T(1,128)S(1)}, s32[1,1536]{1,0:T(1,128)}, u32[]{:S(2)}) copy-start(s32[1,1536]{1,0:T(1,128)} %param.34) | copy-start | bytes 18436
  40.2 153.1 %copy-start.33 = (s32[1,1536,8]{1,2,0:T(8,128)S(1)}, s32[1,1536,8]{1,2,0:T(8,128)}, u32[]{:S(2)}) copy-start(s32[1,1536,8]{1,2,0:T(8,128)} %param.35) | copy-start | bytes 147460
  40.3 519.4 %all-gather.12.cloned.1.call-start = ((), (), s32[]{:S(2)}) async-start(), calls=%async_computation.10 | async-start | bytes 18874368 | tf_op jit(solution)/shard_map/all_gather | solution.py:459
  40.8 567.9 %all-gather.14.cloned.1.call-start = ((), (), s32[]{:S(2)}) async-start(), calls=%async_computation.11 | async-start | bytes 18874368 | tf_op jit(solution)/shard_map/all_gather | solution.py:460
  41.4 776.9 %reduce-scatter.7.cloned.1.call-start = ((), (), s32[]{:S(2)}) async-start(), calls=%async_computation.12 | async-start | bytes 18874368 | tf_op jit(solution)/shard_map/reduce_scatter | solution.py:513
  185.7 242.8 %collective-permute-start = (bf16[384,2048]{1,0:T(8,128)(2,1)}, bf16[384,2048]{1,0:T(8,128)(2,1)}, u32[]{:S(2)}, u32[]{:S(2)}) collective-permute-start(bf16[384,2048]{1,0:T(8,128)(2,1)} %param.19), channel_id=1, source_target_pairs={{0,1},{1,2},{2,3},{4,5},{5,6},{6,7},{8,9},{9,10},{10,11},{12,13},{... | collective-permute-start | bytes 4718600 | tf_op jit(solution)/shard_map/ppermute | solution.py:373
  188.6 239.8 %collective-permute-start.1 = (bf16[384,2048]{1,0:T(8,128)(2,1)}, bf16[384,2048]{1,0:T(8,128)(2,1)}, u32[]{:S(2)}, u32[]{:S(2)}) collective-permute-start(bf16[384,2048]{1,0:T(8,128)(2,1)} %param.19), channel_id=1, source_target_pairs={{1,0},{2,1},{3,2},{5,4},{6,5},{7,6},{9,8},{10,9},{11,10},{13,12},{... | collective-permute-start | bytes 4718600 | tf_op jit(solution)/shard_map/ppermute | solution.py:374
  198.1 24.3 %copy-start.35 = (f32[1536]{0:T(1024)}, f32[1536]{0:T(1024)S(1)}, u32[]{:S(2)}) copy-start(f32[1536]{0:T(1024)S(1)} %add_rsqrt_fusion) | copy-start | bytes 18436
  200.7 311.7 %copy-start.21 = (s32[4,1536]{1,0:T(4,128)}, s32[4,1536]{1,0:T(4,128)S(1)}, u32[]{:S(2)}) copy-start(s32[4,1536]{1,0:T(4,128)S(1)} %select_bitcast_fusion) | copy-start | bytes 73732
  205.8 16.6 %copy-start.27 = (f32[2048]{0:T(1024)}, f32[2048]{0:T(1024)S(1)}, u32[]{:S(2)}) copy-start(f32[2048]{0:T(1024)S(1)} %get-tuple-element.151) | copy-start | bytes 24580
  205.8 115.3 %copy-start.23 = (f32[2048]{0:T(1024)}, f32[2048]{0:T(1024)S(1)}, u32[]{:S(2)}) copy-start(f32[2048]{0:T(1024)S(1)} %get-tuple-element.150) | copy-start | bytes 24580
  248.6 26.3 %copy-start.2 = (f32[512]{0:T(512)}, f32[512]{0:T(512)S(1)}, u32[]{:S(2)}) copy-start(f32[512]{0:T(512)S(1)} %get-tuple-element.154) | copy-start | bytes 6148
  248.6 26.3 %copy-start.4 = (f32[512]{0:T(512)}, f32[512]{0:T(512)S(1)}, u32[]{:S(2)}) copy-start(f32[512]{0:T(512)S(1)} %get-tuple-element.155) | copy-start | bytes 6148
  275.0 1.3 copy-start
  321.2 1.7 copy-start.8
  321.2 107.2 %copy-start.31 = (f32[384]{0:T(512)}, f32[384]{0:T(512)S(1)}, u32[]{:S(2)}) copy-start(f32[384]{0:T(512)S(1)} %add_rsqrt_fusion.3) | copy-start | bytes 4612
  428.4 43.5 %copy-start.11 = (bf16[1536,2048]{1,0:T(8,128)(2,1)S(1)}, bf16[1536,2048]{1,0:T(8,128)(2,1)}, u32[]{:S(2)}) copy-start(bf16[1536,2048]{1,0:T(8,128)(2,1)} %shard_map.286) | copy-start | bytes 18874372
  428.5 36.8 %collective-permute-start.2 = (bf16[384,2048]{1,0:T(8,128)(2,1)}, bf16[384,2048]{1,0:T(8,128)(2,1)S(1)}, u32[]{:S(2)}, u32[]{:S(2)}) collective-permute-start(bf16[384,2048]{1,0:T(8,128)(2,1)} %collective-permute-done), channel_id=1, source_target_pairs={{0,1},{1,2},{2,3},{4,5},{5,6},{6,7},{8,9},{9,10},{10,11},{12,13},{... | collective-permute-start | bytes 4718600 | tf_op jit(solution)/shard_map/ppermute | solution.py:373
  431.7 36.6 %collective-permute-start.3 = (bf16[384,2048]{1,0:T(8,128)(2,1)}, bf16[384,2048]{1,0:T(8,128)(2,1)S(1)}, u32[]{:S(2)}, u32[]{:S(2)}) collective-permute-start(bf16[384,2048]{1,0:T(8,128)(2,1)} %collective-permute-done.1), channel_id=1, source_target_pairs={{1,0},{2,1},{3,2},{5,4},{6,5},{7,6},{9,8},{10,9},{11,10},{13,12},{... | collective-permute-start | bytes 4718600 | tf_op jit(solution)/shard_map/ppermute | solution.py:374
  468.3 34.9 %collective-permute-start.4 = (bf16[384,2048]{1,0:T(8,128)(2,1)S(1)}, bf16[384,2048]{1,0:T(8,128)(2,1)S(1)}, u32[]{:S(2)}, u32[]{:S(2)}) collective-permute-start(bf16[384,2048]{1,0:T(8,128)(2,1)S(1)} %collective-permute-done.2), channel_id=1, source_target_pairs={{0,1},{1,2},{2,3},{4,5},{5,6},{6,7},{8,9},{9,10},{10,11},{12,13},{... | collective-permute-start | bytes 4718600 | tf_op jit(solution)/shard_map/ppermute | solution.py:373
  474.9 0.6 copy-start.19
  475.5 31.1 %copy-start.25 = (f32[4,1536]{1,0:T(4,128)}, f32[4,1536]{1,0:T(4,128)S(1)}, u32[]{:S(2)}) copy-start(f32[4,1536]{1,0:T(4,128)S(1)} %dynamic-slice_bitcast_fusion) | copy-start | bytes 73732
  477.9 34.4 %collective-permute-start.5 = (bf16[384,2048]{1,0:T(8,128)(2,1)S(1)}, bf16[384,2048]{1,0:T(8,128)(2,1)S(1)}, u32[]{:S(2)}, u32[]{:S(2)}) collective-permute-start(bf16[384,2048]{1,0:T(8,128)(2,1)S(1)} %collective-permute-done.3), channel_id=1, source_target_pairs={{1,0},{2,1},{3,2},{5,4},{6,5},{7,6},{9,8},{10,9},{11,10},{13,12},{... | collective-permute-start | bytes 4718600 | tf_op jit(solution)/shard_map/ppermute | solution.py:374
  608.7 329.0 %reduce-scatter.9.cloned.1.call-start = ((), (), s32[]{:S(2)}) async-start(), calls=%async_computation.13 | async-start | bytes 18874368 | tf_op jit(solution)/shard_map/reduce_scatter | solution.py:519
  662.7 476.9 %reduce-scatter.11.cloned.1.call-start = ((), (), s32[]{:S(2)}) async-start(), calls=%async_computation.14 | async-start | bytes 18874368 | tf_op jit(solution)/shard_map/reduce_scatter | solution.py:522
  682.8 26.1 %copy-start.22 = (s32[4,1536]{1,0:T(4,128)S(1)}, s32[4,1536]{1,0:T(4,128)}, u32[]{:S(2)}) copy-start(s32[4,1536]{1,0:T(4,128)} %copy-done.21) | copy-start | bytes 73732
  682.8 34.3 %copy-start.26 = (f32[4,1536]{1,0:T(4,128)S(1)}, f32[4,1536]{1,0:T(4,128)}, u32[]{:S(2)}) copy-start(f32[4,1536]{1,0:T(4,128)} %copy-done.25) | copy-start | bytes 73732
  712.5 104.4 %all-to-all-start = ((f32[4,4,384]{2,0,1:T(4,128)}), f32[4,4,384]{2,0,1:T(4,128)S(1)}, u32[]{:S(2)}, u32[]{:S(2)}) async-start(f32[4,4,384]{2,0,1:T(4,128)} %bitcast.19), calls=%async_computation.1 | async-start | bytes 49152 | tf_op jit(solution)/shard_map/all_to_all | solution.py:527
  717.0 538.9 %reduce-scatter.13.cloned.1.call-start = ((), (), s32[]{:S(2)}) async-start(), calls=%async_computation.15 | async-start | bytes 7864320 | tf_op jit(solution)/shard_map/reduce_scatter | solution.py:539
  743.4 629.9 %reduce-scatter.17.cloned.1.call-start = ((), (), s32[]{:S(2)}) async-start(), calls=%async_computation.17 | async-start | bytes 2359296 | tf_op jit(solution)/shard_map/reduce_scatter | solution.py:552
  792.4 24.5 %copy-start.20 = (f32[1536,16]{0,1:T(8,128)S(1)}, f32[1536,16]{0,1:T(8,128)}, u32[]{:S(2)}) copy-start(f32[1536,16]{0,1:T(8,128)} %copy-done.19) | copy-start | bytes 294916
  792.4 24.6 %copy-start.13 = (bf16[384,2048]{1,0:T(8,128)(2,1)S(1)}, bf16[384,2048]{1,0:T(8,128)(2,1)}, u32[]{:S(2)}) copy-start(bf16[384,2048]{1,0:T(8,128)(2,1)} %multiply_convert_fusion.6.x) | copy-start | bytes 4718596
  822.5 119.5 %copy-start.24 = (f32[2048]{0:T(1024)S(1)}, f32[2048]{0:T(1024)}, u32[]{:S(2)}) copy-start(f32[2048]{0:T(1024)} %copy-done.23) | copy-start | bytes 24580
  822.5 119.5 %copy-start.32 = (f32[384]{0:T(512)S(1)}, f32[384]{0:T(512)}, u32[]{:S(2)}) copy-start(f32[384]{0:T(512)} %copy-done.31) | copy-start | bytes 4612
  937.7 4.3 copy-start.14
  937.8 4.2 copy-start.9
  944.6 1.7 copy-start.12
  1139.6 40.1 %slice-start = ((s8[9437184]{0:T(1024)(128)(4,1)}), s8[4194304]{0:T(1024)(128)(4,1)S(1)}, s32[]{:S(2)}) async-start(s8[9437184]{0:T(1024)(128)(4,1)} %bitcast.121), calls=%async_computation.18 | async-start | bytes 8388608
  1143.9 8.2 copy-start.1
  1143.9 35.8 %slice-start.1 = ((s8[9437184]{0:T(1024)(128)(4,1)}), s8[4194304]{0:T(1024)(128)(4,1)S(1)}, s32[]{:S(2)}) async-start(s8[9437184]{0:T(1024)(128)(4,1)} %bitcast.121), calls=%async_computation.19 | async-start | bytes 8388608
  1143.9 35.8 %slice-start.2 = ((s8[9437184]{0:T(1024)(128)(4,1)}), s8[1048576]{0:T(1024)(128)(4,1)S(1)}, s32[]{:S(2)}) async-start(s8[9437184]{0:T(1024)(128)(4,1)} %bitcast.121), calls=%async_computation.20 | async-start | bytes 2097152
  1152.0 27.7 %copy-start.3 = (f32[512]{0:T(512)S(1)}, f32[512]{0:T(512)}, u32[]{:S(2)}) copy-start(f32[512]{0:T(512)} %copy-done.2) | copy-start | bytes 6148
  1152.0 27.7 %copy-start.5 = (f32[512]{0:T(512)S(1)}, f32[512]{0:T(512)}, u32[]{:S(2)}) copy-start(f32[512]{0:T(512)} %copy-done.4) | copy-start | bytes 6148
  1152.0 27.7 %copy-start.29 = (f32[1536]{0:T(1024)S(1)}, f32[1536]{0:T(1024)}, u32[]{:S(2)}) copy-start(f32[1536]{0:T(1024)} %get-tuple-element.158) | copy-start | bytes 18436
  1152.0 27.7 %copy-start.30 = (f32[1536]{0:T(1024)S(1)}, f32[1536]{0:T(1024)}, u32[]{:S(2)}) copy-start(f32[1536]{0:T(1024)} %get-tuple-element.159) | copy-start | bytes 18436
  1179.7 4.4 copy-start.6
  1179.8 14.9 %copy-start.18 = (bf16[1536,512]{1,0:T(8,128)(2,1)S(1)}, bf16[1536,512]{1,0:T(8,128)(2,1)}, u32[]{:S(2)}) copy-start(bf16[1536,512]{1,0:T(8,128)(2,1)} %get-tuple-element.52.x) | copy-start | bytes 4718596
  1202.1 6.7 copy-start.7
  1202.1 6.7 copy-start.36
  1208.7 16.5 %copy-start.17 = (bf16[1536,512]{1,0:T(8,128)(2,1)}, bf16[1536,512]{1,0:T(8,128)(2,1)S(1)}, u32[]{:S(2)}) copy-start(bf16[1536,512]{1,0:T(8,128)(2,1)S(1)} %get-tuple-element.168) | copy-start | bytes 4718596
  1208.8 176.1 %reduce-scatter.15.cloned.1.call-start = ((), (), s32[]{:S(2)}) async-start(), calls=%async_computation.16 | async-start | bytes 7667712 | tf_op jit(solution)/shard_map/reduce_scatter | solution.py:586
  1208.8 19.2 %copy-start.28 = (f32[2048]{0:T(1024)S(1)}, f32[2048]{0:T(1024)}, u32[]{:S(2)}) copy-start(f32[2048]{0:T(1024)} %copy-done.27) | copy-start | bytes 24580
  1226.4 1.0 copy-start.16
  1228.0 15.8 %copy-start.15 = (bf16[2048,16]{1,0:T(8,128)(2,1)S(1)}, bf16[2048,16]{1,0:T(8,128)(2,1)}, u32[]{:S(2)}) copy-start(bf16[2048,16]{1,0:T(8,128)(2,1)} %copy.191) | copy-start | bytes 196612
  1255.9 122.0 %copy-start.10 = (f32[384,2048]{1,0:T(8,128)S(1)}, f32[384,2048]{1,0:T(8,128)}, u32[]{:S(2)}) copy-start(f32[384,2048]{1,0:T(8,128)} %copy-done.8) | copy-start | bytes 9437188
  1373.3 10.8 collective-permute-start.6
Sparse Core Ops, SparseCore 0:
  38.8 48.7 all-gather.5
  90.5 86.9 all-gather.7
  179.4 93.3 all-gather.9
  274.5 89.8 all-gather.11
  366.2 89.8 all-gather.13
  608.8 114.7 reduce-scatter.6
  727.2 115.9 reduce-scatter.8
  846.8 115.9 reduce-scatter.10
  965.1 158.9 reduce-scatter.12
  1208.9 40.9 reduce-scatter.16
  1256.0 63.6 reduce-scatter.14

commit v3 on v2

--- a/solution.py
+++ b/solution.py
@@ -17,6 +17,8 @@
 CLEN = 128
 BLOCKS = GTOK // CLEN
 TILE = 256
+ROWS = 768
+FTILE = 256
 EPS = 1e-05
 BOTH = ("dp", "expert")
 F32 = jnp.float32
@@ -180,119 +182,368 @@
     )(order, q_rot, k_rot, v_in, lse, grad_mixed, cos, sin)
 
 
-ANY=pl.BlockSpec(memory_space=pl.ANY); VM=pl.BlockSpec(memory_space=pltpu.VMEM)
-
-def peer(i): return {"expert": i}
+ANY = pl.BlockSpec(memory_space=pl.ANY)
+VM = pl.BlockSpec(memory_space=pltpu.VMEM)
+DMA = pltpu.SemaphoreType.DMA
+
+
+def params(cid, mib=60):
+    return pltpu.CompilerParams(collective_id=cid, has_side_effects=True, vmem_limit_bytes=mib * 2**20)
+
+
+def peer(i):
+    return {"expert": i}
+
+
+def remote(src, dst, send_sem, recv_sem, to):
+    return pltpu.make_async_remote_copy(
+        src_ref=src, dst_ref=dst, send_sem=send_sem, recv_sem=recv_sem, device_id=peer(to), device_id_type=MESH
+    )
+
 
 def greet_line(n):
-    p=lax.axis_index("expert")
-    bar=pltpu.get_barrier_semaphore()
-    @pl.when(p>0)
-    def _(): pl.semaphore_signal(bar,inc=1,device_id=peer(p-1))
-    @pl.when(p<n-1)
-    def _(): pl.semaphore_signal(bar,inc=1,device_id=peer(p+1))
-    pl.semaphore_wait(bar,(p>0).astype(jnp.int32)+(p<n-1).astype(jnp.int32))
+    p = lax.axis_index("expert")
+    bar = pltpu.get_barrier_semaphore()
+
+    @pl.when(p > 0)
+    def _():
+        pl.semaphore_signal(bar, inc=1, device_id=peer(p - 1), device_id_type=MESH)
+
+    @pl.when(p < n - 1)
+    def _():
+        pl.semaphore_signal(bar, inc=1, device_id=peer(p + 1), device_id_type=MESH)
+
+    pl.semaphore_wait(bar, (p > 0).astype(jnp.int32) + (p < n - 1).astype(jnp.int32))
     return p
 
+
 def greet_all(n):
-    p=lax.axis_index("expert")
-    bar=pltpu.get_barrier_semaphore()
-    for s in range(1,n): pl.semaphore_signal(bar,inc=1,device_id=peer(lax.rem(p+s,n)))
-    pl.semaphore_wait(bar,n-1)
+    p = lax.axis_index("expert")
+    bar = pltpu.get_barrier_semaphore()
+    for s in range(1, n):
+        pl.semaphore_signal(bar, inc=1, device_id=peer(lax.rem(p + s, n)), device_id_type=MESH)
+    pl.semaphore_wait(bar, n - 1)
     return p
 
-def params(cid,mb=60): return pltpu.CompilerParams(collective_id=cid,has_side_effects=True,vmem_limit_bytes=mb*2**20)
-
-def ag_kernel(n,rows,x,out,to_right,to_left,recv,local):
-    p=greet_line(n)
-    at=lambda j: out.at[pl.ds(pl.multiple_of(j*rows,rows),rows)]
-    own=pltpu.make_async_copy(x,at(p),local); own.start()
-    def copy(src,j,sems,q):
-        return pltpu.make_async_remote_copy(src_ref=src,dst_ref=at(j),send_sem=sems.at[j],recv_sem=recv.at[j],device_id=peer(q),device_id_type=MESH)
-    right=lambda src,j: copy(src,j,to_right,p+1)
-    left=lambda src,j: copy(src,j,to_left,p-1)
-    @pl.when(p<n-1)
-    def _(): right(x,p).start()
-    @pl.when(p>0)
-    def _(): left(x,p).start()
-    for s in range(1,n):
-        j=p-s
-        @pl.when(j>=0)
+
+class Gather:
+    sems = lambda n: [DMA((n,))] * 3
+
+    def __init__(self, p, n, own, at, sems):
+        self.p, self.n, self.own, self.at = p, n, own, at
+        self.to_right, self.to_left, self.recv = sems
+
+    def right(self, src, j):
+        return remote(src, self.at(j), self.to_right.at[j], self.recv.at[j], self.p + 1)
+
+    def left(self, src, j):
+        return remote(src, self.at(j), self.to_left.at[j], self.recv.at[j], self.p - 1)
+
+    def start(self):
+        @pl.when(self.p < self.n - 1)
         def _():
-            right(at(j),j).wait_recv()
-            @pl.when(p<n-1)
-            def _(): right(at(j),j).start()
-        k=p+s
-        @pl.when(k<n)
+            self.right(self.own, self.p).start()
+
+        @pl.when(self.p > 0)
         def _():
-            left(at(k),k).wait_recv()
-            @pl.when(p>0)
-            def _(): left(at(k),k).start()
+            self.left(self.own, self.p).start()
+
+    def step(self, s, use=None):
+        p, n = self.p, self.n
+        j, k = p - s, p + s
+
+        @pl.when(j >= 0)
+        def _():
+            self.right(self.at(j), j).wait_recv()
+
+            @pl.when(p < n - 1)
+            def _():
+                self.right(self.at(j), j).start()
+
+        @pl.when(k < n)
+        def _():
+            self.left(self.at(k), k).wait_recv()
+
+            @pl.when(p > 0)
+            def _():
+                self.left(self.at(k), k).start()
+
+        if use is not None:
+            for i, here in ((j, j >= 0), (k, k < n)):
+                pl.when(here)(functools.partial(use, i))
+
+    def finish(self):
+        for j in range(self.n):
+
+            @pl.when((j <= self.p) & (self.p < self.n - 1))
+            def _():
+                self.right(self.own, j).wait_send()
+
+            @pl.when((j >= self.p) & (self.p > 0))
+            def _():
+                self.left(self.own, j).wait_send()
+
+
+class Reduce:
+    pieces, depth = 4, 2
+    sems = lambda n: [DMA((n * Reduce.pieces,))] * 4
+    boxes = lambda n, rows, width: [pltpu.VMEM((n * Reduce.pieces, rows // Reduce.pieces, width), BF16)] * 2
+
+    def __init__(self, p, n, rows, part, make, boxes, sems):
+        self.p, self.n, self.rows, self.part, self.make = p, n, rows, part, make
+        self.from_left, self.from_right = boxes
+        self.to_right, self.to_left, self.recv_r, self.recv_l = sems
+        self.order = [(s, c) for s in range(n - 1) for c in range(self.pieces)]
+
+    def at(self, j, c):
+        size = self.rows // self.pieces
+        return self.part.at[pl.ds(pl.multiple_of(j * self.rows + c * size, size), size)]
+
+    def right(self, j, c):
+        i = j * self.pieces + c
+        return remote(self.at(j, c), self.from_left.at[i], self.to_right.at[i], self.recv_r.at[i], self.p + 1)
+
+    def left(self, j, c):
+        i = j * self.pieces + c
+        return remote(self.at(j, c), self.from_right.at[i], self.to_left.at[i], self.recv_l.at[i], self.p - 1)
+
+    def add(self, j, c, box):
+        total = self.at(j, c)[...].astype(F32) + box[j * self.pieces + c].astype(F32)
+        self.at(j, c)[...] = total.astype(BF16)
+
+    def step(self, s):
+        p, n = self.p, self.n
+        j, k = n - 1 - s, s
+        pl.when(j > p)(lambda: self.make(j))
+        pl.when(k < p)(lambda: self.make(k))
+        for c in range(self.pieces):
+            m = s * self.pieces + c
+
+            @pl.when(j > p)
+            def _():
+                @pl.when(p > 0)
+                def _():
+                    self.right(j, c).wait_recv()
+                    self.add(j, c, self.from_left)
+
+                if m >= self.depth:
+                    s0, c0 = self.order[m - self.depth]
+                    self.right(n - 1 - s0, c0).wait_send()
+                self.right(j, c).start()
+
+            @pl.when(k < p)
+            def _():
+                @pl.when(p < n - 1)
+                def _():
+                    self.left(k, c).wait_recv()
+                    self.add(k, c, self.from_right)
+
+                if m >= self.depth:
+                    s0, c0 = self.order[m - self.depth]
+                    self.left(s0, c0).wait_send()
+                self.left(k, c).start()
+
+    def finish(self, out, base=None):
+        p, n, size = self.p, self.n, self.rows // self.pieces
+        self.make(p)
+        for c in range(self.pieces):
+
+            @pl.when(p > 0)
+            def _():
+                self.right(p, c).wait_recv()
+                self.add(p, c, self.from_left)
+
+            @pl.when(p < n - 1)
+            def _():
+                self.left(p, c).wait_recv()
+                self.add(p, c, self.from_right)
+
+            here = pl.ds(c * size, size)
+            if base is None:
+                out[here] = self.at(p, c)[...]
+            else:
+                out[here] = (base[here].astype(F32) + self.at(p, c)[...].astype(F32)).astype(out.dtype)
+        for m, (s, c) in enumerate(self.order):
+            pl.when((n - 1 - s > p) & (m >= (n - 1 - p) * self.pieces - self.depth))(
+                lambda s=s, c=c: self.right(n - 1 - s, c).wait_send()
+            )
+            pl.when((s < p) & (m >= p * self.pieces - self.depth))(lambda s=s, c=c: self.left(s, c).wait_send())
+
+
+def rows_of(ref, rows):
+    return lambda j: ref.at[pl.ds(pl.multiple_of(j * rows, rows), rows)]
+
+
+def ag_kernel(n, rows, x, out, to_right, to_left, recv, local):
+    p = greet_line(n)
+    at = rows_of(out, rows)
+    own = pltpu.make_async_copy(x, at(p), local)
+    own.start()
+    line = Gather(p, n, x, at, (to_right, to_left, recv))
+    line.start()
+    for s in range(1, n):
+        line.step(s)
     own.wait()
-    for j in range(n):
-        @pl.when((j<=p)&(p<n-1))
-        def _(): right(x,j).wait_send()
-        @pl.when((j>=p)&(p>0))
-        def _(): left(x,j).wait_send()
-
-def ag_z(x,n,cid):
-    rows=x.shape[0]
-    return pl.pallas_call(functools.partial(ag_kernel,n,rows),out_shape=jax.ShapeDtypeStruct((n*rows,)+x.shape[1:],x.dtype),
-        in_specs=[ANY],out_specs=ANY,scratch_shapes=[pltpu.SemaphoreType.DMA((n,))]*3+[pltpu.SemaphoreType.DMA],
-        compiler_params=params(cid))(x)
-
-def rs_kernel(n,rows,C,depth,part,out,from_left,from_right,to_right,to_left,recv_r,recv_l):
-    p=greet_line(n)
-    size=rows//C
-    def at(j,c): return part.at[pl.ds(pl.multiple_of(j*rows+c*size,size),size)]
-    def right(j,c): return pltpu.make_async_remote_copy(src_ref=at(j,c),dst_ref=from_left.at[j*C+c],send_sem=to_right.at[j*C+c],recv_sem=recv_r.at[j*C+c],device_id=peer(p+1),device_id_type=MESH)
-    def left(j,c): return pltpu.make_async_remote_copy(src_ref=at(j,c),dst_ref=from_right.at[j*C+c],send_sem=to_left.at[j*C+c],recv_sem=recv_l.at[j*C+c],device_id=peer(p-1),device_id_type=MESH)
-    def add(j,c,buf):
-        at(j,c)[...]=(at(j,c)[...].astype(F32)+buf[j*C+c].astype(F32)).astype(BF16)
-    order=[(s,c) for s in range(n-1) for c in range(C)]
-    for m,(s,c) in enumerate(order):
-        j=n-1-s
-        @pl.when(j>p)
-        def _():
-            @pl.when(p>0)
-            def _():
-                right(j,c).wait_recv(); add(j,c,from_left)
-            if m>=depth:
-                s0,c0=order[m-depth]
-                right(n-1-s0,c0).wait_send()
-            right(j,c).start()
-        k=s
-        @pl.when(k<p)
-        def _():
-            @pl.when(p<n-1)
-            def _():
-                left(k,c).wait_recv(); add(k,c,from_right)
-            if m>=depth:
-                s0,c0=order[m-depth]
-                left(s0,c0).wait_send()
-            left(k,c).start()
-    for c in range(C):
-        @pl.when(p>0)
-        def _():
-            right(p,c).wait_recv(); add(p,c,from_left)
-        @pl.when(p<n-1)
-        def _():
-            left(p,c).wait_recv(); add(p,c,from_right)
-        out[pl.ds(c*size,size)]=at(p,c)[...]
-    for m,(s,c) in enumerate(order):
-        j=n-1-s
-        last_r=(n-1-p)*C
-        @pl.when((j>p)&(m>=last_r-depth))
-        def _(): right(j,c).wait_send()
-        last_l=p*C
-        @pl.when((s<p)&(m>=last_l-depth))
-        def _(): left(s,c).wait_send()
-
-def rs_z(part,n,cid,C=4,depth=2):
-    rows=part.shape[0]//n; D=part.shape[1]
-    return pl.pallas_call(functools.partial(rs_kernel,n,rows,C,depth),out_shape=jax.ShapeDtypeStruct((rows,D),BF16),
-        in_specs=[VM],out_specs=VM,scratch_shapes=[pltpu.VMEM((n*C,rows//C,D),BF16)]*2+[pltpu.SemaphoreType.DMA((n*C,))]*4,
-        compiler_params=params(cid))(part)
+    line.finish()
+
+
+def ag_z(x, n, cid):
+    rows = x.shape[0]
+    return pl.pallas_call(
+        functools.partial(ag_kernel, n, rows),
+        out_shape=jax.ShapeDtypeStruct((n * rows,) + x.shape[1:], x.dtype),
+        in_specs=[ANY],
+        out_specs=ANY,
+        scratch_shapes=Gather.sems(n) + [DMA],
+        compiler_params=params(cid),
+    )(x)
+
+
+def gather_kernel(n, rows, x, slot, small, grads, logits, rows_out, grads_out, *rest):
+    shards, picked, picked_grads, to_right, to_left, recv, out_sems = rest
+    p = greet_line(n)
+    experts = slot.shape[1]
+    line = Gather(p, n, x, lambda j: shards.at[j], (to_right, to_left, recv))
+    line.start()
+
+    def pick(j, e):
+        places = lax.broadcasted_iota(jnp.int32, (CAP, rows), 0)
+        return (slot[j, e : e + 1] == places).astype(F32).astype(BF16)
+
+    def use(j, block, first=False):
+        logits[pl.ds(pl.multiple_of(j * rows, rows), rows), :] = plain(block[...], small[...])
+        for e in range(experts):
+            new = plain(pick(j, e), block[...])
+            picked[e] = new.astype(BF16) if first else (picked[e].astype(F32) + new).astype(BF16)
+
+    def copy_out(e, src, dst, k):
+        return pltpu.make_async_copy(src.at[e], dst.at[e], out_sems.at[k, e])
+
+    use(p, x, True)
+    for e in range(experts):
+        for j in range(n):
+            new = plain(pick(j, e), grads[j * rows : (j + 1) * rows])
+            picked_grads[e] = new.astype(BF16) if j == 0 else (picked_grads[e].astype(F32) + new).astype(BF16)
+        copy_out(e, picked_grads, grads_out, 1).start()
+    for s in range(1, n):
+        line.step(s, lambda j: use(j, shards.at[j]))
+    for e in range(experts):
+        copy_out(e, picked, rows_out, 0).start()
+    for e in range(experts):
+        copy_out(e, picked, rows_out, 0).wait()
+        copy_out(e, picked_grads, grads_out, 1).wait()
+    line.finish()
+
+
+def gather_rows(x, slot, small, grads, n, cid):
+    rows, width = x.shape
+    experts = slot.shape[1]
+    wide = (experts, CAP, width)
+    return pl.pallas_call(
+        functools.partial(gather_kernel, n, rows),
+        out_shape=[
+            jax.ShapeDtypeStruct((n * rows, small.shape[1]), F32),
+            jax.ShapeDtypeStruct(wide, BF16),
+            jax.ShapeDtypeStruct(wide, BF16),
+        ],
+        in_specs=[VM] * 4,
+        out_specs=[VM, ANY, ANY],
+        scratch_shapes=[pltpu.VMEM((n, rows, width), BF16), pltpu.VMEM(wide, BF16), pltpu.VMEM(wide, BF16)]
+        + Gather.sems(n)
+        + [DMA((2, experts))],
+        compiler_params=params(cid),
+    )(x, slot, small, grads)
+
+
+def rs_kernel(n, rows, part, out, left_box, right_box, *sems):
+    p = greet_line(n)
+    line = Reduce(p, n, rows, part, lambda j: None, (left_box, right_box), sems)
+    for s in range(n - 1):
+        line.step(s)
+    line.finish(out)
+
+
+def rs_z(part, n, cid):
+    rows, width = part.shape[0] // n, part.shape[1]
+    return pl.pallas_call(
+        functools.partial(rs_kernel, n, rows),
+        out_shape=jax.ShapeDtypeStruct((rows, width), BF16),
+        in_specs=[VM],
+        out_specs=VM,
+        scratch_shapes=Reduce.boxes(n, rows, width) + Reduce.sems(n),
+        compiler_params=params(cid),
+    )(part)
+
+
+def combine(part, rows, slot, weight, blocks):
+    def make(j):
+        total, e = None, 0
+        for block in blocks:
+            for i in range(block.shape[0]):
+                places = lax.broadcasted_iota(jnp.int32, (rows, CAP), 1)
+                chosen = slot[j, :, e : e + 1] == places
+                scale = 1.0 if weight is None else weight[j, :, e : e + 1]
+                term = plain(jnp.where(chosen, scale, 0.0).astype(BF16), block[i])
+                total = term if total is None else total + term
+                e += 1
+        part[pl.ds(pl.multiple_of(j * rows, rows), rows), :] = total.astype(BF16)
+
+    return make
+
+
+def combine_kernel(n, rows, slot, low, high, out, part, left_box, right_box, *sems):
+    p = greet_line(n)
+    make = combine(part, rows, slot, None, (low, high))
+    line = Reduce(p, n, rows, part, make, (left_box, right_box), sems)
+    for s in range(n - 1):
+        line.step(s)
+    line.finish(out)
+
+
+def combine_z(slot, low, high, n, cid):
+    rows, width = slot.shape[1], low.shape[2]
+    return pl.pallas_call(
+        functools.partial(combine_kernel, n, rows),
+        out_shape=jax.ShapeDtypeStruct((rows, width), BF16),
+        in_specs=[VM] * 3,
+        out_specs=VM,
+        scratch_shapes=[pltpu.VMEM((n * rows, width), BF16)] + Reduce.boxes(n, rows, width) + Reduce.sems(n),
+        compiler_params=params(cid),
+    )(slot, low, high)
+
+
+def both_kernel(n, rows, x, slot, weight, low, high, base, all_out, out, part, left_box, right_box, *sems):
+    p = greet_line(n)
+    at = rows_of(all_out, rows)
+    own = pltpu.make_async_copy(x, at(p), sems[7])
+    own.start()
+    gather = Gather(p, n, x, at, sems[:3])
+    gather.start()
+    make = combine(part, rows, slot, weight, (low, high))
+    line = Reduce(p, n, rows, part, make, (left_box, right_box), sems[3:7])
+    for s in range(n - 1):
+        line.step(s)
+        gather.step(s + 1)
+    line.finish(out, base)
+    own.wait()
+    gather.finish()
+
+
+def gather_and_combine(x, slot, weight, low, high, base, n, cid):
+    rows, width = x.shape
+    return pl.pallas_call(
+        functools.partial(both_kernel, n, rows),
+        out_shape=[jax.ShapeDtypeStruct((n * rows, width), x.dtype), jax.ShapeDtypeStruct((rows, width), BF16)],
+        in_specs=[ANY] + [VM] * 5,
+        out_specs=[ANY, VM],
+        scratch_shapes=[pltpu.VMEM((n * rows, width), BF16)]
+        + Reduce.boxes(n, rows, width)
+        + Gather.sems(n)
+        + Reduce.sems(n)
+        + [DMA],
+        compiler_params=params(cid),
+    )(x, slot, weight, low, high, base)
+
 
 def a2a_kernel(n,rows,cols,x,out,send,recv,local):
     p=greet_all(n)
@@ -312,7 +563,7 @@
 def a2a_z(x,n,cid):
     rows=x.shape[0]//n; cols=x.shape[1]
     return pl.pallas_call(functools.partial(a2a_kernel,n,rows,cols),out_shape=jax.ShapeDtypeStruct((rows,n*cols),x.dtype),
-        in_specs=[ANY],out_specs=ANY,scratch_shapes=[pltpu.SemaphoreType.DMA((n,))]*2+[pltpu.SemaphoreType.DMA],
+        in_specs=[ANY],out_specs=ANY,scratch_shapes=[DMA((n,))]*2+[DMA],
         compiler_params=params(cid))(x)
 
 def exchange_kernel(n, rows, x, out, send, recv, local):
@@ -343,7 +594,7 @@
         out_shape=jax.ShapeDtypeStruct(x.shape, x.dtype),
         in_specs=[ANY],
         out_specs=ANY,
-        scratch_shapes=[pltpu.SemaphoreType.DMA((n,))] * 2 + [pltpu.SemaphoreType.DMA],
+        scratch_shapes=[DMA((n,))] * 2 + [DMA],
         compiler_params=params(cid),
     )(x)
 
@@ -361,7 +612,112 @@
 
 def sum_z(x,n,cid):
     return pl.pallas_call(functools.partial(sum_kernel,n),out_shape=jax.ShapeDtypeStruct(x.shape,x.dtype),in_specs=[VM],out_specs=VM,
-        scratch_shapes=[pltpu.VMEM((n,)+x.shape,x.dtype)]+[pltpu.SemaphoreType.DMA((n,))]*2,compiler_params=params(cid))(x)
+        scratch_shapes=[pltpu.VMEM((n,)+x.shape,x.dtype)]+[DMA((n,))]*2,compiler_params=params(cid))(x)
+
+
+def expert_kernel(
+    slot, weight, x, g, gate, up, down, eo_out, gin_out, route_out, gu_out, gd_out, xt, w_col, both, scaled, eo, gin
+):
+    f = pl.program_id(1)
+    tile = gate.shape[2]
+    chunks = CAP // ROWS
+    tokens = slot.shape[2]
+    x, g = x.at[0], g.at[0]
+
+    def one_hot(start):
+        place = lax.broadcasted_iota(jnp.int32, (ROWS, tokens), 0) + start
+        return slot[0] == place
+
+    @pl.when(f == 0)
+    def _():
+        @pl.loop(0, chunks)
+        def _(c):
+            here = pl.ds(pl.multiple_of(c * ROWS, ROWS), ROWS)
+            chosen = one_hot(c * ROWS)
+            w_col[here, :] = jnp.sum(jnp.where(chosen, weight[0], 0.0), axis=1, keepdims=True)
+            eo[here, :] = jnp.zeros((ROWS, x.shape[1]), F32)
+            gin[here, :] = jnp.zeros((ROWS, x.shape[1]), F32)
+
+        xt[...] = x[...].T
+
+    @pl.loop(0, chunks)
+    def _(c):
+        here = pl.ds(pl.multiple_of(c * ROWS, ROWS), ROWS)
+        a = plain(x[here, :], gate[0])
+        b = plain(x[here, :], up[0])
+        h = by_transpose(g[here, :], down[0]) * w_col[here, :]
+        sig = 1.0 / (1.0 + jnp.exp(-a))
+        silu = a * sig
+        hidden = silu * b
+        gg = (h * b * (sig * (1.0 + a * (1.0 - sig)))).astype(BF16)
+        gu = (h * silu).astype(BF16)
+        both[here, 0:tile] = gg
+        both[here, tile : 2 * tile] = gu
+        scaled[here, :] = (hidden * w_col[here, :]).astype(BF16)
+        eo[here, :] += plain(hidden.astype(BF16), down[0])
+        gin[here, :] += by_transpose(gg, gate[0]) + by_transpose(gu, up[0])
+
+    pieces, rows = gu_out.shape[0], gu_out.shape[2]
+
+    grad_both = plain(xt[...], both[...]).astype(BF16)
+    for c in range(pieces):
+        gu_out[c, 0] = grad_both[c * rows : (c + 1) * rows]
+
+    down_rows = gd_out.shape[2]
+    grad_down = cross_rows(scaled[...], g[...]).astype(BF16)
+    for c in range(gd_out.shape[0]):
+        gd_out[c, 0] = grad_down[c * down_rows : (c + 1) * down_rows]
+
+    @pl.when(f == pl.num_programs(1) - 1)
+    def _():
+        eo_out[0] = eo[...].astype(BF16)
+        gin_out[0] = gin[...].astype(BF16)
+        route = jnp.zeros((1, tokens), F32)
+        for c in range(chunks):
+            here = pl.ds(c * ROWS, ROWS)
+            dots = jnp.sum(eo[here, :].astype(BF16).astype(F32) * g[here, :].astype(F32), axis=1, keepdims=True)
+            route = route + jnp.sum(jnp.where(one_hot(c * ROWS), dots, 0.0), axis=0, keepdims=True)
+        route_out[0] = route
+
+
+def experts(first, count, dp, slot, weight, x, g, gate, up, down):
+    tokens, width = slot.shape[2], x.shape[2]
+    ff = gate.shape[2]
+    steps = ff // FTILE
+    line = pl.BlockSpec((1, 1, tokens), lambda e, f: (first + e, 0, 0))
+    column = pl.BlockSpec((1, width, FTILE), lambda e, f: (first + e, 0, f))
+    row = pl.BlockSpec((1, FTILE, width), lambda e, f: (first + e, f, 0))
+    slots_in = pl.BlockSpec((1, CAP, width), lambda e, f: (first + e, 0, 0), pipeline_mode=pl.Buffered(2))
+    slots_out = pl.BlockSpec((1, CAP, width), lambda e, f: (e, 0, 0), pipeline_mode=pl.Buffered(1))
+    down_rows = ff // dp
+    return pl.pallas_call(
+        expert_kernel,
+        grid=(count, steps),
+        in_specs=[line, line, slots_in, slots_in, column, column, row],
+        out_specs=[
+            slots_out,
+            slots_out,
+            pl.BlockSpec((1, 1, tokens), lambda e, f: (e, 0, 0)),
+            pl.BlockSpec((dp, 1, width // dp, 2 * FTILE), lambda e, f: (0, e, 0, f)),
+            pl.BlockSpec((FTILE // down_rows, 1, down_rows, width), lambda e, f: (f, e, 0, 0)),
+        ],
+        out_shape=[
+            jax.ShapeDtypeStruct((count, CAP, width), BF16),
+            jax.ShapeDtypeStruct((count, CAP, width), BF16),
+            jax.ShapeDtypeStruct((count, 1, tokens), F32),
+            jax.ShapeDtypeStruct((dp, count, width // dp, 2 * ff), BF16),
+            jax.ShapeDtypeStruct((dp, count, down_rows, width), BF16),
+        ],
+        scratch_shapes=[
+            pltpu.VMEM((width, CAP), BF16),
+            pltpu.VMEM((CAP, 1), F32),
+            pltpu.VMEM((CAP, 2 * FTILE), BF16),
+            pltpu.VMEM((CAP, FTILE), BF16),
+            pltpu.VMEM((CAP, width), F32),
+            pltpu.VMEM((CAP, width), F32),
+        ],
+        compiler_params=pltpu.CompilerParams(vmem_limit_bytes=60 * 2**20),
+    )(slot, weight, x, g, gate, up, down)
 
 
 def row_moves(ways, dp):
@@ -473,8 +829,9 @@
     my_hits = lax.dynamic_slice_in_dim(hits, z * experts_here, experts_here, axis=1)
     my_slot = lax.dynamic_slice_in_dim(slot, z * experts_here, experts_here, axis=1)
     my_slot = jnp.where(my_hits & (my_slot < CAP), my_slot, -1)
-    chosen = my_slot.T[:, None, :] == jnp.arange(CAP, dtype=jnp.int32)[None, :, None]
-    pick = chosen.astype(BF16)
+    slot_lines = my_slot.T[:, None, :]
+    slot_shards = my_slot.T.reshape(experts_here, ways, tok_dev).transpose(1, 0, 2)
+    slot_cols = my_slot.reshape(ways, tok_dev, experts_here)
 
     token_f = tokens_all.astype(F32)
     inverse_in = lax.rsqrt(jnp.mean(token_f * token_f, axis=-1, keepdims=True) + EPS)
@@ -482,61 +839,36 @@
     qkv = plain(normed, qkv_weight)
     squares = jnp.sum(jnp.square(qkv[:, : 2 * cols]).reshape(GTOK, 2, cols), axis=-1)
     squares = sum_z(jnp.pad(squares.T, ((0, 6), (0, 0))), ways, 3)
+    up, down, squares = later(sent, squares)
+    sent = hops(up, down, steps[1] - steps[0], ways)
     inv_q = lax.rsqrt(squares[0] / width + EPS)[:, None]
     inv_k = lax.rsqrt(squares[1] / width + EPS)[:, None]
     q_rot, k_rot, v_b, mixed_heads, lse = attend(order, qkv, inv_q, inv_k, gain_q, gain_k, cos, sin)
+    up, down, mixed_heads = later(sent, mixed_heads)
+    grad_all = line_up(*hops(up, down, ways - steps[1], ways), ways)
     mixed = a2a_z(mixed_heads, ways, 4)
     own_f = tokens.astype(F32)
     resid = own_f + plain(mixed, out_full)
     mix_inverse = lax.rsqrt(jnp.mean(resid * resid, axis=-1, keepdims=True) + EPS)
     mix_unit = resid * mix_inverse
     mix = (mix_unit * mix_gain).astype(BF16)
-    mix_all = ag_z(mix, ways, 5)
-    up, down, mix_all = later(sent, mix_all)
-    sent = hops(up, down, steps[1] - steps[0], ways)
-
-    router_all = jax.nn.softmax(plain(mix_all, router_full), axis=-1)
+    logits, inputs, grad_rows = gather_rows(mix, slot_shards, small, grad_all, ways, 5)
+
+    router_all = jax.nn.softmax(logits[:, 4 : 4 + EXPERTS], axis=-1)
     my_weight = lax.dynamic_slice_in_dim(router_all, z * experts_here, experts_here, axis=1)
-    slot_weight = jnp.sum(jnp.where(chosen, my_weight.T[:, None, :], 0.0), axis=-1)
-    inputs = jnp.einsum("est,td->esd", pick, mix_all, preferred_element_type=F32).astype(BF16)
-    up, down, inputs = later(sent, inputs)
-    grad_all = line_up(*hops(up, down, ways - steps[1], ways), ways)
-    gate_pre = jnp.einsum("esd,edf->esf", inputs, gate_full, preferred_element_type=F32)
-    up_pre = jnp.einsum("esd,edf->esf", inputs, up_full, preferred_element_type=F32)
-    sig = jax.nn.sigmoid(gate_pre)
-    silu = gate_pre * sig
-    hidden = (silu * up_pre).astype(BF16)
-    grad_slots = jnp.einsum("est,td->esd", pick, grad_all, preferred_element_type=F32)
-    grad_eo = (grad_slots * slot_weight[:, :, None]).astype(BF16)
-    grad_down = jnp.einsum("esf,esd->efd", hidden, grad_eo, preferred_element_type=F32).astype(BF16)
-    grad_eo, grad_down = lax.optimization_barrier((grad_eo, grad_down))
-    out_down = lax.psum_scatter(grad_down, "dp", scatter_dimension=1, tiled=True).astype(F32)
-    grad_hidden = jnp.einsum("esd,efd->esf", grad_eo, down_full, preferred_element_type=F32)
-    grad_gate = (grad_hidden * up_pre * (sig * (1.0 + gate_pre * (1.0 - sig)))).astype(BF16)
-    grad_up = (grad_hidden * silu).astype(BF16)
-    grad_gate_w = jnp.einsum("esd,esf->edf", inputs, grad_gate, preferred_element_type=F32).astype(BF16)
-    grad_gate, grad_up, grad_gate_w = lax.optimization_barrier((grad_gate, grad_up, grad_gate_w))
-    out_gate = lax.psum_scatter(grad_gate_w, "dp", scatter_dimension=1, tiled=True).astype(F32)
-    grad_up_w = jnp.einsum("esd,esf->edf", inputs, grad_up, preferred_element_type=F32).astype(BF16)
-    grad_gate, grad_up, hidden, grad_up_w = lax.optimization_barrier((grad_gate, grad_up, hidden, grad_up_w))
-    out_up = lax.psum_scatter(grad_up_w, "dp", scatter_dimension=1, tiled=True).astype(F32)
-
-    expert_out = jnp.einsum("esf,efd->esd", hidden, down_full, preferred_element_type=F32).astype(BF16)
-    slot_dots = jnp.sum(grad_slots * expert_out.astype(F32), axis=-1)
-    my_route_grad = jnp.sum(jnp.where(chosen, slot_dots[:, :, None], 0.0), axis=1)
+    weight_lines = my_weight.T[:, None, :]
+    weight_cols = my_weight.reshape(ways, tok_dev, experts_here)
+    half = experts_here // 2
+    work = (half, lax.axis_size("dp"), slot_lines, weight_lines, inputs, grad_rows, gate_full, up_full, down_full)
+    out_low, in_low, route_low, both_low, down_low = experts(0, *work)
+    sum_both_low = lax.psum_scatter(both_low, "dp", scatter_dimension=0, tiled=True)
+    sum_down_low = lax.psum_scatter(down_low, "dp", scatter_dimension=0, tiled=True)
+    out_high, in_high, route_high, both_high, down_high = experts(half, *work)
+    sum_both_high = lax.psum_scatter(both_high, "dp", scatter_dimension=0, tiled=True)
+    sum_down_high = lax.psum_scatter(down_high, "dp", scatter_dimension=0, tiled=True)
+    my_route_grad = jnp.concatenate([route_low, route_high], axis=0)[:, 0]
     route_grad = lax.all_to_all(my_route_grad, "expert", split_axis=1, concat_axis=0, tiled=True).T
-    grad_in = (
-        jnp.einsum("esf,edf->esd", grad_gate, gate_full, preferred_element_type=F32)
-        + jnp.einsum("esf,edf->esd", grad_up, up_full, preferred_element_type=F32)
-    ).astype(BF16)
-    part = cross_rows(
-        pick.reshape(experts_here * CAP, GTOK), grad_in.reshape(experts_here * CAP, width)
-    ).astype(BF16)
-    part, out_down = lax.optimization_barrier((part, out_down))
-    grad_routed = rs_z(part, ways, 6).astype(F32)
-    spread = jnp.where(chosen, my_weight.T[:, None, :], 0.0).astype(BF16).reshape(experts_here * CAP, GTOK)
-    part = cross_rows(spread, expert_out.reshape(experts_here * CAP, width)).astype(BF16)
-    moe = lax.psum_scatter(part, "expert", scatter_dimension=0, tiled=True)
+    grad_routed = combine_z(slot_cols, in_low, in_high, ways, 6).astype(F32)
 
     router = lax.dynamic_slice_in_dim(router_all, first_row, tok_dev, axis=0)
     grad_logits = (router * (route_grad - jnp.sum(router * route_grad, axis=-1, keepdims=True))).astype(BF16)
@@ -545,14 +877,14 @@
     grad_mix_gain = jnp.sum(grad_mix * mix_unit, axis=0)
     grad_resid = cotangent.astype(F32) + norm_back(grad_mix, mix_unit, mix_inverse, mix_gain)
     grad_branch = grad_resid.astype(BF16)
-    grad_branch, out_gate = lax.optimization_barrier((grad_branch, out_gate))
-    branch_all = ag_z(grad_branch, ways, 7)
+    grad_branch, sum_both_low, sum_down_low = lax.optimization_barrier((grad_branch, sum_both_low, sum_down_low))
+    branch_all, output = gather_and_combine(grad_branch, slot_cols, weight_cols, out_low, out_high, resid, ways, 7)
     grad_heads = by_transpose(branch_all, out_mine).astype(BF16)
     grad_out_w = cross_rows(mixed_heads, branch_all).astype(BF16)
     out_out = lax.psum_scatter(grad_out_w, "dp", scatter_dimension=0, tiled=True)
     out_out = lax.ppermute(out_out, BOTH, row_moves(ways, lax.axis_size("dp"))).astype(F32)
 
-    grad_heads, out_up = lax.optimization_barrier((grad_heads, out_up))
+    grad_heads, sum_both_high = lax.optimization_barrier((grad_heads, sum_both_high))
     dq, dk, dv = attend_back(order, q_rot, k_rot, v_b, lse, grad_heads, cos, sin)
     q_unit = qkv[:, :cols] * inv_q
     k_unit = qkv[:, cols : 2 * cols] * inv_k
@@ -567,8 +899,7 @@
     grad_qkv = jnp.concatenate([grad_q, grad_k, dv], axis=1)
     grad_normed_part = by_transpose(grad_qkv, qkv_weight)
     grad_attend_gain = jnp.sum(grad_normed_part * (token_f * inverse_in), axis=0)
-    part, moe = lax.optimization_barrier((grad_normed_part.astype(BF16), moe))
-    output = (resid + moe.astype(F32)).astype(BF16)
+    part, sum_down_high = lax.optimization_barrier((grad_normed_part.astype(BF16), sum_down_high))
     grad_normed = rs_z(part, ways, 9).astype(F32)
     own_inverse = lax.dynamic_slice_in_dim(inverse_in, first_row, tok_dev, axis=0)
     input_grad = grad_resid + norm_back(grad_normed, own_f * own_inverse, own_inverse, attend_gain)
@@ -589,6 +920,11 @@
         grad_qkv_w[:, :, i * cols : (i + 1) * cols].transpose(1, 0, 2).reshape(-1, width).astype(F32)
         for i in range(3)
     ]
+    sums = jnp.concatenate([sum_both_low[0], sum_both_high[0]], axis=0).astype(F32)
+    sums = sums.reshape(sums.shape[:2] + (-1, 2, FTILE))
+    out_gate = sums[:, :, :, 0].reshape(gate_weight.shape)
+    out_up = sums[:, :, :, 1].reshape(gate_weight.shape)
+    out_down = jnp.concatenate([sum_down_low[0], sum_down_high[0]], axis=0).astype(F32)
     packed = jnp.sum(grad_qkv_w[:, :, 3 * cols :].astype(F32), axis=0)
     return (
         output,

time: 1430 us -> 1330 us (0.930)
  matrix products: 401 us -> 75.4 us
  Pallas kernels: 825 us -> 1010 us
  local copies, waits for them, and re-layouts: 50 us -> 115 us
  waiting for transfers between devices: 38.2 us -> 4.27 us
  starting transfers between devices: 29.3 us -> 50.3 us
    pallas_call x2 -> x6, Pallas kernels: 230 us -> 679 us  [the longest x1 175 us: gather_and_combine(): pl.pallas_call(functools.partial(both_kernel, n, rows), out_shape=[jax.Sh...]
    pallas_call x3 -> x1, Pallas kernels: 438 us -> 144 us  [ag_z(): pl.pallas_call(functools.partial(ag_kernel, n, rows), out_shape=jax.Shape...]
    dot_general x11 -> x0, matrix products: 270 us -> none  [the longest x1 33.5 us: body(): jnp.einsum('esd,efd->esf', grad_eo, down_full, preferred_element_type=F32)]
    dot_general x5 -> x3, matrix products: 74.3 us -> 23.3 us  [cross_rows(): lax.dot_general(left, right, (((0,), (0,)), ((), ())), preferred_element_...]
    slice x0 -> x2, local copies, waits for them, and re-layouts: none -> 31.6 us  [the longest x1 29.7 us: body(): out_up = sums[:, :, :, 1].reshape(gate_weight.shape)]
    pallas_call x1, Pallas kernels: 36 us -> 65 us  [a2a_z(): pl.pallas_call(functools.partial(a2a_kernel, n, rows, cols), out_shape=ja...]
    ppermute x3, waiting for transfers between devices: 28.5 us -> 0.01 us  [hops(): lax.ppermute(up[-1], 'expert', [(i, i + 1) for i in range(ways - 1)])]
    all_to_all x1, starting transfers between devices: 4.52 us -> 24.6 us  [body(): lax.all_to_all(my_route_grad, 'expert', split_axis=1, concat_axis=0, tile...]
  transfers between devices with their start and end apart: 19 -> 19, of which waited for: 4 -> 1; matrix products, arithmetic and copies ran while one was open for 35% -> 17% of each run, Pallas kernels for 54% -> 66%
where the time goes in v3:
time: 1330 us
  Pallas kernels  1010 us (76%)
  local copies, waits for them, and re-layouts  115 us (9%)
  matrix products  75.4 us (6%)
  other arithmetic  58.6 us (4%)
  starting transfers between devices  50.3 us (4%)
  between operations  15 us (1%)
    pallas_call x1, Pallas kernels, gather_and_combine(): pl.pallas_call(functools.partial(both_kernel, n, rows), out_shape=[jax.Sh...  175 us
    pallas_call x2, Pallas kernels, experts(): pl.pallas_call(expert_kernel, grid=(count, steps), in_specs=[line, line,...  163 us
    pallas_call x1, Pallas kernels, ag_z(): pl.pallas_call(functools.partial(ag_kernel, n, rows), out_shape=jax.Shape...  144 us
    pallas_call x1, Pallas kernels, combine_z(): pl.pallas_call(functools.partial(combine_kernel, n, rows), out_shape=jax....  134 us
    pallas_call x1, Pallas kernels, rs_z(): pl.pallas_call(functools.partial(rs_kernel, n, rows), out_shape=jax.Shape...  104 us
    pallas_call x1, Pallas kernels, gather_rows(): pl.pallas_call(functools.partial(gather_kernel, n, rows), out_shape=[jax....  103 us
    pallas_call x1, Pallas kernels, a2a_z(): pl.pallas_call(functools.partial(a2a_kernel, n, rows, cols), out_shape=ja...  65 us
    pallas_call x2, Pallas kernels, exchange_z(): pl.pallas_call(functools.partial(exchange_kernel, n, x.shape[0] // n), ou...  45 us
  transfers between devices with their start and end apart: 19, of which 1 were waited for; matrix products, arithmetic and copies ran while one was open for 17% of the time, Pallas kernels for 66%

profile of v3, /device:TPU:10, one launch (start us, length us, event | category | flops | bytes accessed | tf_op | source)
XLA Modules:
  0.0 1326.9 jit_solution(17531856784021240058)
XLA Ops:
  11.9 1.8 pad_maximum_fusion.3
  15.3 22.1 %shard_map.282 = bf16[256,1664]{1,0:T(8,128)(2,1)} custom-call(bf16[256,1664]{1,0:T(8,128)(2,1)} %pad_maximum_fusion.4.x), custom_call_target="tpu_custom_call" | custom-call | tf_op jit(solution)/shard_map/pallas_call | solution.py:592
  40.2 144.2 %shard_map.281 = bf16[1536,2048]{1,0:T(8,128)(2,1)} custom-call(bf16[384,2048]{1,0:T(8,128)(2,1)} %x.7), custom_call_target="tpu_custom_call" | custom-call | tf_op jit(solution)/shard_map/pallas_call | solution.py:392
  184.4 3.0 collective-permute-start
  187.4 4.3 collective-permute-start.1
  192.0 4.7 fusion.4
  196.7 1.8 convert_reduce_fusion
  198.5 15.4 %fusion.9 = f32[1536,1536]{0,1:T(8,128)S(1)} fusion(bf16[2048,1664]{1,0:T(8,128)(2,1)} %all-gather.6.cloned.1.call-done, bf16[1536,2048]{1,0:T(8,128)(2,1)} %shard_map.281, f32[2048]{0:T(1024)S(1)} %get-tuple-element.163, f32[1536]{0:T(1024)S(1)} %add_rsqrt_fusion), kind=kOutput, calls=%fused_computation.16 | convolution fusion | flops 9676259328 | bytes 22034432 | tf_op jit(solution)/shard_map/dot_general | solution.py:47
  213.9 3.6 copy-done.9
  218.8 11.2 shard_map.283
  230.1 2.6 collective-permute-start.2
  232.7 4.9 collective-permute-start.3
  237.8 2.8 fusion.24
  241.1 9.6 copy.174.q_pre.k_pre.v_pre
  252.2 1.3 slice.125
  253.9 25.9 %shard_map.284 = (bf16[1536,512]{1,0:T(8,128)(2,1)S(1)}, bf16[1536,512]{1,0:T(8,128)(2,1)}, bf16[1536,512]{1,0:T(8,128)(2,1)}, bf16[1536,512]{1,0:T(8,128)(2,1)}, f32[1536,512]{1,0:T(8,128)}) custom-call(s32[12]{0:T(128)S(1)} %select_reduce_fusion.1.order, f32[1536,1536]{1,0:T(8,128)} %copy.174.q_pre.k_pre.v_pre, f32[1536,1536]{1,0:T(8,128)} %copy.174.q_pre.k_pre.v_pre, ...), custom_call_target="tpu_custom_call" | custom-call | tf_op jit(solution)/shard_map/pallas_call | solution.py:109
  280.9 1.9 collective-permute-start.4
  284.1 1.6 fusion.5
  286.3 1.9 slice.129.small
  288.2 4.0 collective-permute-start.5
  292.2 65.0 %shard_map.285 = bf16[384,2048]{1,0:T(8,128)(2,1)} custom-call(bf16[1536,512]{1,0:T(8,128)(2,1)} %get-tuple-element.62.x), custom_call_target="tpu_custom_call" | custom-call | tf_op jit(solution)/shard_map/pallas_call | solution.py:565
  357.3 1.6 constant_dynamic-update-slice_fusion.5
  359.0 1.5 constant_dynamic-update-slice_fusion.4
  360.7 1.6 constant_dynamic-update-slice_fusion.2
  362.2 1.5 constant_dynamic-update-slice_fusion.1
  363.7 1.5 constant_dynamic-update-slice_fusion
  365.3 3.3 constant_dynamic-slice_fusion.1.grads
  368.5 6.5 multiply_reduce_fusion.6
  375.1 1.6 copy-done.4
  376.7 1.5 multiply_convert_fusion.2.x
  378.2 103.1 %shard_map.286 = (f32[1536,128]{1,0:T(8,128)}, bf16[4,768,2048]{2,1,0:T(8,128)(2,1)}, bf16[4,768,2048]{2,1,0:T(8,128)(2,1)}) custom-call(bf16[384,2048]{1,0:T(8,128)(2,1)} %multiply_convert_fusion.2.x, s32[4,4,384]{2,1,0:T(4,128)} %bitcast.102, bf16[2048,128]{1,0:T(8,128)(2,1)} %slice.129.small, bf16[1536,2048]{1,0:T(8,128)(2,1)} %constant_dynamic-slice_fusion.1.grads), custom_call_target="tpu_custom_call" | custom-call | tf_op jit(solution)/shard_map/pallas_call | solution.py:442
  481.3 1.4 copy.181
  483.5 81.5 %shard_map.287 = (bf16[2,768,2048]{2,1,0:T(8,128)(2,1)}, bf16[2,768,2048]{2,1,0:T(8,128)(2,1)}, f32[2,1,1536]{2,1,0:T(1,128)}, bf16[8,2,256,2048]{3,2,1,0:T(8,128)(2,1)}, bf16[8,2,128,2048]{3,2,1,0:T(8,128)(2,1)}) custom-call(s32[4,1,1536]{2,1,0:T(1,128)} %broadcast_in_dim.88.slot, f32[4,1,1536]{2,1,0:T(1,128)} %broadcast_in_dim.89.weight, ...), custom_call_target="tpu_custom_call" | custom-call | tf_op jit(solution)/shard_map/pallas_call | solution.py:693
  565.8 81.7 %shard_map.288 = (bf16[2,768,2048]{2,1,0:T(8,128)(2,1)}, bf16[2,768,2048]{2,1,0:T(8,128)(2,1)}, f32[2,1,1536]{2,1,0:T(1,128)}, bf16[8,2,256,2048]{3,2,1,0:T(8,128)(2,1)}, bf16[8,2,128,2048]{3,2,1,0:T(8,128)(2,1)}) custom-call(s32[4,1,1536]{2,1,0:T(1,128)} %broadcast_in_dim.88.slot, f32[4,1,1536]{2,1,0:T(1,128)} %broadcast_in_dim.89.weight, ...), custom_call_target="tpu_custom_call" | custom-call | tf_op jit(solution)/shard_map/pallas_call | solution.py:693
  648.4 1.2 copy.179
  650.3 24.6 %all-to-all-start = ((f32[4,4,384]{2,0,1:T(4,128)}), f32[4,4,384]{2,0,1:T(4,128)S(1)}, u32[]{:S(2)}, u32[]{:S(2)}) async-start(f32[4,4,384]{2,0,1:T(4,128)} %bitcast.36), calls=%async_computation | async-start | bytes 49152 | tf_op jit(solution)/shard_map/all_to_all | solution.py:870
  674.8 1.2 copy.183
  676.0 134.0 %shard_map.289 = bf16[384,2048]{1,0:T(8,128)(2,1)} custom-call(s32[4,384,4]{2,1,0:T(8,128)} %bitcast.89, bf16[2,768,2048]{2,1,0:T(8,128)(2,1)} %get-tuple-element.72.low, bf16[2,768,2048]{2,1,0:T(8,128)(2,1)} %get-tuple-element.73.high), custom_call_target="tpu_custom_call" | custom-call | tf_op jit(solution)/shard_map/pallas_call | solution.py:505
  811.5 4.2 multiply_reduce_fusion
  815.6 1.4 stack.50
  817.5 2.1 fusion.37.x
  819.6 174.8 %shard_map.290 = (bf16[1536,2048]{1,0:T(8,128)(2,1)}, bf16[384,2048]{1,0:T(8,128)(2,1)}) custom-call(bf16[384,2048]{1,0:T(8,128)(2,1)} %fusion.37.x, s32[4,384,4]{2,1,0:T(8,128)} %bitcast.90, f32[4,384,4]{2,1,0:T(8,128)} %bitcast.94, bf16[2,768,2048]{2,1,0:T(8,128)(2,1)} %get-tuple-element.79.low, bf16[2,768,2048]{2,1,0:T(8,128)(2,1)} %get-tuple-element.80.high, ...), custom_call_target="tpu_custom_call" | custom-call | tf_op jit(solution)/shard_map/pallas_call | solution.py:534
  994.4 8.2 convolution_convert_fusion.2.grad_mixed
  1002.7 27.5 %shard_map.291 = (f32[1536,512]{1,0:T(8,128)}, f32[1536,512]{1,0:T(8,128)}, bf16[1536,512]{1,0:T(8,128)(2,1)S(1)}) custom-call(s32[12]{0:T(128)S(1)} %select_reduce_fusion.1.order, bf16[1536,512]{1,0:T(8,128)(2,1)S(1)} %copy-done.1, bf16[1536,512]{1,0:T(8,128)(2,1)} %get-tuple-element.83.k_rot, bf16[1536,512]{1,0:T(8,128)(2,1)} %get-tuple-element.84.v_in, ...), custom_call_target="tpu_custom_call" | custom-call | tf_op jit(solution)/shard_map/pallas_call | solution.py:166
  1030.2 6.1 multiply_reduce_fusion.1
  1037.0 11.2 shard_map.292
  1049.1 7.5 convolution_convert_fusion.1
  1056.6 6.6 multiply_convert_fusion.1
  1063.3 16.3 %fusion.3 = (bf16[2048]{0:T(1024)(128)(2,1)S(1)}, bf16[1536,2048]{1,0:T(8,128)(2,1)}) fusion(bf16[1536,2048]{1,0:T(8,128)(2,1)} %shard_map.281, f32[1536]{0:T(1024)S(1)} %add_rsqrt_fusion, bf16[2048,1664]{1,0:T(8,128)(2,1)} %all-gather.6.cloned.1.call-done, bf16[1536,512]{1,0:T(8,128)(2,1)S(1)} %copy-done.3, bf16[1536,512]{1,0:T(8,128)(2,1)} %get-tuple-element.179, ...), kind=kOutput, calls=%fused_computation.5 | convolution fusion | flops 9693558784 | bytes 23603200 | tf_op jit(solution)/shard_map/dot_general | solution.py:43
  1082.1 15.4 %convolution_convert_fusion = bf16[2048,1536]{1,0:T(8,128)(2,1)} fusion(bf16[1536,512]{1,0:T(8,128)(2,1)S(1)} %copy-done.3, bf16[1536,512]{1,0:T(8,128)(2,1)} %get-tuple-element.179, bf16[1536,512]{1,0:T(8,128)(2,1)} %copy-done.18, bf16[1536,2048]{1,0:T(8,128)(2,1)} %shard_map.281, f32[2048]{0:T(1024)S(1)} %copy-done.24, f32[1536]{0:T(1024)S(1)} %add_rsqrt_fusion), kind=kOutput, calls=%fused_computation.11 | convolution fusion | flops 9693560832 | bytes 17315840 | tf_op jit(solution)/shard_map/dot_general | solution.py:39
  1097.6 12.1 concatenate.51
  1109.8 3.3 concatenate.53
  1113.1 4.8 concatenate.52
  1117.9 9.7 maximum_convert_fusion
  1127.6 29.7 %slice_reduce_fusion = (f32[4,256,4,256]{3,2,1,0:T(4,128)}, f32[4,256,4,256]{3,2,1,0:T(4,128)}) fusion(f32[4,256,4,2,256]{4,3,2,1,0:T(2,128)} %maximum_convert_fusion), kind=kLoop, calls=%fused_computation.21 | loop fusion | bytes 16777216 | tf_op jit(solution)/shard_map/slice | solution.py:926
  1157.3 5.8 reshape_squeeze.14
  1163.1 5.9 reshape_squeeze.15
  1169.0 103.5 %shard_map.293 = bf16[384,2048]{1,0:T(8,128)(2,1)} custom-call(bf16[1536,2048]{1,0:T(8,128)(2,1)} %get-tuple-element.93.part), custom_call_target="tpu_custom_call" | custom-call | tf_op jit(solution)/shard_map/pallas_call | solution.py:468
  1272.5 2.8 fusion.15
  1275.3 4.9 fusion.18
  1280.3 4.6 collective-permute-start.6
  1284.9 3.8 maximum_convert_fusion.1
  1289.9 22.8 %shard_map.294 = bf16[256,1664]{1,0:T(8,128)(2,1)} custom-call(bf16[256,1664]{1,0:T(8,128)(2,1)} %reduce-scatter.15.cloned.1.call-done.x), custom_call_target="tpu_custom_call" | custom-call | tf_op jit(solution)/shard_map/pallas_call | solution.py:592
  1312.8 1.4 convert_bitcast_fusion
  (185 shorter events, 32.4 us)
Async XLA Ops:
  7.2 189.5 %all-gather.6.cloned.1.call-start = ((), (), s32[]{:S(2)}) async-start(), calls=%async_computation.7 | async-start | bytes 7667712 | tf_op jit(solution)/shard_map/all_gather | solution.py:800
  9.9 4.1 copy-start.31
  9.9 4.1 copy-start.32
  9.9 4.1 copy-start.33
  10.0 4.1 copy-start.34
  10.0 4.1 copy-start.35
  37.5 331.1 %all-gather.8.cloned.1.call-start = ((), (), s32[]{:S(2)}) async-start(), calls=%async_computation.8 | async-start | bytes 8650752 | tf_op jit(solution)/shard_map/all_gather | solution.py:806
  38.2 445.2 %all-gather.10.cloned.1.call-start = ((), (), s32[]{:S(2)}) async-start(), calls=%async_computation.9 | async-start | bytes 18874368 | tf_op jit(solution)/shard_map/all_gather | solution.py:814
  39.0 444.5 %all-gather.12.cloned.1.call-start = ((), (), s32[]{:S(2)}) async-start(), calls=%async_computation.10 | async-start | bytes 18874368 | tf_op jit(solution)/shard_map/all_gather | solution.py:815
  39.5 443.9 %all-gather.14.cloned.1.call-start = ((), (), s32[]{:S(2)}) async-start(), calls=%async_computation.11 | async-start | bytes 18874368 | tf_op jit(solution)/shard_map/all_gather | solution.py:816
  40.1 144.3 %copy-start.11 = (bf16[384,2048]{1,0:T(8,128)(2,1)S(1)}, bf16[384,2048]{1,0:T(8,128)(2,1)}, u32[]{:S(2)}) copy-start(bf16[384,2048]{1,0:T(8,128)(2,1)} %param.19) | copy-start | bytes 4718596
  40.1 151.6 %copy-start.29 = (s32[1,1536]{1,0:T(1,128)S(1)}, s32[1,1536]{1,0:T(1,128)}, u32[]{:S(2)}) copy-start(s32[1,1536]{1,0:T(1,128)} %param.32) | copy-start | bytes 18436
  40.1 151.7 %copy-start.26 = (s32[1,1536]{1,0:T(1,128)S(1)}, s32[1,1536]{1,0:T(1,128)}, u32[]{:S(2)}) copy-start(s32[1,1536]{1,0:T(1,128)} %param.33) | copy-start | bytes 18436
  40.2 779.5 %reduce-scatter.9.cloned.1.call-start = ((), (), s32[]{:S(2)}) async-start(), calls=%async_computation.13 | async-start | bytes 9437184 | tf_op jit(solution)/shard_map/reduce_scatter | solution.py:865
  184.4 45.7 %collective-permute-start = (bf16[384,2048]{1,0:T(8,128)(2,1)S(1)}, bf16[384,2048]{1,0:T(8,128)(2,1)}, u32[]{:S(2)}, u32[]{:S(2)}) collective-permute-start(bf16[384,2048]{1,0:T(8,128)(2,1)S(1)} %copy-done.11), channel_id=1, source_target_pairs={{0,1},{1,2},{2,3},{4,5},{5,6},{6,7},{8,9},{9,10},{10,11},{12,13},{... | collective-permute-start | bytes 4718600 | tf_op jit(solution)/shard_map/ppermute | solution.py:729
  187.4 42.7 %collective-permute-start.1 = (bf16[384,2048]{1,0:T(8,128)(2,1)S(1)}, bf16[384,2048]{1,0:T(8,128)(2,1)}, u32[]{:S(2)}, u32[]{:S(2)}) collective-permute-start(bf16[384,2048]{1,0:T(8,128)(2,1)S(1)} %copy-done.11), channel_id=1, source_target_pairs={{1,0},{2,1},{3,2},{5,4},{6,5},{7,6},{9,8},{10,9},{11,10},{13,12},{... | collective-permute-start | bytes 4718600 | tf_op jit(solution)/shard_map/ppermute | solution.py:730
  198.5 15.4 %copy-start.23 = (f32[2048]{0:T(1024)}, f32[2048]{0:T(1024)S(1)}, u32[]{:S(2)}) copy-start(f32[2048]{0:T(1024)S(1)} %get-tuple-element.163) | copy-start | bytes 24580
  213.9 3.6 copy-start.9
  230.1 50.8 %collective-permute-start.2 = (bf16[384,2048]{1,0:T(8,128)(2,1)}, bf16[384,2048]{1,0:T(8,128)(2,1)}, u32[]{:S(2)}, u32[]{:S(2)}) collective-permute-start(bf16[384,2048]{1,0:T(8,128)(2,1)} %collective-permute-done), channel_id=1, source_target_pairs={{0,1},{1,2},{2,3},{4,5},{5,6},{6,7},{8,9},{9,10},{10,11},{12,13},{... | collective-permute-start | bytes 4718600 | tf_op jit(solution)/shard_map/ppermute | solution.py:729
  232.7 48.2 %collective-permute-start.3 = (bf16[384,2048]{1,0:T(8,128)(2,1)}, bf16[384,2048]{1,0:T(8,128)(2,1)}, u32[]{:S(2)}, u32[]{:S(2)}) collective-permute-start(bf16[384,2048]{1,0:T(8,128)(2,1)} %collective-permute-done.1), channel_id=1, source_target_pairs={{1,0},{2,1},{3,2},{5,4},{6,5},{7,6},{9,8},{10,9},{11,10},{13,12},{... | collective-permute-start | bytes 4718600 | tf_op jit(solution)/shard_map/ppermute | solution.py:730
  253.8 29.0 %copy-start.30 = (s32[1,1536]{1,0:T(1,128)S(1)}, s32[1,1536]{1,0:T(1,128)}, u32[]{:S(2)}) copy-start(s32[1,1536]{1,0:T(1,128)} %param.34) | copy-start | bytes 18436
  253.8 29.0 %copy-start.25 = (s32[1,1536,8]{1,2,0:T(8,128)S(1)}, s32[1,1536,8]{1,2,0:T(8,128)}, u32[]{:S(2)}) copy-start(s32[1,1536,8]{1,2,0:T(8,128)} %param.35) | copy-start | bytes 147460
  279.8 1.1 copy-start
  280.9 76.3 %collective-permute-start.4 = (bf16[384,2048]{1,0:T(8,128)(2,1)}, bf16[384,2048]{1,0:T(8,128)(2,1)S(1)}, u32[]{:S(2)}, u32[]{:S(2)}) collective-permute-start(bf16[384,2048]{1,0:T(8,128)(2,1)} %collective-permute-done.2), channel_id=1, source_target_pairs={{0,1},{1,2},{2,3},{4,5},{5,6},{6,7},{8,9},{9,10},{10,11},{12,13},{... | collective-permute-start | bytes 4718600 | tf_op jit(solution)/shard_map/ppermute | solution.py:729
  285.7 71.6 %copy-start.21 = (s32[1536,4]{0,1:T(4,128)}, s32[1536,4]{0,1:T(4,128)S(1)}, u32[]{:S(2)}) copy-start(s32[1536,4]{0,1:T(4,128)S(1)} %and_select_fusion) | copy-start | bytes 73732
  288.2 75.6 %collective-permute-start.5 = (bf16[384,2048]{1,0:T(8,128)(2,1)}, bf16[384,2048]{1,0:T(8,128)(2,1)}, u32[]{:S(2)}, u32[]{:S(2)}) collective-permute-start(bf16[384,2048]{1,0:T(8,128)(2,1)} %collective-permute-done.3), channel_id=1, source_target_pairs={{1,0},{2,1},{3,2},{5,4},{6,5},{7,6},{9,8},{10,9},{11,10},{13,12},{... | collective-permute-start | bytes 4718600 | tf_op jit(solution)/shard_map/ppermute | solution.py:730
  357.3 3.2 copy-start.12
  365.2 3.3 copy-start.14
  375.0 1.6 copy-start.4
  565.0 254.6 %reduce-scatter.7.cloned.1.call-start = ((), (), s32[]{:S(2)}) async-start(), calls=%async_computation.12 | async-start | bytes 18874368 | tf_op jit(solution)/shard_map/reduce_scatter | solution.py:864
  565.8 436.9 %reduce-scatter.11.cloned.1.call-start = ((), (), s32[]{:S(2)}) async-start(), calls=%async_computation.14 | async-start | bytes 18874368 | tf_op jit(solution)/shard_map/reduce_scatter | solution.py:867
  647.6 462.2 %reduce-scatter.13.cloned.1.call-start = ((), (), s32[]{:S(2)}) async-start(), calls=%async_computation.15 | async-start | bytes 9437184 | tf_op jit(solution)/shard_map/reduce_scatter | solution.py:868
  647.6 0.7 copy-start.22
  647.6 1.9 copy-start.27
  647.7 1.9 copy-start.28
  650.3 159.8 %all-to-all-start = ((f32[4,4,384]{2,0,1:T(4,128)}), f32[4,4,384]{2,0,1:T(4,128)S(1)}, u32[]{:S(2)}, u32[]{:S(2)}) async-start(f32[4,4,384]{2,0,1:T(4,128)} %bitcast.36), calls=%async_computation | async-start | bytes 49152 | tf_op jit(solution)/shard_map/all_to_all | solution.py:870
  674.8 605.5 %reduce-scatter.17.cloned.1.call-start = ((), (), s32[]{:S(2)}) async-start(), calls=%async_computation.17 | async-start | bytes 2359296 | tf_op jit(solution)/shard_map/reduce_scatter | solution.py:884
  676.0 134.1 %copy-start.10 = (bf16[384,2048]{1,0:T(8,128)(2,1)S(1)}, bf16[384,2048]{1,0:T(8,128)(2,1)}, u32[]{:S(2)}) copy-start(bf16[384,2048]{1,0:T(8,128)(2,1)} %multiply_convert_fusion.2.x) | copy-start | bytes 4718596
  811.4 6.0 copy-start.5
  811.5 6.0 copy-start.13
  815.6 1.9 copy-start.7
  994.4 8.2 copy-start.1
  1030.2 6.1 copy-start.2
  1030.2 18.9 %copy-start.19 = (bf16[1536,512]{1,0:T(8,128)(2,1)S(1)}, bf16[1536,512]{1,0:T(8,128)(2,1)}, u32[]{:S(2)}) copy-start(bf16[1536,512]{1,0:T(8,128)(2,1)} %get-tuple-element.62.x) | copy-start | bytes 4718596
  1056.6 6.7 copy-start.3
  1063.2 16.4 %copy-start.18 = (bf16[1536,512]{1,0:T(8,128)(2,1)}, bf16[1536,512]{1,0:T(8,128)(2,1)S(1)}, u32[]{:S(2)}) copy-start(bf16[1536,512]{1,0:T(8,128)(2,1)S(1)} %get-tuple-element.178) | copy-start | bytes 4718596
  1063.2 226.7 %reduce-scatter.15.cloned.1.call-start = ((), (), s32[]{:S(2)}) async-start(), calls=%async_computation.16 | async-start | bytes 7667712 | tf_op jit(solution)/shard_map/reduce_scatter | solution.py:917
  1063.3 18.8 %copy-start.24 = (f32[2048]{0:T(1024)S(1)}, f32[2048]{0:T(1024)}, u32[]{:S(2)}) copy-start(f32[2048]{0:T(1024)} %copy-done.23) | copy-start | bytes 24580
  1080.4 1.0 copy-start.17
  1082.1 15.5 %copy-start.15 = (bf16[2048,16]{1,0:T(8,128)(2,1)S(1)}, bf16[2048,16]{1,0:T(8,128)(2,1)}, u32[]{:S(2)}) copy-start(bf16[2048,16]{1,0:T(8,128)(2,1)} %copy.191) | copy-start | bytes 196612
  1082.1 15.5 %copy-start.16 = (bf16[2048,1]{1,0:T(8,128)(2,1)S(1)}, bf16[2048,1]{1,0:T(8,128)(2,1)}, u32[]{:S(2)}) copy-start(bf16[2048,1]{1,0:T(8,128)(2,1)} %stack.50) | copy-start | bytes 12292
  1169.0 106.3 %copy-start.8 = (f32[384,2048]{1,0:T(8,128)S(1)}, f32[384,2048]{1,0:T(8,128)}, u32[]{:S(2)}) copy-start(f32[384,2048]{1,0:T(8,128)} %copy-done.7) | copy-start | bytes 9437188
  1272.5 2.8 copy-start.6
  1280.3 8.8 collective-permute-start.6
  1312.7 6.3 copy-start.20
Sparse Core Ops, SparseCore 0:
  37.6 48.7 all-gather.5
  89.3 86.9 all-gather.7
  178.2 93.3 all-gather.9
  273.3 89.8 all-gather.11
  365.0 89.8 all-gather.13
  565.2 88.9 reduce-scatter.8
  658.2 115.9 reduce-scatter.6
  778.1 115.9 reduce-scatter.10
  898.0 71.2 reduce-scatter.12
  1063.3 42.6 reduce-scatter.16
  1109.9 65.5 reduce-scatter.14

commit v4 on v3

--- a/solution.py
+++ b/solution.py
@@ -19,6 +19,7 @@
 TILE = 256
 ROWS = 768
 FTILE = 256
+NTILE = 384
 EPS = 1e-05
 BOTH = ("dp", "expert")
 F32 = jnp.float32
@@ -197,11 +198,16 @@
 
 def remote(src, dst, send_sem, recv_sem, to):
     return pltpu.make_async_remote_copy(
-        src_ref=src, dst_ref=dst, send_sem=send_sem, recv_sem=recv_sem, device_id=peer(to), device_id_type=MESH
+        src_ref=src,
+        dst_ref=dst,
+        send_sem=send_sem,
+        recv_sem=recv_sem,
+        device_id=to if isinstance(to, dict) else peer(to),
+        device_id_type=MESH,
     )
 
 
-def greet_line(n):
+def greet_line(n, others=()):
     p = lax.axis_index("expert")
     bar = pltpu.get_barrier_semaphore()
 
@@ -213,7 +219,9 @@
     def _():
         pl.semaphore_signal(bar, inc=1, device_id=peer(p + 1), device_id_type=MESH)
 
-    pl.semaphore_wait(bar, (p > 0).astype(jnp.int32) + (p < n - 1).astype(jnp.int32))
+    for other in others:
+        pl.semaphore_signal(bar, inc=1, device_id=other, device_id_type=MESH)
+    pl.semaphore_wait(bar, (p > 0).astype(jnp.int32) + (p < n - 1).astype(jnp.int32) + len(others))
     return p
 
 
@@ -227,46 +235,48 @@
 
 
 class Gather:
-    sems = lambda n: [DMA((n,))] * 3
-
-    def __init__(self, p, n, own, at, sems):
-        self.p, self.n, self.own, self.at = p, n, own, at
+    sems = lambda n, pieces=1: [DMA((n * pieces,))] * 3
+
+    def __init__(self, p, n, own, at, sems, pieces=1):
+        self.p, self.n, self.own, self.at, self.pieces = p, n, own, at, pieces
         self.to_right, self.to_left, self.recv = sems
 
-    def right(self, src, j):
-        return remote(src, self.at(j), self.to_right.at[j], self.recv.at[j], self.p + 1)
-
-    def left(self, src, j):
-        return remote(src, self.at(j), self.to_left.at[j], self.recv.at[j], self.p - 1)
-
-    def start(self):
+    def right(self, src, j, c):
+        i = j * self.pieces + c
+        return remote(src, self.at(j, c), self.to_right.at[i], self.recv.at[i], self.p + 1)
+
+    def left(self, src, j, c):
+        i = j * self.pieces + c
+        return remote(src, self.at(j, c), self.to_left.at[i], self.recv.at[i], self.p - 1)
+
+    def start(self, c=0):
         @pl.when(self.p < self.n - 1)
         def _():
-            self.right(self.own, self.p).start()
+            self.right(self.own(c), self.p, c).start()
 
         @pl.when(self.p > 0)
         def _():
-            self.left(self.own, self.p).start()
-
-    def step(self, s, use=None):
+            self.left(self.own(c), self.p, c).start()
+
+    def step(self, s, use=None, c=0):
         p, n = self.p, self.n
         j, k = p - s, p + s
 
         @pl.when(j >= 0)
         def _():
-            self.right(self.at(j), j).wait_recv()
+            self.right(self.at(j, c), j, c).wait_recv()
 
             @pl.when(p < n - 1)
             def _():
-                self.right(self.at(j), j).start()
+                self.right(self.at(j, c), j, c).start()
 
         @pl.when(k < n)
         def _():
-            self.left(self.at(k), k).wait_recv()
+            self.left(self.at(k, c), k, c).wait_recv()
 
             @pl.when(p > 0)
             def _():
-                self.left(self.at(k), k).start()
+                self.left(self.at(k, c), k, c).start()
 
         if use is not None:
             for i, here in ((j, j >= 0), (k, k < n)):
@@ -274,14 +284,15 @@
 
     def finish(self):
         for j in range(self.n):
-
-            @pl.when((j <= self.p) & (self.p < self.n - 1))
-            def _():
-                self.right(self.own, j).wait_send()
-
-            @pl.when((j >= self.p) & (self.p > 0))
-            def _():
-                self.left(self.own, j).wait_send()
+            for c in range(self.pieces):
+
+                @pl.when((j <= self.p) & (self.p < self.n - 1))
+                def _():
+                    self.right(self.own(c), j, c).wait_send()
+
+                @pl.when((j >= self.p) & (self.p > 0))
+                def _():
+                    self.left(self.own(c), j, c).wait_send()
 
 
 class Reduce:
@@ -311,37 +322,44 @@
         total = self.at(j, c)[...].astype(F32) + box[j * self.pieces + c].astype(F32)
         self.at(j, c)[...] = total.astype(BF16)
 
-    def step(self, s):
+    def make_step(self, s):
+        j, k = self.n - 1 - s, s
+        pl.when(j > self.p)(lambda: self.make(j))
+        pl.when(k < self.p)(lambda: self.make(k))
+
+    def piece(self, s, c):
         p, n = self.p, self.n
         j, k = n - 1 - s, s
-        pl.when(j > p)(lambda: self.make(j))
-        pl.when(k < p)(lambda: self.make(k))
+        m = s * self.pieces + c
+
+        @pl.when(j > p)
+        def _():
+            @pl.when(p > 0)
+            def _():
+                self.right(j, c).wait_recv()
+                self.add(j, c, self.from_left)
+
+            if m >= self.depth:
+                s0, c0 = self.order[m - self.depth]
+                self.right(n - 1 - s0, c0).wait_send()
+            self.right(j, c).start()
+
+        @pl.when(k < p)
+        def _():
+            @pl.when(p < n - 1)
+            def _():
+                self.left(k, c).wait_recv()
+                self.add(k, c, self.from_right)
+
+            if m >= self.depth:
+                s0, c0 = self.order[m - self.depth]
+                self.left(s0, c0).wait_send()
+            self.left(k, c).start()
+
+    def step(self, s):
+        self.make_step(s)
         for c in range(self.pieces):
-            m = s * self.pieces + c
-
-            @pl.when(j > p)
-            def _():
-                @pl.when(p > 0)
-                def _():
-                    self.right(j, c).wait_recv()
-                    self.add(j, c, self.from_left)
-
-                if m >= self.depth:
-                    s0, c0 = self.order[m - self.depth]
-                    self.right(n - 1 - s0, c0).wait_send()
-                self.right(j, c).start()
-
-            @pl.when(k < p)
-            def _():
-                @pl.when(p < n - 1)
-                def _():
-                    self.left(k, c).wait_recv()
-                    self.add(k, c, self.from_right)
-
-                if m >= self.depth:
-                    s0, c0 = self.order[m - self.depth]
-                    self.left(s0, c0).wait_send()
-                self.left(k, c).start()
+            self.piece(s, c)
 
     def finish(self, out, base=None):
         p, n, size = self.p, self.n, self.rows // self.pieces
@@ -374,36 +392,94 @@
     return lambda j: ref.at[pl.ds(pl.multiple_of(j * rows, rows), rows)]
 
 
-def ag_kernel(n, rows, x, out, to_right, to_left, recv, local):
-    p = greet_line(n)
+def ag_kernel(n, rows, x, *rest):
+    count = (len(rest) - 7) // 2
+    blocks, out, fulls = rest[:count], rest[count], rest[count + 1 : 2 * count + 1]
+    to_right, to_left, recv, local, sent, came = rest[2 * count + 1 :]
+    d = lax.axis_index("dp")
+    core, by_x, by_y = lax.rem(d, 2), lax.rem(d // 2, 2), d // 4
+    d_x, d_y, d_c = d + 2 - 4 * by_x, d + 4 - 8 * by_y, d + 1 - 2 * core
+    d_far = d_x + 4 - 8 * by_y
+    x_way, y_way, c_way = {"dp": d_x}, {"dp": d_y}, {"dp": d_c}
+    p = greet_line(n, (x_way, y_way, c_way) if count else ())
     at = rows_of(out, rows)
-    own = pltpu.make_async_copy(x, at(p), local)
+    own = pltpu.make_async_copy(x, at(p), local.at[0])
     own.start()
-    line = Gather(p, n, x, at, (to_right, to_left, recv))
+    line = Gather(p, n, lambda c: x, lambda j, c: at(j), (to_right, to_left, recv))
     line.start()
-    for s in range(1, n):
+
+    def send(a, src, first, size, kind, way):
+        dst = fulls[a].at[pl.ds(pl.multiple_of(first, size), size)]
+        return remote(dst if src is None else src, dst, sent.at[a, kind], came.at[a, kind], way)
+
+    def moves(a):
+        size = blocks[a].shape[0]
+        half = size // 2
+        return [
+            lambda: send(a, blocks[a], d * size, size, 0, x_way),
+            lambda: send(a, blocks[a], d * size, size, 1, y_way),
+            lambda: send(a, blocks[a], d * size, size, 2, c_way),
+            lambda: send(a, None, d_x * size, half, 3, y_way),
+            lambda: send(a, None, d_y * size + half, half, 4, x_way),
+            lambda: send(a, None, d_x * size, size, 5, c_way),
+            lambda: send(a, None, d_y * size, size, 6, c_way),
+            lambda: send(a, None, d_far * size, size, 7, c_way),
+        ]
+
+    all_moves = [moves(a) for a in range(count)]
+    locals_ = [
+        pltpu.make_async_copy(
+            blocks[a],
+            fulls[a].at[pl.ds(pl.multiple_of(d * blocks[a].shape[0], blocks[a].shape[0]), blocks[a].shape[0])],
+            local.at[a + 1],
+        )
+        for a in range(count)
+    ]
+    for a in range(count):
+        locals_[a].start()
+        for k in range(3):
+            all_moves[a][k]().start()
+    for a in range(count):
+        for k in (0, 1):
+            all_moves[a][k]().wait_recv()
+        for k in (3, 4, 5, 6):
+            all_moves[a][k]().start()
+    line.step(1)
+    for a in range(count):
+        for k in (3, 4):
+            all_moves[a][k]().wait_recv()
+        all_moves[a][7]().start()
+    for s in range(2, n):
         line.step(s)
+    for a in range(count):
+        locals_[a].wait()
+        for k in (2, 5, 6, 7):
+            all_moves[a][k]().wait_recv()
+        for k in range(8):
+            all_moves[a][k]().wait_send()
     own.wait()
     line.finish()
 
 
-def ag_z(x, n, cid):
+def ag_z(x, n, cid, blocks=()):
     rows = x.shape[0]
+    count = len(blocks)
+    grown = lambda b, k: jax.ShapeDtypeStruct((k * b.shape[0],) + b.shape[1:], b.dtype)
     return pl.pallas_call(
         functools.partial(ag_kernel, n, rows),
-        out_shape=jax.ShapeDtypeStruct((n * rows,) + x.shape[1:], x.dtype),
-        in_specs=[ANY],
-        out_specs=ANY,
-        scratch_shapes=Gather.sems(n) + [DMA],
+        out_shape=[grown(x, n)] + [grown(b, 8) for b in blocks],
+        in_specs=[ANY] * (1 + count),
+        out_specs=[ANY] * (1 + count),
+        scratch_shapes=Gather.sems(n) + [DMA((1 + count,)), DMA((max(count, 1), 8)), DMA((max(count, 1), 8))],
         compiler_params=params(cid),
-    )(x)
+    )(x, *blocks)
 
 
 def gather_kernel(n, rows, x, slot, small, grads, logits, rows_out, grads_out, *rest):
     shards, picked, picked_grads, to_right, to_left, recv, out_sems = rest
     p = greet_line(n)
     experts = slot.shape[1]
-    line = Gather(p, n, x, lambda j: shards.at[j], (to_right, to_left, recv))
+    line = Gather(p, n, lambda c: x, lambda j, c: shards.at[j], (to_right, to_left, recv))
     line.start()
 
     def pick(j, e):
@@ -517,13 +593,24 @@
     at = rows_of(all_out, rows)
     own = pltpu.make_async_copy(x, at(p), sems[7])
     own.start()
-    gather = Gather(p, n, x, at, sems[:3])
-    gather.start()
+    size = rows // Reduce.pieces
+    piece = lambda j, c: all_out.at[pl.ds(pl.multiple_of(j * rows + c * size, size), size)]
+    gather = Gather(p, n, lambda c: x.at[pl.ds(c * size, size)], piece, sems[:3], Reduce.pieces)
     make = combine(part, rows, slot, weight, (low, high))
     line = Reduce(p, n, rows, part, make, (left_box, right_box), sems[3:7])
-    for s in range(n - 1):
-        line.step(s)
-        gather.step(s + 1)
+    for s in range(n):
+        if s == 0:
+            gather.start(0)
+            gather.start(1)
+        if s < n - 1:
+            line.make_step(s)
+        for c in range(Reduce.pieces):
+            if s:
+                gather.step(s, c=c)
+            elif c > 1:
+                gather.start(c)
+            if s < n - 1:
+                line.piece(s, c)
     line.finish(out, base)
     own.wait()
     gather.finish()
@@ -538,7 +625,7 @@
         out_specs=[ANY, VM],
         scratch_shapes=[pltpu.VMEM((n * rows, width), BF16)]
         + Reduce.boxes(n, rows, width)
-        + Gather.sems(n)
+        + Gather.sems(n, Reduce.pieces)
         + Reduce.sems(n)
         + [DMA],
         compiler_params=params(cid),
@@ -657,11 +744,12 @@
         eo[here, :] += plain(hidden.astype(BF16), down[0])
         gin[here, :] += by_transpose(gg, gate[0]) + by_transpose(gu, up[0])
 
-    pieces, rows = gu_out.shape[0], gu_out.shape[2]
+    pieces, rows = gu_out.shape[0], gu_out.shape[3]
 
     grad_both = plain(xt[...], both[...]).astype(BF16)
     for c in range(pieces):
-        gu_out[c, 0] = grad_both[c * rows : (c + 1) * rows]
+        gu_out[c, 0, 0] = grad_both[c * rows : (c + 1) * rows, :tile]
+        gu_out[c, 1, 0] = grad_both[c * rows : (c + 1) * rows, tile:]
 
     down_rows = gd_out.shape[2]
     grad_down = cross_rows(scaled[...], g[...]).astype(BF16)
@@ -698,14 +786,14 @@
             slots_out,
             slots_out,
             pl.BlockSpec((1, 1, tokens), lambda e, f: (e, 0, 0)),
-            pl.BlockSpec((dp, 1, width // dp, 2 * FTILE), lambda e, f: (0, e, 0, f)),
+            pl.BlockSpec((dp, 2, 1, width // dp, FTILE), lambda e, f: (0, 0, e, 0, f)),
             pl.BlockSpec((FTILE // down_rows, 1, down_rows, width), lambda e, f: (f, e, 0, 0)),
         ],
         out_shape=[
             jax.ShapeDtypeStruct((count, CAP, width), BF16),
             jax.ShapeDtypeStruct((count, CAP, width), BF16),
             jax.ShapeDtypeStruct((count, 1, tokens), F32),
-            jax.ShapeDtypeStruct((dp, count, width // dp, 2 * ff), BF16),
+            jax.ShapeDtypeStruct((dp, 2, count, width // dp, ff), BF16),
             jax.ShapeDtypeStruct((dp, count, down_rows, width), BF16),
         ],
         scratch_shapes=[
@@ -726,8 +814,9 @@
 
 def hops(up, down, count, ways):
     for _ in range(count):
-        up = up + [lax.ppermute(up[-1], "expert", [(i, i + 1) for i in range(ways - 1)])]
-        down = down + [lax.ppermute(down[-1], "expert", [(i + 1, i) for i in range(ways - 1)])]
+        h = len(up)
+        up = up + [lax.ppermute(up[-1], "expert", [(i, i + 1) for i in range(h - 1, ways - 1)])]
+        down = down + [lax.ppermute(down[-1], "expert", [(i + 1, i) for i in range(ways - h)])]
     return up, down
 
 
@@ -742,6 +831,36 @@
     rows = down[0].shape[0]
     start = (ways - 1 - lax.axis_index("expert")) * rows
     return lax.dynamic_slice_in_dim(line, start, ways * rows, axis=0)
+
+
+def norm_qkv_kernel(columns, x, gain, weight, out, normed, inverse):
+    values = x[...].astype(F32)
+    inv = lax.rsqrt(jnp.mean(values * values, axis=1, keepdims=True) + EPS)
+    rows = (values * inv * gain[...]).astype(BF16)
+    inverse[...] = inv
+    normed[...] = rows
+    out[...] = plain(rows, weight[:, :columns])
+
+
+def norm_qkv(x, gain, weight, columns):
+    tokens, width = x.shape
+    tile = lambda w: pl.BlockSpec((NTILE, w), lambda i: (i, 0))
+    return pl.pallas_call(
+        functools.partial(norm_qkv_kernel, columns),
+        grid=(tokens // NTILE,),
+        in_specs=[
+            tile(width),
+            pl.BlockSpec((1, width), lambda i: (0, 0)),
+            pl.BlockSpec(weight.shape, lambda i: (0, 0), pipeline_mode=pl.Buffered(1)),
+        ],
+        out_specs=[tile(columns), tile(width), tile(1)],
+        out_shape=[
+            jax.ShapeDtypeStruct((tokens, columns), F32),
+            jax.ShapeDtypeStruct((tokens, width), BF16),
+            jax.ShapeDtypeStruct((tokens, 1), F32),
+        ],
+        compiler_params=pltpu.CompilerParams(vmem_limit_bytes=48 * 2**20),
+    )(x, gain, weight)
 
 
 def block_order(segs, places):
@@ -795,22 +914,23 @@
     small = jnp.pad(small, ((0, 0), (0, SMALL - small.shape[1])))
     shard = jnp.stack([query_weight, key_weight, value_weight], axis=1)
     shard = shard.reshape(-1, 3, ways, cols).transpose(2, 0, 1, 3).reshape(ways, -1, 3 * cols)
-    shard = jnp.concatenate([shard, jnp.broadcast_to(small[None], (ways,) + small.shape)], axis=2)
+    rest = jnp.concatenate([small, out_weight], axis=1)
+    shard = jnp.concatenate([shard, jnp.broadcast_to(rest[None], (ways,) + rest.shape)], axis=2)
     shard = exchange_z(shard.reshape(-1, shard.shape[-1]), ways, 1)
-    dense = lax.all_gather(shard, "dp", axis=0, tiled=True)
+    shards = shard[:, : 3 * cols + SMALL], shard[:, 3 * cols + SMALL :]
+    if lax.axis_size("dp") == 8:
+        tokens_all, dense, out_full = ag_z(tokens, ways, 2, shards)
+    else:
+        (tokens_all,) = ag_z(tokens, ways, 2)
+        dense, out_full = (lax.all_gather(s, "dp", axis=0, tiled=True) for s in shards)
     qkv_weight = dense[:, : 3 * cols]
     small = dense[:, 3 * cols :]
-    shard, out_weight, gate_weight, up_weight, down_weight = lax.optimization_barrier(
-        (shard, out_weight, gate_weight, up_weight, down_weight)
-    )
-    out_full = lax.all_gather(out_weight, BOTH, axis=0, tiled=True)
     attend_gain = small[:, 0].astype(F32)
     mix_gain = small[:, 3].astype(F32)
     router_full = small[:, 4 : 4 + EXPERTS]
     my_gains = lax.dynamic_slice_in_dim(small[:, 1:3], z * cols, cols, axis=0).astype(F32)
     gain_q, gain_k = my_gains[:, 0][None], my_gains[:, 1][None]
     out_mine = lax.dynamic_slice_in_dim(out_full, z * cols, cols, axis=0)
-    tokens_all = ag_z(tokens, ways, 2)
     gate_full = lax.all_gather(gate_weight, "dp", axis=1, tiled=True)
     up_full = lax.all_gather(up_weight, "dp", axis=1, tiled=True)
     down_full = lax.all_gather(down_weight, "dp", axis=1, tiled=True)
@@ -833,10 +953,7 @@
     slot_shards = my_slot.T.reshape(experts_here, ways, tok_dev).transpose(1, 0, 2)
     slot_cols = my_slot.reshape(ways, tok_dev, experts_here)
 
-    token_f = tokens_all.astype(F32)
-    inverse_in = lax.rsqrt(jnp.mean(token_f * token_f, axis=-1, keepdims=True) + EPS)
-    normed = (token_f * inverse_in * attend_gain).astype(BF16)
-    qkv = plain(normed, qkv_weight)
+    qkv, normed, inverse_in = norm_qkv(tokens_all, attend_gain[None], dense, 3 * cols)
     squares = jnp.sum(jnp.square(qkv[:, : 2 * cols]).reshape(GTOK, 2, cols), axis=-1)
     squares = sum_z(jnp.pad(squares.T, ((0, 6), (0, 0))), ways, 3)
     up, down, squares = later(sent, squares)
@@ -898,7 +1015,7 @@
     grad_k = (inv_k * (dk * gain_k - k_unit * inner[1][:, None])).astype(BF16)
     grad_qkv = jnp.concatenate([grad_q, grad_k, dv], axis=1)
     grad_normed_part = by_transpose(grad_qkv, qkv_weight)
-    grad_attend_gain = jnp.sum(grad_normed_part * (token_f * inverse_in), axis=0)
+    grad_attend_gain = jnp.sum(grad_normed_part * (tokens_all.astype(F32) * inverse_in), axis=0)
     part, sum_down_high = lax.optimization_barrier((grad_normed_part.astype(BF16), sum_down_high))
     grad_normed = rs_z(part, ways, 9).astype(F32)
     own_inverse = lax.dynamic_slice_in_dim(inverse_in, first_row, tok_dev, axis=0)
@@ -920,10 +1037,8 @@
         grad_qkv_w[:, :, i * cols : (i + 1) * cols].transpose(1, 0, 2).reshape(-1, width).astype(F32)
         for i in range(3)
     ]
-    sums = jnp.concatenate([sum_both_low[0], sum_both_high[0]], axis=0).astype(F32)
-    sums = sums.reshape(sums.shape[:2] + (-1, 2, FTILE))
-    out_gate = sums[:, :, :, 0].reshape(gate_weight.shape)
-    out_up = sums[:, :, :, 1].reshape(gate_weight.shape)
+    planes = [jnp.concatenate([sum_both_low[0, i], sum_both_high[0, i]], axis=0) for i in range(2)]
+    out_gate, out_up = planes[0].astype(F32), planes[1].astype(F32)
     out_down = jnp.concatenate([sum_down_low[0], sum_down_high[0]], axis=0).astype(F32)
     packed = jnp.sum(grad_qkv_w[:, :, 3 * cols :].astype(F32), axis=0)
     return (

time: 1330 us -> 1310 us (0.985)
  local copies, waits for them, and re-layouts: 115 us -> 71.4 us
  Pallas kernels: 1010 us -> 1040 us
  matrix products: 75.4 us -> 59.9 us
    slice x1 -> x2, local copies, waits for them, and re-layouts: 29.7 us -> 4.55 us  [body(): shards = (shard[:, :3 * cols + SMALL], shard[:, 3 * cols + SMALL:])]
    pallas_call x2, Pallas kernels: 45 us -> 67.9 us  [exchange_z(): pl.pallas_call(functools.partial(exchange_kernel, n, x.shape[0] // n), ou...]
    pallas_call x1 -> x2, Pallas kernels: 144 us -> 160 us  [the longest x1 144 us: ag_z(): pl.pallas_call(functools.partial(ag_kernel, n, rows), out_shape=[grown(x,...]
    dot_general x3 -> x2, matrix products: 23.4 us -> 8.07 us  [plain(): lax.dot_general(left, right, (((1,), (0,)), ((), ())), preferred_element_...]
  transfers between devices with their start and end apart: 19 -> 17, of which waited for: 1 -> 2; matrix products, arithmetic and copies ran while one was open for 17% -> 14% of each run, Pallas kernels for 66% -> 72%
where the time goes in v4:
time: 1310 us; the launch traced here: 1300 us
  Pallas kernels  1040 us (79%)
  local copies, waits for them, and re-layouts  71.4 us (5%)
  other arithmetic  60.4 us (5%)
  matrix products  59.9 us (5%)
  starting transfers between devices  49.7 us (4%)
  between operations  15.3 us (1%)
    pallas_call x1, Pallas kernels, gather_and_combine(): pl.pallas_call(functools.partial(both_kernel, n, rows), out_shape=[jax.Sh...  175 us
    pallas_call x2, Pallas kernels, experts(): pl.pallas_call(expert_kernel, grid=(count, steps), in_specs=[line, line,...  164 us
    pallas_call x1, Pallas kernels, ag_z(): pl.pallas_call(functools.partial(ag_kernel, n, rows), out_shape=[grown(x,...  144 us
    pallas_call x1, Pallas kernels, combine_z(): pl.pallas_call(functools.partial(combine_kernel, n, rows), out_shape=jax....  139 us
    pallas_call x1, Pallas kernels, gather_rows(): pl.pallas_call(functools.partial(gather_kernel, n, rows), out_shape=[jax....  106 us
    pallas_call x1, Pallas kernels, rs_z(): pl.pallas_call(functools.partial(rs_kernel, n, rows), out_shape=jax.Shape...  99 us
    pallas_call x2, Pallas kernels, exchange_z(): pl.pallas_call(functools.partial(exchange_kernel, n, x.shape[0] // n), ou...  67.9 us
    pallas_call x1, Pallas kernels, a2a_z(): pl.pallas_call(functools.partial(a2a_kernel, n, rows, cols), out_shape=ja...  54.5 us
  transfers between devices with their start and end apart: 17, of which 2 were waited for; matrix products, arithmetic and copies ran while one was open for 14% of the time, Pallas kernels for 72%

profile of v4, /device:TPU:10, one launch (start us, length us, event | category | flops | bytes accessed | tf_op | source)
XLA Modules:
  0.0 1304.4 jit_solution(6907929594952548592)
XLA Ops:
  11.4 1.8 pad_maximum_fusion.4
  13.9 1.4 pad_maximum_fusion.3.x
  15.2 44.6 %shard_map.281 = bf16[256,3712]{1,0:T(8,128)(2,1)} custom-call(bf16[256,3712]{1,0:T(8,128)(2,1)} %pad_maximum_fusion.3.x), custom_call_target="tpu_custom_call" | custom-call | tf_op jit(solution)/shard_map/pallas_call | solution.py:679
  59.9 2.4 slice.104.rest_1_
  62.3 2.1 slice.103.rest_0_
  64.4 143.7 %shard_map.282 = (bf16[1536,2048]{1,0:T(8,128)(2,1)}, bf16[2048,1664]{1,0:T(8,128)(2,1)}, bf16[2048,2048]{1,0:T(8,128)(2,1)}) custom-call(bf16[384,2048]{1,0:T(8,128)(2,1)} %x.7, bf16[256,1664]{1,0:T(8,128)(2,1)} %slice.103.rest_0_, bf16[256,2048]{1,0:T(8,128)(2,1)} %slice.104.rest_1_), custom_call_target="tpu_custom_call" | custom-call | tf_op jit(solution)/shard_map/pallas_call | solution.py:468
  208.1 3.7 collective-permute-start
  211.8 3.8 collective-permute-start.1
  215.7 1.8 convert_reduce_fusion
  217.5 16.8 %shard_map.283 = (f32[1536,1536]{1,0:T(8,128)}, bf16[1536,2048]{1,0:T(8,128)(2,1)}, f32[1536,1]{1,0:T(8,128)S(1)}) custom-call(bf16[1536,2048]{1,0:T(8,128)(2,1)} %get-tuple-element.60.x, f32[1,2048]{1,0:T(1,128)S(1)} %bitcast.91, bf16[2048,1664]{1,0:T(8,128)(2,1)} %get-tuple-element.61.weight), custom_call_target="tpu_custom_call" | custom-call | tf_op jit(solution)/shard_map/pallas_call | solution.py:848
  234.3 7.4 slice_multiply_fusion
  241.7 1.2 slice.111
  242.9 1.9 slice.115.small
  244.8 9.4 reshape.230
  254.2 6.0 reduce_sum.135
  261.1 8.5 shard_map.284
  271.1 1.6 fusion
  273.4 4.9 collective-permute-start.2
  278.3 2.1 collective-permute-start.3
  280.9 2.8 fusion.17
  285.8 25.9 %shard_map.285 = (bf16[1536,512]{1,0:T(8,128)(2,1)S(1)}, bf16[1536,512]{1,0:T(8,128)(2,1)}, bf16[1536,512]{1,0:T(8,128)(2,1)}, bf16[1536,512]{1,0:T(8,128)(2,1)}, f32[1536,512]{1,0:T(8,128)}) custom-call(s32[12]{0:T(128)S(1)} %select_reduce_fusion.1.order, f32[1536,1536]{1,0:T(8,128)} %get-tuple-element.62.q_pre.k_pre.v_pre, ...), custom_call_target="tpu_custom_call" | custom-call | tf_op jit(solution)/shard_map/pallas_call | solution.py:110
  313.7 1.8 collective-permute-start.4
  315.5 3.3 collective-permute-start.5
  318.9 54.5 %shard_map.286 = bf16[384,2048]{1,0:T(8,128)(2,1)} custom-call(bf16[1536,512]{1,0:T(8,128)(2,1)} %get-tuple-element.67.x), custom_call_target="tpu_custom_call" | custom-call | tf_op jit(solution)/shard_map/pallas_call | solution.py:652
  373.4 6.5 multiply_reduce_fusion.7
  380.0 1.7 multiply_convert_fusion.2.x
  381.6 1.5 constant_dynamic-update-slice_fusion.6
  383.2 1.6 constant_dynamic-update-slice_fusion.5
  384.8 1.5 constant_dynamic-update-slice_fusion.4
  386.5 1.5 constant_dynamic-update-slice_fusion.2
  388.0 1.5 constant_dynamic-update-slice_fusion.1
  389.6 1.5 constant_dynamic-update-slice_fusion
  391.1 3.3 constant_dynamic-slice_fusion.1.grads
  394.3 105.5 %shard_map.287 = (f32[1536,128]{1,0:T(8,128)}, bf16[4,768,2048]{2,1,0:T(8,128)(2,1)}, bf16[4,768,2048]{2,1,0:T(8,128)(2,1)}) custom-call(bf16[384,2048]{1,0:T(8,128)(2,1)} %multiply_convert_fusion.2.x, s32[4,4,384]{2,1,0:T(4,128)} %bitcast.108, bf16[2048,128]{1,0:T(8,128)(2,1)} %slice.115.small, bf16[1536,2048]{1,0:T(8,128)(2,1)} %constant_dynamic-slice_fusion.1.grads), custom_call_target="tpu_custom_call" | custom-call | tf_op jit(solution)/shard_map/pallas_call | solution.py:518
  499.9 1.4 copy.157
  502.0 81.8 %shard_map.288 = (bf16[2,768,2048]{2,1,0:T(8,128)(2,1)}, bf16[2,768,2048]{2,1,0:T(8,128)(2,1)}, f32[2,1,1536]{2,1,0:T(1,128)}, bf16[8,2,2,256,1024]{4,3,2,1,0:T(8,128)(2,1)}, bf16[8,2,128,2048]{3,2,1,0:T(8,128)(2,1)}) custom-call(s32[4,1,1536]{2,1,0:T(1,128)} %broadcast_in_dim.87.slot, f32[4,1,1536]{2,1,0:T(1,128)} %broadcast_in_dim.88.weight, ...), custom_call_target="tpu_custom_call" | custom-call | tf_op jit(solution)/shard_map/pallas_call | solution.py:781
  584.5 82.0 %shard_map.289 = (bf16[2,768,2048]{2,1,0:T(8,128)(2,1)}, bf16[2,768,2048]{2,1,0:T(8,128)(2,1)}, f32[2,1,1536]{2,1,0:T(1,128)}, bf16[8,2,2,256,1024]{4,3,2,1,0:T(8,128)(2,1)}, bf16[8,2,128,2048]{3,2,1,0:T(8,128)(2,1)}) custom-call(s32[4,1,1536]{2,1,0:T(1,128)} %broadcast_in_dim.87.slot, f32[4,1,1536]{2,1,0:T(1,128)} %broadcast_in_dim.88.weight, ...), custom_call_target="tpu_custom_call" | custom-call | tf_op jit(solution)/shard_map/pallas_call | solution.py:781
  667.5 1.2 copy.155
  669.7 24.9 %all-to-all-start = ((f32[4,4,384]{2,0,1:T(4,128)}), f32[4,4,384]{2,0,1:T(4,128)S(1)}, u32[]{:S(2)}, u32[]{:S(2)}) async-start(f32[4,4,384]{2,0,1:T(4,128)} %bitcast.40), calls=%async_computation | async-start | bytes 49152 | tf_op jit(solution)/shard_map/all_to_all | solution.py:987
  695.8 139.3 %shard_map.290 = bf16[384,2048]{1,0:T(8,128)(2,1)} custom-call(s32[4,384,4]{2,1,0:T(8,128)} %bitcast.94, bf16[2,768,2048]{2,1,0:T(8,128)(2,1)} %get-tuple-element.74.low, bf16[2,768,2048]{2,1,0:T(8,128)(2,1)} %get-tuple-element.75.high), custom_call_target="tpu_custom_call" | custom-call | tf_op jit(solution)/shard_map/pallas_call | solution.py:581
  836.5 4.4 multiply_reduce_fusion.1
  841.0 1.4 stack.50
  842.8 2.1 fusion.30.x
  845.0 174.6 %shard_map.291 = (bf16[1536,2048]{1,0:T(8,128)(2,1)}, bf16[384,2048]{1,0:T(8,128)(2,1)}) custom-call(bf16[384,2048]{1,0:T(8,128)(2,1)} %fusion.30.x, s32[4,384,4]{2,1,0:T(8,128)} %bitcast.95, f32[4,384,4]{2,1,0:T(8,128)} %bitcast.100, bf16[2,768,2048]{2,1,0:T(8,128)(2,1)} %get-tuple-element.81.low, bf16[2,768,2048]{2,1,0:T(8,128)(2,1)} %get-tuple-element.82.high, ...), custom_call_target="tpu_custom_call" | custom-call | tf_op jit(solution)/shard_map/pallas_call | solution.py:621
  1019.6 8.2 convolution_convert_fusion.2.grad_mixed
  1027.9 27.5 %shard_map.292 = (f32[1536,512]{1,0:T(8,128)}, f32[1536,512]{1,0:T(8,128)}, bf16[1536,512]{1,0:T(8,128)(2,1)S(1)}) custom-call(s32[12]{0:T(128)S(1)} %select_reduce_fusion.1.order, bf16[1536,512]{1,0:T(8,128)(2,1)S(1)} %copy-done.1, bf16[1536,512]{1,0:T(8,128)(2,1)} %get-tuple-element.86.k_rot, bf16[1536,512]{1,0:T(8,128)(2,1)} %get-tuple-element.87.v_in, ...), custom_call_target="tpu_custom_call" | custom-call | tf_op jit(solution)/shard_map/pallas_call | solution.py:167
  1055.4 6.1 multiply_reduce_fusion.2
  1062.2 15.8 %shard_map.293 = f32[8,1536]{1,0:T(8,128)} custom-call(f32[8,1536]{1,0:T(8,128)} %select_maximum_fusion.x), custom_call_target="tpu_custom_call" | custom-call | tf_op jit(solution)/shard_map/pallas_call | solution.py:701
  1078.9 7.5 convolution_convert_fusion.1
  1086.4 6.6 multiply_convert_fusion.1
  1093.0 16.3 %multiply_reduce_fusion = (bf16[2048]{0:T(1024)(128)(2,1)S(1)}, bf16[1536,2048]{1,0:T(8,128)(2,1)}) fusion(bf16[1536,2048]{1,0:T(8,128)(2,1)} %get-tuple-element.60.x, f32[1536]{0:T(1024)S(1)} %reduce.17, bf16[2048,1664]{1,0:T(8,128)(2,1)} %get-tuple-element.61.weight, bf16[1536,512]{1,0:T(8,128)(2,1)S(1)} %copy-done.7, ...), kind=kOutput, calls=%fused_computation | convolution fusion | flops 9693558784 | bytes 23603200 | tf_op jit(solution)/shard_map/dot_general | solution.py:44
  1112.5 15.1 %convolution_convert_fusion = bf16[2048,1536]{1,0:T(8,128)(2,1)} fusion(bf16[1536,2048]{1,0:T(8,128)(2,1)} %get-tuple-element.97, bf16[1536,512]{1,0:T(8,128)(2,1)S(1)} %copy-done.7, bf16[1536,512]{1,0:T(8,128)(2,1)} %get-tuple-element.181, bf16[1536,512]{1,0:T(8,128)(2,1)} %copy-done.25), kind=kOutput, calls=%fused_computation.5 | convolution fusion | flops 9680977920 | bytes 17301504 | tf_op jit(solution)/shard_map/dot_general | solution.py:40
  1127.6 12.0 concatenate.53
  1140.8 99.0 %shard_map.294 = bf16[384,2048]{1,0:T(8,128)(2,1)} custom-call(bf16[1536,2048]{1,0:T(8,128)(2,1)} %get-tuple-element.96.part), custom_call_target="tpu_custom_call" | custom-call | tf_op jit(solution)/shard_map/pallas_call | solution.py:544
  1239.9 2.3 fusion.8
  1242.2 2.8 slice_bitcast_fusion
  1246.5 2.4 maximum_convert_fusion.2
  1248.9 1.3 copy-done.10
  1251.2 3.3 fusion.11
  1254.5 4.6 collective-permute-start.6
  1259.1 3.8 maximum_convert_fusion.1
  1263.0 2.3 maximum_convert_fusion
  1266.6 23.3 %shard_map.295 = bf16[256,1664]{1,0:T(8,128)(2,1)} custom-call(bf16[256,1664]{1,0:T(8,128)(2,1)} %reduce-scatter.15.cloned.1.call-done.x), custom_call_target="tpu_custom_call" | custom-call | tf_op jit(solution)/shard_map/pallas_call | solution.py:679
  1290.0 1.4 convert_bitcast_fusion
  (202 shorter events, 34.2 us)
Async XLA Ops:
  7.2 2.3 copy-start.32
  7.2 494.8 %all-gather.4.cloned.1.call-start = ((), (), s32[]{:S(2)}) async-start(), calls=%async_computation.7 | async-start | bytes 18874368 | tf_op jit(solution)/shard_map/all_gather | solution.py:934
  7.9 2.2 copy-start.33
  7.9 2.8 copy-start.34
  7.9 494.1 %all-gather.6.cloned.1.call-start = ((), (), s32[]{:S(2)}) async-start(), calls=%async_computation.8 | async-start | bytes 18874368 | tf_op jit(solution)/shard_map/all_gather | solution.py:935
  8.7 493.3 %all-gather.8.cloned.1.call-start = ((), (), s32[]{:S(2)}) async-start(), calls=%async_computation.9 | async-start | bytes 18874368 | tf_op jit(solution)/shard_map/all_gather | solution.py:936
  9.4 835.5 %reduce-scatter.9.cloned.1.call-start = ((), (), s32[]{:S(2)}) async-start(), calls=%async_computation.11 | async-start | bytes 9437184 | tf_op jit(solution)/shard_map/reduce_scatter | solution.py:982
  10.3 3.1 copy-start.42
  10.3 3.1 copy-start.43
  10.3 3.1 copy-start.44
  10.3 3.1 copy-start.45
  10.3 3.1 copy-start.46
  10.3 3.4 copy-start.35
  59.9 148.2 %copy-start.14 = (bf16[384,2048]{1,0:T(8,128)(2,1)S(1)}, bf16[384,2048]{1,0:T(8,128)(2,1)}, u32[]{:S(2)}) copy-start(bf16[384,2048]{1,0:T(8,128)(2,1)} %param.19) | copy-start | bytes 4718596
  208.1 65.3 %collective-permute-start = (bf16[384,2048]{1,0:T(8,128)(2,1)S(1)}, bf16[384,2048]{1,0:T(8,128)(2,1)}, u32[]{:S(2)}, u32[]{:S(2)}) collective-permute-start(bf16[384,2048]{1,0:T(8,128)(2,1)S(1)} %copy-done.14), channel_id=1, source_target_pairs={{0,1},{1,2},{2,3},{4,5},{5,6},{6,7},{8,9},{9,10},{10,11},{12,13},{... | collective-permute-start | bytes 4718600 | tf_op jit(solution)/shard_map/ppermute | solution.py:818
  211.8 61.6 %collective-permute-start.1 = (bf16[384,2048]{1,0:T(8,128)(2,1)S(1)}, bf16[384,2048]{1,0:T(8,128)(2,1)}, u32[]{:S(2)}, u32[]{:S(2)}) collective-permute-start(bf16[384,2048]{1,0:T(8,128)(2,1)S(1)} %copy-done.14), channel_id=1, source_target_pairs={{1,0},{2,1},{3,2},{5,4},{6,5},{7,6},{9,8},{10,9},{11,10},{13,12},{... | collective-permute-start | bytes 4718600 | tf_op jit(solution)/shard_map/ppermute | solution.py:819
  217.5 16.8 %copy-start.4 = (f32[2048]{0:T(1024)}, f32[2048]{0:T(1024)S(1)}, u32[]{:S(2)}) copy-start(f32[2048]{0:T(1024)S(1)} %get-tuple-element.165) | copy-start | bytes 24580
  234.3 7.4 copy-start.2
  254.2 15.5 %copy-start.40 = (s32[1,1536]{1,0:T(1,128)S(1)}, s32[1,1536]{1,0:T(1,128)}, u32[]{:S(2)}) copy-start(s32[1,1536]{1,0:T(1,128)} %param.32) | copy-start | bytes 18436
  254.2 15.6 %copy-start.37 = (s32[1,1536]{1,0:T(1,128)S(1)}, s32[1,1536]{1,0:T(1,128)}, u32[]{:S(2)}) copy-start(s32[1,1536]{1,0:T(1,128)} %param.33) | copy-start | bytes 18436
  254.2 15.7 %copy-start.41 = (s32[1,1536]{1,0:T(1,128)S(1)}, s32[1,1536]{1,0:T(1,128)}, u32[]{:S(2)}) copy-start(s32[1,1536]{1,0:T(1,128)} %param.34) | copy-start | bytes 18436
  254.2 15.7 %copy-start.36 = (s32[1,1536,8]{1,2,0:T(8,128)S(1)}, s32[1,1536,8]{1,2,0:T(8,128)}, u32[]{:S(2)}) copy-start(s32[1,1536,8]{1,2,0:T(8,128)} %param.35) | copy-start | bytes 147460
  272.7 11.5 copy-start.30
  273.4 39.4 %collective-permute-start.2 = (bf16[384,2048]{1,0:T(8,128)(2,1)}, bf16[384,2048]{1,0:T(8,128)(2,1)}, u32[]{:S(2)}, u32[]{:S(2)}) collective-permute-start(bf16[384,2048]{1,0:T(8,128)(2,1)} %collective-permute-done), channel_id=1, source_target_pairs={{1,2},{2,3},{5,6},{6,7},{9,10},{10,11},{13,14},{14,15},{17,18},{18... | collective-permute-start | bytes 4718600 | tf_op jit(solution)/shard_map/ppermute | solution.py:818
  278.3 35.4 %collective-permute-start.3 = (bf16[384,2048]{1,0:T(8,128)(2,1)}, bf16[384,2048]{1,0:T(8,128)(2,1)}, u32[]{:S(2)}, u32[]{:S(2)}) collective-permute-start(bf16[384,2048]{1,0:T(8,128)(2,1)} %collective-permute-done.1), channel_id=1, source_target_pairs={{1,0},{2,1},{5,4},{6,5},{9,8},{10,9},{13,12},{14,13},{17,16},{18,1... | collective-permute-start | bytes 4718600 | tf_op jit(solution)/shard_map/ppermute | solution.py:819
  311.7 1.1 copy-start
  312.8 60.6 %copy-start.18 = (bf16[384,2048]{1,0:T(8,128)(2,1)S(1)}, bf16[384,2048]{1,0:T(8,128)(2,1)}, u32[]{:S(2)}) copy-start(bf16[384,2048]{1,0:T(8,128)(2,1)} %x.7) | copy-start | bytes 4718596
  313.7 67.9 %collective-permute-start.4 = (bf16[384,2048]{1,0:T(8,128)(2,1)}, bf16[384,2048]{1,0:T(8,128)(2,1)}, u32[]{:S(2)}, u32[]{:S(2)}) collective-permute-start(bf16[384,2048]{1,0:T(8,128)(2,1)} %collective-permute-done.2), channel_id=1, source_target_pairs={{2,3},{6,7},{10,11},{14,15},{18,19},{22,23},{26,27},{30,31}} | collective-permute-start | bytes 4718600 | tf_op jit(solution)/shard_map/ppermute | solution.py:818
  315.5 74.0 %collective-permute-start.5 = (bf16[384,2048]{1,0:T(8,128)(2,1)}, bf16[384,2048]{1,0:T(8,128)(2,1)}, u32[]{:S(2)}, u32[]{:S(2)}) collective-permute-start(bf16[384,2048]{1,0:T(8,128)(2,1)} %collective-permute-done.3), channel_id=1, source_target_pairs={{1,0},{5,4},{9,8},{13,12},{17,16},{21,20},{25,24},{29,28}} | collective-permute-start | bytes 4718600 | tf_op jit(solution)/shard_map/ppermute | solution.py:819
  379.9 3.2 copy-start.8
  383.2 3.2 copy-start.15
  583.8 261.1 %reduce-scatter.7.cloned.1.call-start = ((), (), s32[]{:S(2)}) async-start(), calls=%async_computation.10 | async-start | bytes 18874368 | tf_op jit(solution)/shard_map/reduce_scatter | solution.py:981
  584.4 443.4 %reduce-scatter.11.cloned.1.call-start = ((), (), s32[]{:S(2)}) async-start(), calls=%async_computation.12 | async-start | bytes 18874368 | tf_op jit(solution)/shard_map/reduce_scatter | solution.py:984
  666.5 474.2 %reduce-scatter.13.cloned.1.call-start = ((), (), s32[]{:S(2)}) async-start(), calls=%async_computation.13 | async-start | bytes 9437184 | tf_op jit(solution)/shard_map/reduce_scatter | solution.py:985
  666.8 0.7 copy-start.31
  666.8 1.9 copy-start.3
  666.8 2.2 copy-start.38
  666.8 2.2 copy-start.39
  669.7 165.4 %all-to-all-start = ((f32[4,4,384]{2,0,1:T(4,128)}), f32[4,4,384]{2,0,1:T(4,128)S(1)}, u32[]{:S(2)}, u32[]{:S(2)}) async-start(f32[4,4,384]{2,0,1:T(4,128)} %bitcast.40), calls=%async_computation | async-start | bytes 49152 | tf_op jit(solution)/shard_map/all_to_all | solution.py:987
  694.6 559.9 %reduce-scatter.17.cloned.1.call-start = ((), (), s32[]{:S(2)}) async-start(), calls=%async_computation.15 | async-start | bytes 2359296 | tf_op jit(solution)/shard_map/reduce_scatter | solution.py:1001
  695.8 139.4 %copy-start.13 = (bf16[384,2048]{1,0:T(8,128)(2,1)S(1)}, bf16[384,2048]{1,0:T(8,128)(2,1)}, u32[]{:S(2)}) copy-start(bf16[384,2048]{1,0:T(8,128)(2,1)} %multiply_convert_fusion.2.x) | copy-start | bytes 4718596
  836.5 6.3 copy-start.9
  836.5 6.3 copy-start.16
  841.0 1.8 copy-start.11
  1019.6 8.2 copy-start.1
  1055.4 6.1 copy-start.6
  1055.4 23.5 %copy-start.26 = (bf16[1536,512]{1,0:T(8,128)(2,1)S(1)}, bf16[1536,512]{1,0:T(8,128)(2,1)}, u32[]{:S(2)}) copy-start(bf16[1536,512]{1,0:T(8,128)(2,1)} %get-tuple-element.67.x) | copy-start | bytes 4718596
  1086.4 6.7 copy-start.7
  1093.0 16.4 %copy-start.25 = (bf16[1536,512]{1,0:T(8,128)(2,1)}, bf16[1536,512]{1,0:T(8,128)(2,1)S(1)}, u32[]{:S(2)}) copy-start(bf16[1536,512]{1,0:T(8,128)(2,1)S(1)} %get-tuple-element.180) | copy-start | bytes 4718596
  1093.0 173.6 %reduce-scatter.15.cloned.1.call-start = ((), (), s32[]{:S(2)}) async-start(), calls=%async_computation.14 | async-start | bytes 7667712 | tf_op jit(solution)/shard_map/reduce_scatter | solution.py:1034
  1111.6 0.8 copy-start.23
  1112.4 15.1 %copy-start.21 = (bf16[2048,16]{1,0:T(8,128)(2,1)S(1)}, bf16[2048,16]{1,0:T(8,128)(2,1)}, u32[]{:S(2)}) copy-start(bf16[2048,16]{1,0:T(8,128)(2,1)} %copy.165) | copy-start | bytes 196612
  1112.4 15.1 %copy-start.22 = (bf16[2048,1]{1,0:T(8,128)(2,1)S(1)}, bf16[2048,1]{1,0:T(8,128)(2,1)}, u32[]{:S(2)}) copy-start(bf16[2048,1]{1,0:T(8,128)(2,1)} %stack.50) | copy-start | bytes 12292
  1140.8 99.1 %copy-start.5 = (f32[2048]{0:T(1024)S(1)}, f32[2048]{0:T(1024)}, u32[]{:S(2)}) copy-start(f32[2048]{0:T(1024)} %copy-done.4) | copy-start | bytes 24580
  1140.8 99.1 %copy-start.19 = (bf16[384,2048]{1,0:T(8,128)(2,1)S(1)}, bf16[384,2048]{1,0:T(8,128)(2,1)}, u32[]{:S(2)}) copy-start(bf16[384,2048]{1,0:T(8,128)(2,1)} %x.7) | copy-start | bytes 4718596
  1239.9 5.1 copy-start.24
  1242.2 3.9 copy-start.29
  1245.0 1.5 copy-start.28
  1245.0 3.9 copy-start.17
  1245.0 3.9 copy-start.20
  1246.5 3.7 copy-start.10
  1246.5 4.7 copy-start.12
  1254.5 11.3 collective-permute-start.6
  1290.0 6.3 copy-start.27
Sparse Core Ops, SparseCore 0:
  9.9 121.8 all-gather.3
  133.7 103.4 all-gather.5
  239.1 89.8 all-gather.7
  584.0 87.5 reduce-scatter.8
  675.4 115.9 reduce-scatter.6
  795.2 115.9 reduce-scatter.10
  915.0 71.2 reduce-scatter.12
  1093.1 41.6 reduce-scatter.16
  1139.8 64.9 reduce-scatter.14

commit v5 on v4

--- a/solution.py
+++ b/solution.py
@@ -304,7 +304,6 @@
         self.p, self.n, self.rows, self.part, self.make = p, n, rows, part, make
         self.from_left, self.from_right = boxes
         self.to_right, self.to_left, self.recv_r, self.recv_l = sems
-        self.order = [(s, c) for s in range(n - 1) for c in range(self.pieces)]
 
     def at(self, j, c):
         size = self.rows // self.pieces
@@ -322,44 +321,36 @@
         total = self.at(j, c)[...].astype(F32) + box[j * self.pieces + c].astype(F32)
         self.at(j, c)[...] = total.astype(BF16)
 
-    def make_step(self, s):
-        j, k = self.n - 1 - s, s
-        pl.when(j > self.p)(lambda: self.make(j))
-        pl.when(k < self.p)(lambda: self.make(k))
-
-    def piece(self, s, c):
+    def pass_on(self, m, count, ends, shard, copy, box):
+        @pl.when((m >= 0) & (m < count))
+        def _():
+            j, c = shard(lax.div(m, self.pieces)), lax.rem(m, self.pieces)
+            pl.when(c == 0)(lambda: self.make(j))
+
+            @pl.when(ends)
+            def _():
+                copy(j, c).wait_recv()
+                self.add(j, c, box)
+
+            @pl.when(m >= self.depth)
+            def _():
+                before = m - self.depth
+                copy(shard(lax.div(before, self.pieces)), lax.rem(before, self.pieces)).wait_send()
+
+            copy(j, c).start()
+
+    def tick(self, t):
         p, n = self.p, self.n
-        j, k = n - 1 - s, s
-        m = s * self.pieces + c
-
-        @pl.when(j > p)
-        def _():
-            @pl.when(p > 0)
-            def _():
-                self.right(j, c).wait_recv()
-                self.add(j, c, self.from_left)
-
-            if m >= self.depth:
-                s0, c0 = self.order[m - self.depth]
-                self.right(n - 1 - s0, c0).wait_send()
-            self.right(j, c).start()
-
-        @pl.when(k < p)
-        def _():
-            @pl.when(p < n - 1)
-            def _():
-                self.left(k, c).wait_recv()
-                self.add(k, c, self.from_right)
-
-            if m >= self.depth:
-                s0, c0 = self.order[m - self.depth]
-                self.left(s0, c0).wait_send()
-            self.left(k, c).start()
-
-    def step(self, s):
-        self.make_step(s)
-        for c in range(self.pieces):
-            self.piece(s, c)
+        to_right = lambda: self.pass_on(t - p, (n - 1 - p) * self.pieces, p > 0, lambda s: n - 1 - s, self.right, self.from_left)
+        to_left = lambda: self.pass_on(t - (n - 1 - p), p * self.pieces, p < n - 1, lambda s: s, self.left, self.from_right)
+        to_right()
+        to_left()
+
+    def run(self, beside=lambda t: None):
+        @pl.loop(0, (self.n - 1) * self.pieces + self.n - 1)
+        def _(t):
+            beside(t)
+            self.tick(t)
 
     def finish(self, out, base=None):
         p, n, size = self.p, self.n, self.rows // self.pieces
@@ -381,11 +372,16 @@
                 out[here] = self.at(p, c)[...]
             else:
                 out[here] = (base[here].astype(F32) + self.at(p, c)[...].astype(F32)).astype(out.dtype)
-        for m, (s, c) in enumerate(self.order):
-            pl.when((n - 1 - s > p) & (m >= (n - 1 - p) * self.pieces - self.depth))(
-                lambda s=s, c=c: self.right(n - 1 - s, c).wait_send()
-            )
-            pl.when((s < p) & (m >= p * self.pieces - self.depth))(lambda s=s, c=c: self.left(s, c).wait_send())
+        for i in range(self.depth):
+            for count, shard, copy in (
+                ((n - 1 - p) * self.pieces, lambda s: n - 1 - s, self.right),
+                (p * self.pieces, lambda s: s, self.left),
+            ):
+                m = count - 1 - i
+
+                @pl.when(m >= 0)
+                def _():
+                    copy(shard(lax.div(m, self.pieces)), lax.rem(m, self.pieces)).wait_send()
 
 
 def rows_of(ref, rows):
@@ -439,18 +435,19 @@
         locals_[a].start()
         for k in range(3):
             all_moves[a][k]().start()
+    line.step(1)
     for a in range(count):
         for k in (0, 1):
             all_moves[a][k]().wait_recv()
         for k in (3, 4, 5, 6):
             all_moves[a][k]().start()
-    line.step(1)
-    for a in range(count):
-        for k in (3, 4):
-            all_moves[a][k]().wait_recv()
-        all_moves[a][7]().start()
     for s in range(2, n):
         line.step(s)
+        if s == 2:
+            for a in range(count):
+                for k in (3, 4):
+                    all_moves[a][k]().wait_recv()
+                all_moves[a][7]().start()
     for a in range(count):
         locals_[a].wait()
         for k in (2, 5, 6, 7):
@@ -534,8 +531,7 @@
 def rs_kernel(n, rows, part, out, left_box, right_box, *sems):
     p = greet_line(n)
     line = Reduce(p, n, rows, part, lambda j: None, (left_box, right_box), sems)
-    for s in range(n - 1):
-        line.step(s)
+    line.run()
     line.finish(out)
 
 
@@ -571,8 +567,7 @@
     p = greet_line(n)
     make = combine(part, rows, slot, None, (low, high))
     line = Reduce(p, n, rows, part, make, (left_box, right_box), sems)
-    for s in range(n - 1):
-        line.step(s)
+    line.run()
     line.finish(out)
 
 
@@ -595,22 +590,20 @@
     own.start()
     size = rows // Reduce.pieces
     piece = lambda j, c: all_out.at[pl.ds(pl.multiple_of(j * rows + c * size, size), size)]
-    gather = Gather(p, n, lambda c: x.at[pl.ds(c * size, size)], piece, sems[:3], Reduce.pieces)
+    gather = Gather(p, n, lambda c: x.at[pl.ds(pl.multiple_of(c * size, size), size)], piece, sems[:3], Reduce.pieces)
     make = combine(part, rows, slot, weight, (low, high))
     line = Reduce(p, n, rows, part, make, (left_box, right_box), sems[3:7])
-    for s in range(n):
-        if s == 0:
-            gather.start(0)
-            gather.start(1)
-        if s < n - 1:
-            line.make_step(s)
-        for c in range(Reduce.pieces):
-            if s:
-                gather.step(s, c=c)
-            elif c > 1:
-                gather.start(c)
-            if s < n - 1:
-                line.piece(s, c)
+    gather.start(0)
+    gather.start(1)
+
+    def beside(t):
+        pl.when(t + 2 < Reduce.pieces)(lambda: gather.start(t + 2))
+
+        @pl.when((t >= 1) & (t - 1 < (n - 1) * Reduce.pieces))
+        def _():
+            gather.step(lax.div(t - 1, Reduce.pieces) + 1, c=lax.rem(t - 1, Reduce.pieces))
+
+    line.run(beside)
     line.finish(out, base)
     own.wait()
     gather.finish()
@@ -833,13 +826,21 @@
     return lax.dynamic_slice_in_dim(line, start, ways * rows, axis=0)
 
 
-def norm_qkv_kernel(columns, x, gain, weight, out, normed, inverse):
+def norm_qkv_kernel(columns, x, gain, weight, out, normed, inverse, squares):
     values = x[...].astype(F32)
     inv = lax.rsqrt(jnp.mean(values * values, axis=1, keepdims=True) + EPS)
     rows = (values * inv * gain[...]).astype(BF16)
     inverse[...] = inv
     normed[...] = rows
-    out[...] = plain(rows, weight[:, :columns])
+    result = plain(rows, weight[:, :columns])
+    out[...] = result
+    third = columns // 3
+    lanes = lax.broadcasted_iota(jnp.int32, (x.shape[0], 128), 1)
+    sums = jnp.zeros((x.shape[0], 128), F32)
+    for i in range(2):
+        part = result[:, i * third : (i + 1) * third]
+        sums = jnp.where(lanes == i, jnp.sum(part * part, axis=1, keepdims=True), sums)
+    squares[...] = sums.T[:8]
 
 
 def norm_qkv(x, gain, weight, columns):
@@ -853,11 +854,12 @@
             pl.BlockSpec((1, width), lambda i: (0, 0)),
             pl.BlockSpec(weight.shape, lambda i: (0, 0), pipeline_mode=pl.Buffered(1)),
         ],
-        out_specs=[tile(columns), tile(width), tile(1)],
+        out_specs=[tile(columns), tile(width), tile(1), pl.BlockSpec((8, NTILE), lambda i: (0, i))],
         out_shape=[
             jax.ShapeDtypeStruct((tokens, columns), F32),
             jax.ShapeDtypeStruct((tokens, width), BF16),
             jax.ShapeDtypeStruct((tokens, 1), F32),
+            jax.ShapeDtypeStruct((8, tokens), F32),
         ],
         compiler_params=pltpu.CompilerParams(vmem_limit_bytes=48 * 2**20),
     )(x, gain, weight)
@@ -931,6 +933,9 @@
     my_gains = lax.dynamic_slice_in_dim(small[:, 1:3], z * cols, cols, axis=0).astype(F32)
     gain_q, gain_k = my_gains[:, 0][None], my_gains[:, 1][None]
     out_mine = lax.dynamic_slice_in_dim(out_full, z * cols, cols, axis=0)
+    tokens_all, gate_weight, up_weight, down_weight = lax.optimization_barrier(
+        (tokens_all, gate_weight, up_weight, down_weight)
+    )
     gate_full = lax.all_gather(gate_weight, "dp", axis=1, tiled=True)
     up_full = lax.all_gather(up_weight, "dp", axis=1, tiled=True)
     down_full = lax.all_gather(down_weight, "dp", axis=1, tiled=True)
@@ -953,17 +958,16 @@
     slot_shards = my_slot.T.reshape(experts_here, ways, tok_dev).transpose(1, 0, 2)
     slot_cols = my_slot.reshape(ways, tok_dev, experts_here)
 
-    qkv, normed, inverse_in = norm_qkv(tokens_all, attend_gain[None], dense, 3 * cols)
-    squares = jnp.sum(jnp.square(qkv[:, : 2 * cols]).reshape(GTOK, 2, cols), axis=-1)
-    squares = sum_z(jnp.pad(squares.T, ((0, 6), (0, 0))), ways, 3)
+    qkv, normed, inverse_in, squares = norm_qkv(tokens_all, attend_gain[None], dense, 3 * cols)
+    squares = sum_z(squares, ways, 3)
     up, down, squares = later(sent, squares)
     sent = hops(up, down, steps[1] - steps[0], ways)
     inv_q = lax.rsqrt(squares[0] / width + EPS)[:, None]
     inv_k = lax.rsqrt(squares[1] / width + EPS)[:, None]
     q_rot, k_rot, v_b, mixed_heads, lse = attend(order, qkv, inv_q, inv_k, gain_q, gain_k, cos, sin)
-    up, down, mixed_heads = later(sent, mixed_heads)
+    mixed = a2a_z(mixed_heads, ways, 4)
+    up, down, mixed = later(sent, mixed)
     grad_all = line_up(*hops(up, down, ways - steps[1], ways), ways)
-    mixed = a2a_z(mixed_heads, ways, 4)
     own_f = tokens.astype(F32)
     resid = own_f + plain(mixed, out_full)
     mix_inverse = lax.rsqrt(jnp.mean(resid * resid, axis=-1, keepdims=True) + EPS)

time: 1310 us -> 1200 us (0.916)
  Pallas kernels: 1040 us -> 941 us
  waiting for transfers between devices: 4.61 us -> 24.5 us
  other arithmetic: 60.4 us -> 47 us
    pallas_call x1, Pallas kernels: 144 us -> 108 us  [ag_z(): pl.pallas_call(functools.partial(ag_kernel, n, rows), out_shape=[grown(x,...]
    pallas_call x1, Pallas kernels: 139 us -> 114 us  [combine_z(): pl.pallas_call(functools.partial(combine_kernel, n, rows), out_shape=jax....]
    pallas_call x1, Pallas kernels: 175 us -> 151 us  [gather_and_combine(): pl.pallas_call(functools.partial(both_kernel, n, rows), out_shape=[jax.Sh...]
    pallas_call x1, Pallas kernels: 54.5 us -> 35.4 us  [a2a_z(): pl.pallas_call(functools.partial(a2a_kernel, n, rows, cols), out_shape=ja...]
    ppermute x3, waiting for transfers between devices: 0.88 us -> 16.8 us  [hops(): lax.ppermute(down[-1], 'expert', [(i + 1, i) for i in range(ways - h)])]
  transfers between devices with their start and end apart: 17 -> 17, of which waited for: 2 -> 3; matrix products, arithmetic and copies ran while one was open for 14% -> 12% of each run, Pallas kernels for 72% -> 57%
where the time goes in v5:
time: 1200 us; the launch traced here: 1190 us
  Pallas kernels  941 us (78%)
  local copies, waits for them, and re-layouts  64.5 us (5%)
  matrix products  60.7 us (5%)
  other arithmetic  47 us (4%)
  starting transfers between devices  40.9 us (3%)
  waiting for transfers between devices  24.5 us (2%)
  between operations  15 us (1%)
    pallas_call x2, Pallas kernels, experts(): pl.pallas_call(expert_kernel, grid=(count, steps), in_specs=[line, line,...  164 us
    pallas_call x1, Pallas kernels, gather_and_combine(): pl.pallas_call(functools.partial(both_kernel, n, rows), out_shape=[jax.Sh...  151 us
    pallas_call x1, Pallas kernels, combine_z(): pl.pallas_call(functools.partial(combine_kernel, n, rows), out_shape=jax....  114 us
    pallas_call x1, Pallas kernels, gather_rows(): pl.pallas_call(functools.partial(gather_kernel, n, rows), out_shape=[jax....  108 us
    pallas_call x1, Pallas kernels, ag_z(): pl.pallas_call(functools.partial(ag_kernel, n, rows), out_shape=[grown(x,...  108 us
    pallas_call x1, Pallas kernels, rs_z(): pl.pallas_call(functools.partial(rs_kernel, n, rows), out_shape=jax.Shape...  99.3 us
    pallas_call x2, Pallas kernels, exchange_z(): pl.pallas_call(functools.partial(exchange_kernel, n, x.shape[0] // n), ou...  65 us
    pallas_call x1, Pallas kernels, a2a_z(): pl.pallas_call(functools.partial(a2a_kernel, n, rows, cols), out_shape=ja...  35.4 us
  transfers between devices with their start and end apart: 17, of which 3 were waited for; matrix products, arithmetic and copies ran while one was open for 12% of the time, Pallas kernels for 57%

profile of v5, /device:TPU:10, one launch (start us, length us, event | category | flops | bytes accessed | tf_op | source)
XLA Modules:
  0.0 1193.2 jit_solution(12214678361541167731)
XLA Ops:
  12.0 1.8 pad_maximum_fusion.4
  14.4 1.4 pad_maximum_fusion.3.x
  15.8 44.6 %shard_map.281 = bf16[256,3712]{1,0:T(8,128)(2,1)} custom-call(bf16[256,3712]{1,0:T(8,128)(2,1)} %pad_maximum_fusion.3.x), custom_call_target="tpu_custom_call" | custom-call | tf_op jit(solution)/shard_map/pallas_call | solution.py:672
  60.4 2.3 slice.101.rest_1_
  62.7 2.1 slice.100.rest_0_
  64.9 108.3 %shard_map.282 = (bf16[1536,2048]{1,0:T(8,128)(2,1)}, bf16[2048,1664]{1,0:T(8,128)(2,1)}, bf16[2048,2048]{1,0:T(8,128)(2,1)}) custom-call(bf16[384,2048]{1,0:T(8,128)(2,1)} %x.5, bf16[256,1664]{1,0:T(8,128)(2,1)} %slice.100.rest_0_, bf16[256,2048]{1,0:T(8,128)(2,1)} %slice.101.rest_1_), custom_call_target="tpu_custom_call" | custom-call | tf_op jit(solution)/shard_map/pallas_call | solution.py:465
  174.7 3.4 collective-permute-start
  178.1 3.6 collective-permute-start.1
  181.7 1.4 slice.107
  183.1 1.9 slice.111.small
  185.0 1.8 convert_reduce_fusion
  186.9 16.7 %shard_map.283 = (f32[1536,1536]{1,0:T(8,128)}, bf16[1536,2048]{1,0:T(8,128)(2,1)}, f32[1536,1]{1,0:T(8,128)S(1)}, f32[8,1536]{1,0:T(8,128)S(1)}) custom-call(bf16[1536,2048]{1,0:T(8,128)(2,1)} %get-tuple-element.66.x, f32[1,2048]{1,0:T(1,128)S(1)} %bitcast.90, bf16[2048,1664]{1,0:T(8,128)(2,1)} %get-tuple-element.67.weight), custom_call_target="tpu_custom_call" | custom-call | tf_op jit(solution)/shard_map/pallas_call | solution.py:849
  205.2 14.5 %shard_map.284 = f32[8,1536]{1,0:T(8,128)} custom-call(f32[8,1536]{1,0:T(8,128)} %copy-done.6), custom_call_target="tpu_custom_call" | custom-call | tf_op jit(solution)/shard_map/pallas_call | solution.py:694
  221.2 1.6 fusion
  223.5 3.8 collective-permute-start.2
  227.3 2.1 collective-permute-start.3
  229.8 2.8 fusion.17
  234.7 25.9 %shard_map.285 = (bf16[1536,512]{1,0:T(8,128)(2,1)S(1)}, bf16[1536,512]{1,0:T(8,128)(2,1)}, bf16[1536,512]{1,0:T(8,128)(2,1)}, bf16[1536,512]{1,0:T(8,128)(2,1)}, f32[1536,512]{1,0:T(8,128)}) custom-call(s32[12]{0:T(128)S(1)} %select_reduce_fusion.1.order, f32[1536,1536]{1,0:T(8,128)} %get-tuple-element.71.q_pre.k_pre.v_pre, ...), custom_call_target="tpu_custom_call" | custom-call | tf_op jit(solution)/shard_map/pallas_call | solution.py:110
  261.7 35.4 %shard_map.286 = bf16[384,2048]{1,0:T(8,128)(2,1)} custom-call(bf16[1536,512]{1,0:T(8,128)(2,1)} %get-tuple-element.73.x), custom_call_target="tpu_custom_call" | custom-call | tf_op jit(solution)/shard_map/pallas_call | solution.py:645
  298.0 1.4 collective-permute-start.5
  299.4 6.5 multiply_reduce_fusion.7
  305.9 1.7 multiply_convert_fusion.2.x
  307.8 1.3 copy-done.9
  309.0 1.9 constant_dynamic-update-slice_fusion.5
  310.9 1.5 constant_dynamic-update-slice_fusion.4
  312.6 1.5 constant_dynamic-update-slice_fusion.2
  314.1 1.5 constant_dynamic-update-slice_fusion.1
  315.6 16.8 %collective-permute-done.5 = bf16[384,2048]{1,0:T(8,128)(2,1)S(1)} collective-permute-done((bf16[384,2048]{1,0:T(8,128)(2,1)}, bf16[384,2048]{1,0:T(8,128)(2,1)S(1)}, u32[]{:S(2)}, u32[]{:S(2)}) %collective-permute-start.5) | collective-permute-done | bytes 1572896 | tf_op jit(solution)/shard_map/ppermute | solution.py:812
  332.6 3.3 constant_dynamic-slice_fusion.1.grads
  335.9 108.4 %shard_map.287 = (f32[1536,128]{1,0:T(8,128)}, bf16[4,768,2048]{2,1,0:T(8,128)(2,1)}, bf16[4,768,2048]{2,1,0:T(8,128)(2,1)}) custom-call(bf16[384,2048]{1,0:T(8,128)(2,1)} %multiply_convert_fusion.2.x, s32[4,4,384]{2,1,0:T(4,128)} %bitcast.107, bf16[2048,128]{1,0:T(8,128)(2,1)} %slice.111.small, bf16[1536,2048]{1,0:T(8,128)(2,1)} %constant_dynamic-slice_fusion.1.grads), custom_call_target="tpu_custom_call" | custom-call | tf_op jit(solution)/shard_map/pallas_call | solution.py:515
  444.3 1.4 copy.153
  446.8 81.8 %shard_map.288 = (bf16[2,768,2048]{2,1,0:T(8,128)(2,1)}, bf16[2,768,2048]{2,1,0:T(8,128)(2,1)}, f32[2,1,1536]{2,1,0:T(1,128)}, bf16[8,2,2,256,1024]{4,3,2,1,0:T(8,128)(2,1)}, bf16[8,2,128,2048]{3,2,1,0:T(8,128)(2,1)}) custom-call(s32[4,1,1536]{2,1,0:T(1,128)} %broadcast_in_dim.87.slot, f32[4,1,1536]{2,1,0:T(1,128)} %broadcast_in_dim.88.weight, ...), custom_call_target="tpu_custom_call" | custom-call | tf_op jit(solution)/shard_map/pallas_call | solution.py:774
  529.3 81.8 %shard_map.289 = (bf16[2,768,2048]{2,1,0:T(8,128)(2,1)}, bf16[2,768,2048]{2,1,0:T(8,128)(2,1)}, f32[2,1,1536]{2,1,0:T(1,128)}, bf16[8,2,2,256,1024]{4,3,2,1,0:T(8,128)(2,1)}, bf16[8,2,128,2048]{3,2,1,0:T(8,128)(2,1)}) custom-call(s32[4,1,1536]{2,1,0:T(1,128)} %broadcast_in_dim.87.slot, f32[4,1,1536]{2,1,0:T(1,128)} %broadcast_in_dim.88.weight, ...), custom_call_target="tpu_custom_call" | custom-call | tf_op jit(solution)/shard_map/pallas_call | solution.py:774
  612.1 1.2 copy.151
  614.3 22.6 %all-to-all-start = ((f32[4,4,384]{2,0,1:T(4,128)}), f32[4,4,384]{2,0,1:T(4,128)S(1)}, u32[]{:S(2)}, u32[]{:S(2)}) async-start(f32[4,4,384]{2,0,1:T(4,128)} %bitcast.39), calls=%async_computation | async-start | bytes 49152 | tf_op jit(solution)/shard_map/all_to_all | solution.py:991
  636.9 1.2 copy.155
  638.1 114.0 %shard_map.290 = bf16[384,2048]{1,0:T(8,128)(2,1)} custom-call(s32[4,384,4]{2,1,0:T(8,128)} %bitcast.93, bf16[2,768,2048]{2,1,0:T(8,128)(2,1)} %get-tuple-element.84.low, bf16[2,768,2048]{2,1,0:T(8,128)(2,1)} %get-tuple-element.85.high), custom_call_target="tpu_custom_call" | custom-call | tf_op jit(solution)/shard_map/pallas_call | solution.py:576
  753.5 5.2 multiply_reduce_fusion.1
  758.7 1.4 stack.50
  760.6 2.1 fusion.30.x
  762.8 151.2 %shard_map.291 = (bf16[1536,2048]{1,0:T(8,128)(2,1)}, bf16[384,2048]{1,0:T(8,128)(2,1)}) custom-call(bf16[384,2048]{1,0:T(8,128)(2,1)} %fusion.30.x, s32[4,384,4]{2,1,0:T(8,128)} %bitcast.94, f32[4,384,4]{2,1,0:T(8,128)} %bitcast.99, bf16[2,768,2048]{2,1,0:T(8,128)(2,1)} %get-tuple-element.91.low, bf16[2,768,2048]{2,1,0:T(8,128)(2,1)} %get-tuple-element.92.high, ...), custom_call_target="tpu_custom_call" | custom-call | tf_op jit(solution)/shard_map/pallas_call | solution.py:614
  914.0 8.3 convolution_convert_fusion.2.grad_mixed
  922.3 27.5 %shard_map.292 = (f32[1536,512]{1,0:T(8,128)}, f32[1536,512]{1,0:T(8,128)}, bf16[1536,512]{1,0:T(8,128)(2,1)S(1)}) custom-call(s32[12]{0:T(128)S(1)} %select_reduce_fusion.1.order, bf16[1536,512]{1,0:T(8,128)(2,1)S(1)} %copy-done.1, bf16[1536,512]{1,0:T(8,128)(2,1)} %get-tuple-element.96.k_rot, bf16[1536,512]{1,0:T(8,128)(2,1)} %get-tuple-element.97.v_in, ...), custom_call_target="tpu_custom_call" | custom-call | tf_op jit(solution)/shard_map/pallas_call | solution.py:167
  949.8 6.1 multiply_reduce_fusion.2
  956.6 10.8 shard_map.293
  968.2 7.5 convolution_convert_fusion.1
  975.7 6.6 multiply_convert_fusion.1
  982.4 16.3 %multiply_reduce_fusion = (bf16[2048]{0:T(1024)(128)(2,1)S(1)}, bf16[1536,2048]{1,0:T(8,128)(2,1)}) fusion(bf16[1536,2048]{1,0:T(8,128)(2,1)} %get-tuple-element.66.x, f32[1536]{0:T(1024)S(1)} %reduce.17, bf16[2048,1664]{1,0:T(8,128)(2,1)} %get-tuple-element.67.weight, bf16[1536,512]{1,0:T(8,128)(2,1)S(1)} %copy-done.8, ...), kind=kOutput, calls=%fused_computation | convolution fusion | flops 9693558784 | bytes 23603200 | tf_op jit(solution)/shard_map/dot_general | solution.py:44
  1001.9 15.0 %convolution_convert_fusion = bf16[2048,1536]{1,0:T(8,128)(2,1)} fusion(bf16[1536,2048]{1,0:T(8,128)(2,1)} %get-tuple-element.107, bf16[1536,512]{1,0:T(8,128)(2,1)S(1)} %copy-done.8, bf16[1536,512]{1,0:T(8,128)(2,1)} %get-tuple-element.191, bf16[1536,512]{1,0:T(8,128)(2,1)} %copy-done.26), kind=kOutput, calls=%fused_computation.5 | convolution fusion | flops 9680977920 | bytes 17301504 | tf_op jit(solution)/shard_map/dot_general | solution.py:40
  1017.0 12.0 %concatenate.53 = bf16[2048,1664]{1,0:T(8,128)(2,1)} concatenate(bf16[2048,1536]{1,0:T(8,128)(2,1)} %convolution_convert_fusion, bf16[2048,1]{1,0:T(8,128)(2,1)S(1)} %stack.49, bf16[2048,1]{1,0:T(8,128)(2,1)} %copy-done.24, bf16[2048,1]{1,0:T(8,128)(2,1)} %constant_dynamic-update-slice_fusion.7, bf16[2048,1]{1,0:T(8,128)(2,1)S(1)} %copy-done.23, bf16[2048,16]{1,0:T(8,128)(2,1)S(1)} %copy-done.22, ...), dimensions={1} | concatenate | bytes 13631488 | tf_op jit(solution)/shard_map/concatenate | solution.py:1037
  1030.2 99.3 %shard_map.294 = bf16[384,2048]{1,0:T(8,128)(2,1)} custom-call(bf16[1536,2048]{1,0:T(8,128)(2,1)} %get-tuple-element.106.part), custom_call_target="tpu_custom_call" | custom-call | tf_op jit(solution)/shard_map/pallas_call | solution.py:540
  1129.5 2.3 fusion.8
  1131.8 2.8 slice_bitcast_fusion
  1134.6 1.1 slice_bitcast_fusion.1
  1136.1 2.4 maximum_convert_fusion.2
  1138.5 1.3 copy-done.11
  1140.8 3.3 fusion.11
  1144.1 2.8 collective-permute-start.6
  1146.8 3.8 maximum_convert_fusion.1
  1150.7 2.3 maximum_convert_fusion
  1153.0 4.8 collective-permute-done.6
  1158.6 20.4 %shard_map.295 = bf16[256,1664]{1,0:T(8,128)(2,1)} custom-call(bf16[256,1664]{1,0:T(8,128)(2,1)} %reduce-scatter.15.cloned.1.call-done.x), custom_call_target="tpu_custom_call" | custom-call | tf_op jit(solution)/shard_map/pallas_call | solution.py:672
  1179.0 1.4 convert_bitcast_fusion
  1185.3 1.1 copy.183
  (193 shorter events, 33.7 us)
Async XLA Ops:
  7.2 439.3 %all-gather.4.cloned.1.call-start = ((), (), s32[]{:S(2)}) async-start(), calls=%async_computation.7 | async-start | bytes 18874368 | tf_op jit(solution)/shard_map/all_gather | solution.py:939
  9.9 4.1 copy-start.40
  9.9 4.1 copy-start.41
  9.9 4.1 copy-start.42
  10.0 4.1 copy-start.43
  10.0 4.1 copy-start.44
  10.0 4.3 copy-start.33
  173.2 1.6 copy-start.15
  173.2 273.3 %all-gather.6.cloned.1.call-start = ((), (), s32[]{:S(2)}) async-start(), calls=%async_computation.8 | async-start | bytes 18874368 | tf_op jit(solution)/shard_map/all_gather | solution.py:940
  173.9 272.9 %all-gather.8.cloned.1.call-start = ((), (), s32[]{:S(2)}) async-start(), calls=%async_computation.9 | async-start | bytes 18874368 | tf_op jit(solution)/shard_map/all_gather | solution.py:941
  174.7 588.1 %reduce-scatter.9.cloned.1.call-start = ((), (), s32[]{:S(2)}) async-start(), calls=%async_computation.11 | async-start | bytes 9437184 | tf_op jit(solution)/shard_map/reduce_scatter | solution.py:986
  174.7 48.7 %collective-permute-start = (bf16[384,2048]{1,0:T(8,128)(2,1)S(1)}, bf16[384,2048]{1,0:T(8,128)(2,1)}, u32[]{:S(2)}, u32[]{:S(2)}) collective-permute-start(bf16[384,2048]{1,0:T(8,128)(2,1)S(1)} %copy-done.15), channel_id=1, source_target_pairs={{0,1},{1,2},{2,3},{4,5},{5,6},{6,7},{8,9},{9,10},{10,11},{12,13},{... | collective-permute-start | bytes 4718600 | tf_op jit(solution)/shard_map/ppermute | solution.py:811
  178.1 45.3 %collective-permute-start.1 = (bf16[384,2048]{1,0:T(8,128)(2,1)S(1)}, bf16[384,2048]{1,0:T(8,128)(2,1)}, u32[]{:S(2)}, u32[]{:S(2)}) collective-permute-start(bf16[384,2048]{1,0:T(8,128)(2,1)S(1)} %copy-done.15), channel_id=1, source_target_pairs={{1,0},{2,1},{3,2},{5,4},{6,5},{7,6},{9,8},{10,9},{11,10},{13,12},{... | collective-permute-start | bytes 4718600 | tf_op jit(solution)/shard_map/ppermute | solution.py:812
  186.9 16.8 %copy-start.4 = (f32[2048]{0:T(1024)}, f32[2048]{0:T(1024)S(1)}, u32[]{:S(2)}) copy-start(f32[2048]{0:T(1024)S(1)} %get-tuple-element.175) | copy-start | bytes 24580
  186.9 32.9 %copy-start.38 = (s32[1,1536]{1,0:T(1,128)S(1)}, s32[1,1536]{1,0:T(1,128)}, u32[]{:S(2)}) copy-start(s32[1,1536]{1,0:T(1,128)} %param.32) | copy-start | bytes 18436
  186.9 33.0 %copy-start.35 = (s32[1,1536]{1,0:T(1,128)S(1)}, s32[1,1536]{1,0:T(1,128)}, u32[]{:S(2)}) copy-start(s32[1,1536]{1,0:T(1,128)} %param.33) | copy-start | bytes 18436
  186.9 33.1 %copy-start.39 = (s32[1,1536]{1,0:T(1,128)S(1)}, s32[1,1536]{1,0:T(1,128)}, u32[]{:S(2)}) copy-start(s32[1,1536]{1,0:T(1,128)} %param.34) | copy-start | bytes 18436
  186.9 33.1 %copy-start.34 = (s32[1,1536,8]{1,2,0:T(8,128)S(1)}, s32[1,1536,8]{1,2,0:T(8,128)}, u32[]{:S(2)}) copy-start(s32[1,1536,8]{1,2,0:T(8,128)} %param.35) | copy-start | bytes 147460
  203.6 0.9 copy-start.2
  204.6 0.6 copy-start.6
  222.8 10.4 copy-start.31
  223.5 73.7 %collective-permute-start.2 = (bf16[384,2048]{1,0:T(8,128)(2,1)}, bf16[384,2048]{1,0:T(8,128)(2,1)}, u32[]{:S(2)}, u32[]{:S(2)}) collective-permute-start(bf16[384,2048]{1,0:T(8,128)(2,1)} %collective-permute-done), channel_id=1, source_target_pairs={{1,2},{2,3},{5,6},{6,7},{9,10},{10,11},{13,14},{14,15},{17,18},{18... | collective-permute-start | bytes 4718600 | tf_op jit(solution)/shard_map/ppermute | solution.py:811
  227.3 69.9 %collective-permute-start.3 = (bf16[384,2048]{1,0:T(8,128)(2,1)}, bf16[384,2048]{1,0:T(8,128)(2,1)}, u32[]{:S(2)}, u32[]{:S(2)}) collective-permute-start(bf16[384,2048]{1,0:T(8,128)(2,1)} %collective-permute-done.1), channel_id=1, source_target_pairs={{1,0},{2,1},{5,4},{6,5},{9,8},{10,9},{13,12},{14,13},{17,16},{18,1... | collective-permute-start | bytes 4718600 | tf_op jit(solution)/shard_map/ppermute | solution.py:812
  260.6 1.1 copy-start
  261.7 37.6 %copy-start.19 = (bf16[384,2048]{1,0:T(8,128)(2,1)S(1)}, bf16[384,2048]{1,0:T(8,128)(2,1)}, u32[]{:S(2)}) copy-start(bf16[384,2048]{1,0:T(8,128)(2,1)} %x.5) | copy-start | bytes 4718596
  297.2 10.4 collective-permute-start.4
  298.0 34.5 %collective-permute-start.5 = (bf16[384,2048]{1,0:T(8,128)(2,1)}, bf16[384,2048]{1,0:T(8,128)(2,1)S(1)}, u32[]{:S(2)}, u32[]{:S(2)}) collective-permute-start(bf16[384,2048]{1,0:T(8,128)(2,1)} %collective-permute-done.3), channel_id=1, source_target_pairs={{1,0},{5,4},{9,8},{13,12},{17,16},{21,20},{25,24},{29,28}} | collective-permute-start | bytes 4718600 | tf_op jit(solution)/shard_map/ppermute | solution.py:812
  305.9 3.1 copy-start.9
  309.0 3.4 copy-start.16
  528.6 234.2 %reduce-scatter.7.cloned.1.call-start = ((), (), s32[]{:S(2)}) async-start(), calls=%async_computation.10 | async-start | bytes 18874368 | tf_op jit(solution)/shard_map/reduce_scatter | solution.py:985
  529.2 393.0 %reduce-scatter.11.cloned.1.call-start = ((), (), s32[]{:S(2)}) async-start(), calls=%async_computation.12 | async-start | bytes 18874368 | tf_op jit(solution)/shard_map/reduce_scatter | solution.py:988
  611.1 419.0 %reduce-scatter.13.cloned.1.call-start = ((), (), s32[]{:S(2)}) async-start(), calls=%async_computation.13 | async-start | bytes 9437184 | tf_op jit(solution)/shard_map/reduce_scatter | solution.py:989
  611.3 0.7 copy-start.32
  611.3 1.9 copy-start.3
  611.4 2.2 copy-start.36
  611.4 2.2 copy-start.37
  614.3 137.8 %all-to-all-start = ((f32[4,4,384]{2,0,1:T(4,128)}), f32[4,4,384]{2,0,1:T(4,128)S(1)}, u32[]{:S(2)}, u32[]{:S(2)}) async-start(f32[4,4,384]{2,0,1:T(4,128)} %bitcast.39), calls=%async_computation | async-start | bytes 49152 | tf_op jit(solution)/shard_map/all_to_all | solution.py:991
  636.9 507.2 %reduce-scatter.17.cloned.1.call-start = ((), (), s32[]{:S(2)}) async-start(), calls=%async_computation.15 | async-start | bytes 2359296 | tf_op jit(solution)/shard_map/reduce_scatter | solution.py:1005
  638.1 114.1 %copy-start.14 = (bf16[384,2048]{1,0:T(8,128)(2,1)S(1)}, bf16[384,2048]{1,0:T(8,128)(2,1)}, u32[]{:S(2)}) copy-start(bf16[384,2048]{1,0:T(8,128)(2,1)} %multiply_convert_fusion.2.x) | copy-start | bytes 4718596
  753.5 7.1 copy-start.10
  753.5 7.1 copy-start.17
  758.7 1.9 copy-start.12
  913.9 8.3 copy-start.1
  949.8 6.1 copy-start.7
  949.8 18.5 %copy-start.27 = (bf16[1536,512]{1,0:T(8,128)(2,1)S(1)}, bf16[1536,512]{1,0:T(8,128)(2,1)}, u32[]{:S(2)}) copy-start(bf16[1536,512]{1,0:T(8,128)(2,1)} %get-tuple-element.73.x) | copy-start | bytes 4718596
  975.7 6.7 copy-start.8
  982.3 16.4 %copy-start.26 = (bf16[1536,512]{1,0:T(8,128)(2,1)}, bf16[1536,512]{1,0:T(8,128)(2,1)S(1)}, u32[]{:S(2)}) copy-start(bf16[1536,512]{1,0:T(8,128)(2,1)S(1)} %get-tuple-element.190) | copy-start | bytes 4718596
  982.3 176.3 %reduce-scatter.15.cloned.1.call-start = ((), (), s32[]{:S(2)}) async-start(), calls=%async_computation.14 | async-start | bytes 7667712 | tf_op jit(solution)/shard_map/reduce_scatter | solution.py:1038
  1001.1 0.8 copy-start.24
  1001.9 15.1 %copy-start.22 = (bf16[2048,16]{1,0:T(8,128)(2,1)S(1)}, bf16[2048,16]{1,0:T(8,128)(2,1)}, u32[]{:S(2)}) copy-start(bf16[2048,16]{1,0:T(8,128)(2,1)} %copy.161) | copy-start | bytes 196612
  1001.9 15.1 %copy-start.23 = (bf16[2048,1]{1,0:T(8,128)(2,1)S(1)}, bf16[2048,1]{1,0:T(8,128)(2,1)}, u32[]{:S(2)}) copy-start(bf16[2048,1]{1,0:T(8,128)(2,1)} %stack.50) | copy-start | bytes 12292
  1030.1 99.4 %copy-start.5 = (f32[2048]{0:T(1024)S(1)}, f32[2048]{0:T(1024)}, u32[]{:S(2)}) copy-start(f32[2048]{0:T(1024)} %copy-done.4) | copy-start | bytes 24580
  1030.1 99.4 %copy-start.20 = (bf16[384,2048]{1,0:T(8,128)(2,1)S(1)}, bf16[384,2048]{1,0:T(8,128)(2,1)}, u32[]{:S(2)}) copy-start(bf16[384,2048]{1,0:T(8,128)(2,1)} %x.5) | copy-start | bytes 4718596
  1129.5 5.1 copy-start.25
  1131.8 3.9 copy-start.30
  1134.6 1.5 copy-start.29
  1134.6 3.9 copy-start.18
  1134.6 3.9 copy-start.21
  1136.1 3.7 copy-start.11
  1136.1 4.7 copy-start.13
  1144.1 13.7 %collective-permute-start.6 = (bf16[64,2048]{1,0:T(8,128)(2,1)}, bf16[64,2048]{1,0:T(8,128)(2,1)S(1)}, u32[]{:S(2)}, u32[]{:S(2)}) collective-permute-start(bf16[64,2048]{1,0:T(8,128)(2,1)} %reduce-scatter.17.cloned.1.call-done), channel_id=1, source_target_pairs={{0,0},{1,8},{2,16},{3,24},{4,1},{5,9},{6,17},{7,25},{8,2},{9,10},{... | collective-permute-start | bytes 786440 | tf_op jit(solution)/shard_map/ppermute | solution.py:1006
  1179.0 6.3 copy-start.28
Sparse Core Ops, SparseCore 0:
  173.3 89.8 all-gather.3
  265.1 89.8 all-gather.5
  356.9 89.8 all-gather.7
  528.7 91.3 reduce-scatter.8
  623.9 115.9 reduce-scatter.6
  743.8 115.9 reduce-scatter.10
  863.6 71.2 reduce-scatter.12
  982.5 41.8 reduce-scatter.16
  1029.1 64.8 reduce-scatter.14

commit v6 on v5

--- a/solution.py
+++ b/solution.py
@@ -20,6 +20,7 @@
 ROWS = 768
 FTILE = 256
 NTILE = 384
+WTILE = 512
 EPS = 1e-05
 BOTH = ("dp", "expert")
 F32 = jnp.float32
@@ -865,6 +866,29 @@
     )(x, gain, weight)
 
 
+def weight_grad_kernel(left, right, extra, out):
+    columns = right.shape[1]
+    out[:, :columns] = cross_rows(left[...], right[...]).astype(BF16)
+    out[:, columns:] = extra[...].astype(BF16)
+
+
+def weight_grad(left, right, extra):
+    tokens, width = left.shape
+    columns, more = right.shape[1], extra.shape[1]
+    return pl.pallas_call(
+        weight_grad_kernel,
+        grid=(width // WTILE,),
+        in_specs=[
+            pl.BlockSpec((tokens, WTILE), lambda i: (0, i)),
+            pl.BlockSpec((tokens, columns), lambda i: (0, 0)),
+            pl.BlockSpec((WTILE, more), lambda i: (i, 0)),
+        ],
+        out_specs=pl.BlockSpec((WTILE, columns + more), lambda i: (i, 0)),
+        out_shape=jax.ShapeDtypeStruct((width, columns + more), BF16),
+        compiler_params=pltpu.CompilerParams(vmem_limit_bytes=48 * 2**20),
+    )(left, right, extra)
+
+
 def block_order(segs, places):
     seg = segs.reshape(BLOCKS, CLEN)[:, 0]
     place = places.reshape(BLOCKS, CLEN)[:, 0]
@@ -959,15 +983,15 @@
     slot_cols = my_slot.reshape(ways, tok_dev, experts_here)
 
     qkv, normed, inverse_in, squares = norm_qkv(tokens_all, attend_gain[None], dense, 3 * cols)
+    up, down, squares = later(sent, squares)
+    sent = hops(up, down, steps[1] - steps[0], ways)
     squares = sum_z(squares, ways, 3)
     up, down, squares = later(sent, squares)
-    sent = hops(up, down, steps[1] - steps[0], ways)
+    grad_all = line_up(*hops(up, down, ways - steps[1], ways), ways)
     inv_q = lax.rsqrt(squares[0] / width + EPS)[:, None]
     inv_k = lax.rsqrt(squares[1] / width + EPS)[:, None]
     q_rot, k_rot, v_b, mixed_heads, lse = attend(order, qkv, inv_q, inv_k, gain_q, gain_k, cos, sin)
     mixed = a2a_z(mixed_heads, ways, 4)
-    up, down, mixed = later(sent, mixed)
-    grad_all = line_up(*hops(up, down, ways - steps[1], ways), ways)
     own_f = tokens.astype(F32)
     resid = own_f + plain(mixed, out_full)
     mix_inverse = lax.rsqrt(jnp.mean(resid * resid, axis=-1, keepdims=True) + EPS)
@@ -1034,7 +1058,7 @@
         ],
         axis=1,
     )
-    grad_qkv_w = jnp.concatenate([cross_rows(normed, grad_qkv), extra], axis=1).astype(BF16)
+    grad_qkv_w = weight_grad(normed, grad_qkv, extra)
     grad_qkv_w = lax.psum_scatter(grad_qkv_w, "dp", scatter_dimension=0, tiled=True)
     grad_qkv_w = exchange_z(grad_qkv_w, ways, 10).reshape(ways, -1, 3 * cols + SMALL)
     grad_w = [

time: 1200 us -> 1220 us (1.017)
  Pallas kernels: 941 us -> 971 us
  waiting for transfers between devices: 24.5 us -> 12.1 us
    pallas_call x2, Pallas kernels: 25.3 us -> 44.5 us  [sum_z(): pl.pallas_call(functools.partial(sum_kernel, n), out_shape=jax.ShapeDtype...]
    ppermute x3, waiting for transfers between devices: 16.8 us -> 2.22 us  [hops(): lax.ppermute(down[-1], 'expert', [(i + 1, i) for i in range(ways - h)])]
    dot_general x3 -> x2, matrix products: 22.8 us -> 9.2 us  [cross_rows(): lax.dot_general(left, right, (((0,), (0,)), ((), ())), preferred_element_...]
    pallas_call x0 -> x1, Pallas kernels: none -> 13.4 us  [weight_grad(): pl.pallas_call(weight_grad_kernel, grid=(width // WTILE,), in_specs=[pl.B...]
  transfers between devices with their start and end apart: 17 -> 17, of which waited for: 3 -> 3; matrix products, arithmetic and copies ran while one was open for 12% -> 11% of each run, Pallas kernels for 57% -> 59%
where the time goes in v6:
time: 1220 us; the launch traced here: 1210 us
  Pallas kernels  971 us (80%)
  local copies, waits for them, and re-layouts  60.9 us (5%)
  other arithmetic  52.2 us (4%)
  matrix products  49.4 us (4%)
  starting transfers between devices  46.5 us (4%)
  between operations  14.9 us (1%)
    pallas_call x2, Pallas kernels, experts(): pl.pallas_call(expert_kernel, grid=(count, steps), in_specs=[line, line,...  163 us
    pallas_call x1, Pallas kernels, gather_and_combine(): pl.pallas_call(functools.partial(both_kernel, n, rows), out_shape=[jax.Sh...  150 us
    pallas_call x1, Pallas kernels, combine_z(): pl.pallas_call(functools.partial(combine_kernel, n, rows), out_shape=jax....  115 us
    pallas_call x1, Pallas kernels, ag_z(): pl.pallas_call(functools.partial(ag_kernel, n, rows), out_shape=[grown(x,...  108 us
    pallas_call x1, Pallas kernels, gather_rows(): pl.pallas_call(functools.partial(gather_kernel, n, rows), out_shape=[jax....  107 us
    pallas_call x1, Pallas kernels, rs_z(): pl.pallas_call(functools.partial(rs_kernel, n, rows), out_shape=jax.Shape...  103 us
    pallas_call x2, Pallas kernels, exchange_z(): pl.pallas_call(functools.partial(exchange_kernel, n, x.shape[0] // n), ou...  65.1 us
    pallas_call x2, Pallas kernels, sum_z(): pl.pallas_call(functools.partial(sum_kernel, n), out_shape=jax.ShapeDtype...  44.5 us
  transfers between devices with their start and end apart: 17, of which 3 were waited for; matrix products, arithmetic and copies ran while one was open for 11% of the time, Pallas kernels for 59%

profile of v6, /device:TPU:10, one launch (start us, length us, event | category | flops | bytes accessed | tf_op | source)
XLA Modules:
  0.0 1207.3 jit_solution(9000008842710981802)
XLA Ops:
  12.0 1.8 pad_maximum_fusion.2
  14.4 1.4 pad_maximum_fusion.1.x
  15.8 44.6 %shard_map.281 = bf16[256,3712]{1,0:T(8,128)(2,1)} custom-call(bf16[256,3712]{1,0:T(8,128)(2,1)} %pad_maximum_fusion.1.x), custom_call_target="tpu_custom_call" | custom-call | tf_op jit(solution)/shard_map/pallas_call | solution.py:673
  60.4 2.3 slice.103.rest_1_
  62.7 2.1 slice.102.rest_0_
  64.9 108.3 %shard_map.282 = (bf16[1536,2048]{1,0:T(8,128)(2,1)}, bf16[2048,1664]{1,0:T(8,128)(2,1)}, bf16[2048,2048]{1,0:T(8,128)(2,1)}) custom-call(bf16[384,2048]{1,0:T(8,128)(2,1)} %x.5, bf16[256,1664]{1,0:T(8,128)(2,1)} %slice.102.rest_0_, bf16[256,2048]{1,0:T(8,128)(2,1)} %slice.103.rest_1_), custom_call_target="tpu_custom_call" | custom-call | tf_op jit(solution)/shard_map/pallas_call | solution.py:466
  174.8 3.4 collective-permute-start
  178.2 3.6 collective-permute-start.1
  181.8 2.1 slice.107
  183.9 2.0 slice.111.small
  187.4 1.6 fusion
  189.6 1.8 convert_reduce_fusion
  191.4 16.7 %shard_map.283 = (f32[1536,1536]{1,0:T(8,128)}, bf16[1536,2048]{1,0:T(8,128)(2,1)}, f32[1536,1]{1,0:T(8,128)S(1)}, f32[8,1536]{1,0:T(8,128)S(1)}) custom-call(bf16[1536,2048]{1,0:T(8,128)(2,1)} %get-tuple-element.65.x, f32[1,2048]{1,0:T(1,128)S(1)} %bitcast.91, bf16[2048,1664]{1,0:T(8,128)(2,1)} %get-tuple-element.66.weight), custom_call_target="tpu_custom_call" | custom-call | tf_op jit(solution)/shard_map/pallas_call | solution.py:850
  210.3 2.6 collective-permute-done
  212.8 2.2 collective-permute-done.1
  215.0 4.6 collective-permute-start.2
  219.7 2.2 collective-permute-start.3
  223.3 2.8 fusion.17
  226.6 33.7 %shard_map.284 = f32[8,1536]{1,0:T(8,128)} custom-call(f32[8,1536]{1,0:T(8,128)} %copy-done.6), custom_call_target="tpu_custom_call" | custom-call | tf_op jit(solution)/shard_map/pallas_call | solution.py:695
  260.3 1.8 collective-permute-start.4
  262.1 4.0 collective-permute-start.5
  267.6 25.9 %shard_map.285 = (bf16[1536,512]{1,0:T(8,128)(2,1)S(1)}, bf16[1536,512]{1,0:T(8,128)(2,1)}, bf16[1536,512]{1,0:T(8,128)(2,1)}, bf16[1536,512]{1,0:T(8,128)(2,1)}, f32[1536,512]{1,0:T(8,128)}) custom-call(s32[12]{0:T(128)S(1)} %select_reduce_fusion.1.order, f32[1536,1536]{1,0:T(8,128)} %get-tuple-element.67.q_pre.k_pre.v_pre, ...), custom_call_target="tpu_custom_call" | custom-call | tf_op jit(solution)/shard_map/pallas_call | solution.py:111
  294.7 32.4 %shard_map.286 = bf16[384,2048]{1,0:T(8,128)(2,1)} custom-call(bf16[1536,512]{1,0:T(8,128)(2,1)} %get-tuple-element.74.x), custom_call_target="tpu_custom_call" | custom-call | tf_op jit(solution)/shard_map/pallas_call | solution.py:646
  327.1 6.5 multiply_reduce_fusion.7
  333.6 1.7 multiply_convert_fusion.2.x
  335.3 1.5 constant_dynamic-update-slice_fusion.6
  336.9 1.6 constant_dynamic-update-slice_fusion.5
  338.5 1.6 constant_dynamic-update-slice_fusion.4
  340.6 1.5 constant_dynamic-update-slice_fusion.1
  342.1 1.6 constant_dynamic-update-slice_fusion
  343.7 3.3 constant_dynamic-slice_fusion.1.grads
  347.0 106.9 %shard_map.287 = (f32[1536,128]{1,0:T(8,128)}, bf16[4,768,2048]{2,1,0:T(8,128)(2,1)}, bf16[4,768,2048]{2,1,0:T(8,128)(2,1)}) custom-call(bf16[384,2048]{1,0:T(8,128)(2,1)} %multiply_convert_fusion.2.x, s32[4,4,384]{2,1,0:T(4,128)} %bitcast.108, bf16[2048,128]{1,0:T(8,128)(2,1)} %slice.111.small, bf16[1536,2048]{1,0:T(8,128)(2,1)} %constant_dynamic-slice_fusion.1.grads), custom_call_target="tpu_custom_call" | custom-call | tf_op jit(solution)/shard_map/pallas_call | solution.py:516
  453.9 1.4 copy.126
  456.1 81.9 %shard_map.288 = (bf16[2,768,2048]{2,1,0:T(8,128)(2,1)}, bf16[2,768,2048]{2,1,0:T(8,128)(2,1)}, f32[2,1,1536]{2,1,0:T(1,128)}, bf16[8,2,2,256,1024]{4,3,2,1,0:T(8,128)(2,1)}, bf16[8,2,128,2048]{3,2,1,0:T(8,128)(2,1)}) custom-call(s32[4,1,1536]{2,1,0:T(1,128)} %broadcast_in_dim.87.slot, f32[4,1,1536]{2,1,0:T(1,128)} %broadcast_in_dim.88.weight, ...), custom_call_target="tpu_custom_call" | custom-call | tf_op jit(solution)/shard_map/pallas_call | solution.py:775
  538.7 81.6 %shard_map.289 = (bf16[2,768,2048]{2,1,0:T(8,128)(2,1)}, bf16[2,768,2048]{2,1,0:T(8,128)(2,1)}, f32[2,1,1536]{2,1,0:T(1,128)}, bf16[8,2,2,256,1024]{4,3,2,1,0:T(8,128)(2,1)}, bf16[8,2,128,2048]{3,2,1,0:T(8,128)(2,1)}) custom-call(s32[4,1,1536]{2,1,0:T(1,128)} %broadcast_in_dim.87.slot, f32[4,1,1536]{2,1,0:T(1,128)} %broadcast_in_dim.88.weight, ...), custom_call_target="tpu_custom_call" | custom-call | tf_op jit(solution)/shard_map/pallas_call | solution.py:775
  623.5 23.1 %all-to-all-start = ((f32[4,4,384]{2,0,1:T(4,128)}), f32[4,4,384]{2,0,1:T(4,128)S(1)}, u32[]{:S(2)}, u32[]{:S(2)}) async-start(f32[4,4,384]{2,0,1:T(4,128)} %bitcast.41), calls=%async_computation | async-start | bytes 49152 | tf_op jit(solution)/shard_map/all_to_all | solution.py:1015
  647.9 114.8 %shard_map.290 = bf16[384,2048]{1,0:T(8,128)(2,1)} custom-call(s32[4,384,4]{2,1,0:T(8,128)} %bitcast.94, bf16[2,768,2048]{2,1,0:T(8,128)(2,1)} %get-tuple-element.84.low, bf16[2,768,2048]{2,1,0:T(8,128)(2,1)} %get-tuple-element.85.high), custom_call_target="tpu_custom_call" | custom-call | tf_op jit(solution)/shard_map/pallas_call | solution.py:577
  762.8 6.7 multiply_reduce_fusion.1
  769.5 1.4 copy.132
  770.9 1.7 fusion.29
  772.8 6.1 fusion.28.x
  778.9 150.0 %shard_map.291 = (bf16[1536,2048]{1,0:T(8,128)(2,1)}, bf16[384,2048]{1,0:T(8,128)(2,1)}) custom-call(bf16[384,2048]{1,0:T(8,128)(2,1)} %fusion.28.x, s32[4,384,4]{2,1,0:T(8,128)} %bitcast.95, f32[4,384,4]{2,1,0:T(8,128)} %bitcast.100, bf16[2,768,2048]{2,1,0:T(8,128)(2,1)} %get-tuple-element.91.low, bf16[2,768,2048]{2,1,0:T(8,128)(2,1)} %get-tuple-element.92.high, ...), custom_call_target="tpu_custom_call" | custom-call | tf_op jit(solution)/shard_map/pallas_call | solution.py:615
  928.9 8.1 convolution_convert_fusion.1.grad_mixed
  937.0 1.4 copy-done.1
  938.4 27.5 %shard_map.292 = (f32[1536,512]{1,0:T(8,128)}, f32[1536,512]{1,0:T(8,128)}, bf16[1536,512]{1,0:T(8,128)(2,1)S(1)}) custom-call(s32[12]{0:T(128)S(1)} %select_reduce_fusion.1.order, bf16[1536,512]{1,0:T(8,128)(2,1)S(1)} %copy-done.1, bf16[1536,512]{1,0:T(8,128)(2,1)} %get-tuple-element.96.k_rot, bf16[1536,512]{1,0:T(8,128)(2,1)} %get-tuple-element.97.v_in, ...), custom_call_target="tpu_custom_call" | custom-call | tf_op jit(solution)/shard_map/pallas_call | solution.py:168
  965.9 5.6 multiply_reduce_fusion.2
  972.2 10.8 shard_map.293
  983.8 7.5 convolution_convert_fusion
  991.9 5.4 multiply_convert_fusion.1
  997.3 17.3 %multiply_reduce_fusion = (f32[2048]{0:T(1024)S(1)}, bf16[1536,2048]{1,0:T(8,128)(2,1)}) fusion(bf16[1536,2048]{1,0:T(8,128)(2,1)} %get-tuple-element.65.x, f32[1536]{0:T(1024)S(1)} %reduce.17, bf16[2048,1664]{1,0:T(8,128)(2,1)} %get-tuple-element.66.weight, bf16[1536,512]{1,0:T(8,128)(2,1)S(1)} %get-tuple-element.104, ...), kind=kOutput, calls=%fused_computation | convolution fusion | flops 9693558784 | bytes 23607296 | tf_op jit(solution)/shard_map/dot_general | solution.py:45
  1020.2 4.2 concatenate.52.extra
  1024.4 2.0 pad_maximum_fusion.right
  1026.4 13.4 %shard_map.295 = bf16[2048,1664]{1,0:T(8,128)(2,1)} custom-call(bf16[1536,2048]{1,0:T(8,128)(2,1)} %get-tuple-element.107.left, bf16[1536,1536]{1,0:T(8,128)(2,1)S(1)} %pad_maximum_fusion.right, f32[2048,128]{1,0:T(8,128)S(1)} %concatenate.52.extra), custom_call_target="tpu_custom_call" | custom-call | tf_op jit(solution)/shard_map/pallas_call | solution.py:878
  1041.0 102.5 %shard_map.294 = bf16[384,2048]{1,0:T(8,128)(2,1)} custom-call(bf16[1536,2048]{1,0:T(8,128)(2,1)} %get-tuple-element.106.part), custom_call_target="tpu_custom_call" | custom-call | tf_op jit(solution)/shard_map/pallas_call | solution.py:541
  1143.5 2.3 fusion.8
  1145.9 2.8 slice_bitcast_fusion
  1150.1 2.4 maximum_convert_fusion.2
  1154.8 3.3 fusion.11
  1158.1 2.8 collective-permute-start.6
  1160.9 3.8 maximum_convert_fusion.1
  1164.7 2.3 maximum_convert_fusion
  1167.0 4.8 collective-permute-done.6
  1172.7 20.5 %shard_map.296 = bf16[256,1664]{1,0:T(8,128)(2,1)} custom-call(bf16[256,1664]{1,0:T(8,128)(2,1)} %reduce-scatter.15.cloned.1.call-done.x), custom_call_target="tpu_custom_call" | custom-call | tf_op jit(solution)/shard_map/pallas_call | solution.py:673
  1193.2 1.4 convert_bitcast_fusion
  (187 shorter events, 41.4 us)
Async XLA Ops:
  7.2 448.9 %all-gather.4.cloned.1.call-start = ((), (), s32[]{:S(2)}) async-start(), calls=%async_computation.7 | async-start | bytes 18874368 | tf_op jit(solution)/shard_map/all_gather | solution.py:963
  9.9 4.1 copy-start.37
  9.9 4.1 copy-start.38
  9.9 4.1 copy-start.39
  10.0 4.1 copy-start.40
  10.0 4.1 copy-start.41
  10.0 4.3 copy-start.30
  173.2 1.6 copy-start.11
  173.2 12.8 %copy-start.35 = (s32[1,1536]{1,0:T(1,128)S(1)}, s32[1,1536]{1,0:T(1,128)}, u32[]{:S(2)}) copy-start(s32[1,1536]{1,0:T(1,128)} %param.32) | copy-start | bytes 18436
  173.2 12.9 %copy-start.32 = (s32[1,1536]{1,0:T(1,128)S(1)}, s32[1,1536]{1,0:T(1,128)}, u32[]{:S(2)}) copy-start(s32[1,1536]{1,0:T(1,128)} %param.33) | copy-start | bytes 18436
  173.2 13.0 %copy-start.36 = (s32[1,1536]{1,0:T(1,128)S(1)}, s32[1,1536]{1,0:T(1,128)}, u32[]{:S(2)}) copy-start(s32[1,1536]{1,0:T(1,128)} %param.34) | copy-start | bytes 18436
  173.2 13.0 %copy-start.31 = (s32[1,1536,8]{1,2,0:T(8,128)S(1)}, s32[1,1536,8]{1,2,0:T(8,128)}, u32[]{:S(2)}) copy-start(s32[1,1536,8]{1,2,0:T(8,128)} %param.35) | copy-start | bytes 147460
  173.2 282.9 %all-gather.6.cloned.1.call-start = ((), (), s32[]{:S(2)}) async-start(), calls=%async_computation.8 | async-start | bytes 18874368 | tf_op jit(solution)/shard_map/all_gather | solution.py:964
  174.0 282.1 %all-gather.8.cloned.1.call-start = ((), (), s32[]{:S(2)}) async-start(), calls=%async_computation.9 | async-start | bytes 18874368 | tf_op jit(solution)/shard_map/all_gather | solution.py:965
  174.7 604.1 %reduce-scatter.9.cloned.1.call-start = ((), (), s32[]{:S(2)}) async-start(), calls=%async_computation.11 | async-start | bytes 9437184 | tf_op jit(solution)/shard_map/reduce_scatter | solution.py:1010
  174.8 38.0 %collective-permute-start = (bf16[384,2048]{1,0:T(8,128)(2,1)S(1)}, bf16[384,2048]{1,0:T(8,128)(2,1)}, u32[]{:S(2)}, u32[]{:S(2)}) collective-permute-start(bf16[384,2048]{1,0:T(8,128)(2,1)S(1)} %copy-done.11), channel_id=1, source_target_pairs={{0,1},{1,2},{2,3},{4,5},{5,6},{6,7},{8,9},{9,10},{10,11},{12,13},{... | collective-permute-start | bytes 4718600 | tf_op jit(solution)/shard_map/ppermute | solution.py:812
  178.2 36.9 %collective-permute-start.1 = (bf16[384,2048]{1,0:T(8,128)(2,1)S(1)}, bf16[384,2048]{1,0:T(8,128)(2,1)S(1)}, u32[]{:S(2)}, u32[]{:S(2)}) collective-permute-start(bf16[384,2048]{1,0:T(8,128)(2,1)S(1)} %copy-done.11), channel_id=1, source_target_pairs={{1,0},{2,1},{3,2},{5,4},{6,5},{7,6},{9,8},{10,9},{11,10},{13,12},{... | collective-permute-start | bytes 4718600 | tf_op jit(solution)/shard_map/ppermute | solution.py:813
  189.0 19.2 %copy-start.28 = (s32[1536,4]{0,1:T(4,128)}, s32[1536,4]{0,1:T(4,128)S(1)}, u32[]{:S(2)}) copy-start(s32[1536,4]{0,1:T(4,128)S(1)} %and_select_fusion) | copy-start | bytes 73732
  208.1 0.9 copy-start.2
  209.0 0.6 copy-start.4
  209.6 0.6 copy-start.6
  215.0 11.5 copy-start.24
  215.0 45.2 %collective-permute-start.2 = (bf16[384,2048]{1,0:T(8,128)(2,1)}, bf16[384,2048]{1,0:T(8,128)(2,1)}, u32[]{:S(2)}, u32[]{:S(2)}) collective-permute-start(bf16[384,2048]{1,0:T(8,128)(2,1)} %collective-permute-done), channel_id=1, source_target_pairs={{1,2},{2,3},{5,6},{6,7},{9,10},{10,11},{13,14},{14,15},{17,18},{18... | collective-permute-start | bytes 4718600 | tf_op jit(solution)/shard_map/ppermute | solution.py:812
  219.7 40.6 %collective-permute-start.3 = (bf16[384,2048]{1,0:T(8,128)(2,1)S(1)}, bf16[384,2048]{1,0:T(8,128)(2,1)}, u32[]{:S(2)}, u32[]{:S(2)}) collective-permute-start(bf16[384,2048]{1,0:T(8,128)(2,1)S(1)} %collective-permute-done.1), channel_id=1, source_target_pairs={{1,0},{2,1},{5,4},{6,5},{9,8},{10,9},{13,12},{14,13},{17,16},{18,1... | collective-permute-start | bytes 4718600 | tf_op jit(solution)/shard_map/ppermute | solution.py:813
  260.3 75.1 %collective-permute-start.4 = (bf16[384,2048]{1,0:T(8,128)(2,1)}, bf16[384,2048]{1,0:T(8,128)(2,1)}, u32[]{:S(2)}, u32[]{:S(2)}) collective-permute-start(bf16[384,2048]{1,0:T(8,128)(2,1)} %collective-permute-done.2), channel_id=1, source_target_pairs={{2,3},{6,7},{10,11},{14,15},{18,19},{22,23},{26,27},{30,31}} | collective-permute-start | bytes 4718600 | tf_op jit(solution)/shard_map/ppermute | solution.py:812
  262.1 80.0 %collective-permute-start.5 = (bf16[384,2048]{1,0:T(8,128)(2,1)}, bf16[384,2048]{1,0:T(8,128)(2,1)}, u32[]{:S(2)}, u32[]{:S(2)}) collective-permute-start(bf16[384,2048]{1,0:T(8,128)(2,1)} %collective-permute-done.3), channel_id=1, source_target_pairs={{1,0},{5,4},{9,8},{13,12},{17,16},{21,20},{25,24},{29,28}} | collective-permute-start | bytes 4718600 | tf_op jit(solution)/shard_map/ppermute | solution.py:813
  293.5 1.2 copy-start
  294.7 32.4 %copy-start.15 = (bf16[384,2048]{1,0:T(8,128)(2,1)S(1)}, bf16[384,2048]{1,0:T(8,128)(2,1)}, u32[]{:S(2)}) copy-start(bf16[384,2048]{1,0:T(8,128)(2,1)} %x.5) | copy-start | bytes 4718596
  333.6 3.2 copy-start.7
  336.9 3.3 copy-start.12
  338.5 1.9 copy-start.25
  538.0 240.8 %reduce-scatter.7.cloned.1.call-start = ((), (), s32[]{:S(2)}) async-start(), calls=%async_computation.10 | async-start | bytes 18874368 | tf_op jit(solution)/shard_map/reduce_scatter | solution.py:1009
  538.6 398.4 %reduce-scatter.11.cloned.1.call-start = ((), (), s32[]{:S(2)}) async-start(), calls=%async_computation.12 | async-start | bytes 18874368 | tf_op jit(solution)/shard_map/reduce_scatter | solution.py:1012
  620.3 420.7 %reduce-scatter.13.cloned.1.call-start = ((), (), s32[]{:S(2)}) async-start(), calls=%async_computation.13 | async-start | bytes 9437184 | tf_op jit(solution)/shard_map/reduce_scatter | solution.py:1013
  620.5 0.7 copy-start.29
  620.5 1.9 copy-start.3
  620.6 2.2 copy-start.33
  620.6 2.2 copy-start.34
  623.5 139.2 %all-to-all-start = ((f32[4,4,384]{2,0,1:T(4,128)}), f32[4,4,384]{2,0,1:T(4,128)S(1)}, u32[]{:S(2)}, u32[]{:S(2)}) async-start(f32[4,4,384]{2,0,1:T(4,128)} %bitcast.41), calls=%async_computation | async-start | bytes 49152 | tf_op jit(solution)/shard_map/all_to_all | solution.py:1015
  646.6 511.5 %reduce-scatter.17.cloned.1.call-start = ((), (), s32[]{:S(2)}) async-start(), calls=%async_computation.15 | async-start | bytes 2359296 | tf_op jit(solution)/shard_map/reduce_scatter | solution.py:1029
  762.8 8.1 copy-start.10
  770.8 1.9 copy-start.13
  937.0 1.4 copy-start.1
  965.9 17.9 %copy-start.22 = (bf16[1536,512]{1,0:T(8,128)(2,1)S(1)}, bf16[1536,512]{1,0:T(8,128)(2,1)}, u32[]{:S(2)}) copy-start(bf16[1536,512]{1,0:T(8,128)(2,1)} %get-tuple-element.74.x) | copy-start | bytes 4718596
  991.4 181.3 %reduce-scatter.15.cloned.1.call-start = ((), (), s32[]{:S(2)}) async-start(), calls=%async_computation.14 | async-start | bytes 7667712 | tf_op jit(solution)/shard_map/reduce_scatter | solution.py:1062
  997.2 17.3 %copy-start.18 = (bf16[1536,512]{1,0:T(8,128)(2,1)}, bf16[1536,512]{1,0:T(8,128)(2,1)S(1)}, u32[]{:S(2)}) copy-start(bf16[1536,512]{1,0:T(8,128)(2,1)S(1)} %get-tuple-element.176) | copy-start | bytes 4718596
  997.3 17.3 %copy-start.19 = (bf16[1536,512]{1,0:T(8,128)(2,1)}, bf16[1536,512]{1,0:T(8,128)(2,1)S(1)}, u32[]{:S(2)}) copy-start(bf16[1536,512]{1,0:T(8,128)(2,1)S(1)} %get-tuple-element.177) | copy-start | bytes 4718596
  1018.2 1.0 copy-start.20
  1040.9 102.6 %copy-start.5 = (f32[2048]{0:T(1024)S(1)}, f32[2048]{0:T(1024)}, u32[]{:S(2)}) copy-start(f32[2048]{0:T(1024)} %copy-done.4) | copy-start | bytes 24580
  1040.9 102.6 %copy-start.16 = (bf16[384,2048]{1,0:T(8,128)(2,1)S(1)}, bf16[384,2048]{1,0:T(8,128)(2,1)}, u32[]{:S(2)}) copy-start(bf16[384,2048]{1,0:T(8,128)(2,1)} %x.5) | copy-start | bytes 4718596
  1143.5 5.1 copy-start.21
  1145.9 3.9 copy-start.27
  1148.6 1.5 copy-start.26
  1148.6 3.9 copy-start.14
  1148.6 3.9 copy-start.17
  1150.1 3.7 copy-start.8
  1150.1 4.7 copy-start.9
  1158.1 13.8 %collective-permute-start.6 = (bf16[64,2048]{1,0:T(8,128)(2,1)}, bf16[64,2048]{1,0:T(8,128)(2,1)S(1)}, u32[]{:S(2)}, u32[]{:S(2)}) collective-permute-start(bf16[64,2048]{1,0:T(8,128)(2,1)} %reduce-scatter.17.cloned.1.call-done), channel_id=1, source_target_pairs={{0,0},{1,8},{2,16},{3,24},{4,1},{5,9},{6,17},{7,25},{8,2},{9,10},{... | collective-permute-start | bytes 786440 | tf_op jit(solution)/shard_map/ppermute | solution.py:1030
  1193.2 6.3 copy-start.23
Sparse Core Ops, SparseCore 0:
  173.3 89.8 all-gather.3
  265.1 89.8 all-gather.5
  357.0 89.8 all-gather.7
  538.1 89.5 reduce-scatter.8
  631.6 115.9 reduce-scatter.6
  751.4 115.9 reduce-scatter.10
  871.2 71.2 reduce-scatter.12
  991.5 41.5 reduce-scatter.16
  1040.0 64.4 reduce-scatter.14
